TPU v7x, 512 devices: a whole 4x8x8 slice. The times are simulated.
512 devices in a mesh: frames: 4 (over y_hi, core), tiles: 128 (over z, y_lo, x).
Axes of the slice: x: 4, y: 8 (y_hi: 2, y_lo: 4; y = y_hi * 4 + y_lo), z: 8, core: 2. Of those that a mesh axis runs over, the one named last changes fastest.
Arguments:
- frames: float32 [80, 8192, 320], P('frames', 'tiles'), may hold values from -6 to 6
- live_first: int32 [128], P('tiles'), may hold values from 0 to 3, as said below
- live_count: int32 [128], P('tiles'), may hold values from 1 to 4, as said below
- shifts: int32 [2, 2], replicated, may hold values from 1 to 63, as said below
Outputs:
- restored_image: float32 [8192, 320], P('tiles')
Inputs may be any that keep to these rules, and one draw needn't show every extreme that they name: live_first[a] + live_count[a] <= 4 for every tile a. `live_count`: each tile has at least one live subfield column. shifts[0] = (1, q) and shifts[1] = (p, 1) with q and p between 1 and 63, one of q and p equal to 63.
All inputs are finite; a program needn't handle non-finite values.
Results may differ from a plain program's by a relative error of at most 0.0003.
Values sent between devices are 32-bit elements; how exact they have to be, the bound alone decides.
No kernel may reach another device: no remote copies, remote signals or barrier semaphores. Data moves between devices by JAX's collectives and lax.ppermute only.
A program may use at most 64 MiB of HBM per device.

v0:
```python
import jax
import jax.numpy as jnp
from jax import lax
from jax.sharding import PartitionSpec as P

ridge_term = 0.1
share_term = 0.0001
tiny_term = 1e-06
highest = lax.Precision.HIGHEST


def from_behind(block, axis, distance):
    devices = range(lax.axis_size(axis))
    route = [(i - distance, i) for i in devices if i - distance in devices]
    return lax.ppermute(block, axis, route)


def taper(side_len):
    position = jnp.arange(side_len, dtype=jnp.float32)
    single = jnp.sin(jnp.pi * (position + 0.5) / side_len) ** 2
    return single[:, None] * single[None, :]


def dft_tables(side_len):
    frequency = jnp.arange(side_len, dtype=jnp.int32)
    phase_angle = (
        2.0
        * jnp.pi
        * (frequency[:, None] * frequency[None, :] % side_len).astype(jnp.float32)
        / side_len
    )
    return (jnp.cos(phase_angle), jnp.sin(phase_angle))


def spectral_eigen(shifts, side_len):
    frequency = jnp.arange(side_len, dtype=jnp.int32)
    eigen_total = jnp.full((side_len, side_len), ridge_term, jnp.float32)
    for s in range(shifts.shape[0]):
        phase_angle = (
            frequency[:, None] * shifts[s, 0] + frequency[None, :] * shifts[s, 1]
        ) % side_len
        eigen_total = (
            eigen_total
            + 2.0
            - 2.0 * jnp.cos(2.0 * jnp.pi * phase_angle.astype(jnp.float32) / side_len)
        )
    return eigen_total


def forward_real(values, cosine_table, sine_table):
    side_len = cosine_table.shape[0]
    stacked_table = jnp.concatenate([cosine_table, sine_table], axis=1)
    right_part = jnp.einsum("...xy,yv->...xv", values, stacked_table, precision=highest)
    upright = jnp.concatenate([cosine_table, sine_table], axis=0)
    products = jnp.einsum("ux,...xv->...uv", upright, right_part, precision=highest)
    real_part = products[..., :side_len, :side_len] - products[..., side_len:, side_len:]
    imag_part = -(products[..., side_len:, :side_len] + products[..., :side_len, side_len:])
    return (real_part, imag_part)


def inverse_real(real_in, imag_in, cosine_table, sine_table):
    side_len = cosine_table.shape[0]
    stacked_table = jnp.concatenate([cosine_table, sine_table], axis=1)
    right_real = jnp.einsum("...xy,yv->...xv", real_in, stacked_table, precision=highest)
    right_imag = jnp.einsum("...xy,yv->...xv", imag_in, stacked_table, precision=highest)
    part_real = right_real[..., :side_len] - right_imag[..., side_len:]
    part_imag = right_real[..., side_len:] + right_imag[..., :side_len]
    upright = jnp.concatenate([part_real, -part_imag], axis=-2)
    products = jnp.einsum("ux,...xv->...uv", stacked_table, upright, precision=highest)
    return products / (side_len * side_len)


def solve_block(spectra, shifts, eigen, window, cosine_table, sine_table):
    power_sum = spectra[0]
    mean_power = jnp.mean(power_sum, axis=(1, 2), keepdims=True)
    normal_rhs = jnp.zeros_like(power_sum)
    for s in range(shifts.shape[0]):
        row_step = shifts[s, 0]
        col_step = shifts[s, 1]
        partner = jnp.roll(power_sum, (-row_step, -col_step), axis=(1, 2))
        scale_term = (
            jnp.sqrt(power_sum * partner + share_term * mean_power * mean_power) + tiny_term
        )
        sine_diff = spectra[1 + s] / scale_term
        normal_rhs = normal_rhs + sine_diff - jnp.roll(sine_diff, (row_step, col_step), axis=(1, 2))
    rhs_real, rhs_imag = forward_real(normal_rhs, cosine_table, sine_table)
    phase_map = inverse_real(rhs_real / eigen, rhs_imag / eigen, cosine_table, sine_table)
    amplitude = jnp.sqrt(power_sum)
    rebuilt = inverse_real(
        amplitude * jnp.cos(phase_map), amplitude * jnp.sin(phase_map), cosine_table, sine_table
    )
    return rebuilt * window


def on_device(frames, live_first, live_count, shifts):
    frame_count, half_side, image_width = frames.shape
    side_len = 2 * half_side
    column_count = image_width // half_side - 1
    shift_count = shifts.shape[0]
    total_frames = frame_count * lax.axis_size("frames")
    window = taper(side_len)
    cosine_table, sine_table = dft_tables(side_len)
    eigen = spectral_eigen(shifts, side_len)
    next_rows = from_behind(frames, "tiles", -1)
    stacked = jnp.concatenate([frames, next_rows], axis=1)

    def add_frame(carry, plane):
        patches = jnp.stack(
            [plane[:, c * half_side : c * half_side + side_len] for c in range(column_count)],
            axis=0,
        )
        real_part, imag_part = forward_real(patches * window, cosine_table, sine_table)
        terms = [real_part * real_part + imag_part * imag_part]
        for s in range(shift_count):
            partner_real = jnp.roll(real_part, (-shifts[s, 0], -shifts[s, 1]), axis=(1, 2))
            partner_imag = jnp.roll(imag_part, (-shifts[s, 0], -shifts[s, 1]), axis=(1, 2))
            terms.append(imag_part * partner_real - real_part * partner_imag)
        return (carry + jnp.stack(terms, axis=0), None)

    initial = jnp.zeros((1 + shift_count, column_count, side_len, side_len), jnp.float32)
    spectra_sum, unused = lax.scan(add_frame, initial, stacked)
    spectra = spectra_sum / total_frames
    summed = lax.psum(spectra, "frames")
    rebuilt = solve_block(summed, shifts, eigen, window, cosine_table, sine_table)
    column_ids = jnp.arange(column_count, dtype=jnp.int32)
    live_mask = (column_ids >= live_first[0]) & (column_ids < live_first[0] + live_count[0])
    rebuilt = rebuilt * live_mask[:, None, None].astype(jnp.float32)
    padding = jnp.zeros((1, side_len, half_side), jnp.float32)
    halves = jnp.concatenate([rebuilt[:, :, :half_side], padding], axis=0) + jnp.concatenate(
        [padding, rebuilt[:, :, half_side:]], axis=0
    )
    image_block = jnp.transpose(halves, (1, 0, 2)).reshape(side_len, image_width)
    from_above = from_behind(image_block[half_side:], "tiles", 1)
    return image_block[:half_side] + from_above


def solution(mesh):
    placed = (P("frames", "tiles", None), P("tiles"), P("tiles"), P())
    return jax.shard_map(
        on_device, mesh=mesh, in_specs=placed, out_specs=P("tiles", None), check_vma=False
    )
```

profile of v0, /device:TPU:64, one launch (start us, length us, event | category | flops | bytes accessed | tf_op | source)
XLA Modules:
  0.0 404.2 jit_solution(3510386956405635419)
XLA Ops:
  6.5 6.8 %collective-permute-start = (f32[20,64,320]{2,1,0:T(8,128)}, f32[20,64,320]{2,1,0:T(8,128)S(1)}, u32[]{:S(2)}, u32[]{:S(2)}) collective-permute-start(f32[20,64,320]{2,1,0:T(8,128)} %param.8), channel_id=1, source_target_pairs={{1,0},{2,1},{3,2},{4,3},{5,4},{6,5},{7,6},{8,7},{9,8},{10,9},{11,1... | collective-permute-start | bytes 4915208 | tf_op jit(solution)/shard_map/ppermute | solution.py:15
  13.3 1.5 fusion.117
  25.4 30.4 %collective-permute-done = f32[20,64,320]{2,1,0:T(8,128)S(1)} collective-permute-done((f32[20,64,320]{2,1,0:T(8,128)}, f32[20,64,320]{2,1,0:T(8,128)S(1)}, u32[]{:S(2)}, u32[]{:S(2)}) %collective-permute-start) | collective-permute-done | bytes 1638432 | tf_op jit(solution)/shard_map/ppermute | solution.py:15
  55.7 3.7 pad_maximum_fusion
  59.4 241.7 %while.13 = (s32[]{:T(128)}, f32[3,4,128,128]{3,2,1,0:T(8,128)S(1)}, f32[20,128,320]{2,1,0:T(8,128)}, f32[128,256]{1,0:T(8,128)S(1)}, f32[256,128]{1,0:T(8,128)S...) while((s32[]{:T(128)}, ...), condition=%wide.region_1.3_spmd.clone, body=%wide.region_0.2_spmd.clone.sunk | while | flops 606355456 | bytes 11470127 | solution.py:121
  63.9 0.9 dynamic-slice_bitcast_fusion.2
  65.6 1.0 convolution_bitcast_fusion.4
  76.0 0.9 dynamic-slice_bitcast_fusion.2
  77.7 1.0 convolution_bitcast_fusion.4
  88.1 0.9 dynamic-slice_bitcast_fusion.2
  89.8 1.0 convolution_bitcast_fusion.4
  100.1 0.9 dynamic-slice_bitcast_fusion.2
  101.8 1.0 convolution_bitcast_fusion.4
  112.2 0.9 dynamic-slice_bitcast_fusion.2
  113.9 1.0 convolution_bitcast_fusion.4
  124.3 0.9 dynamic-slice_bitcast_fusion.2
  126.0 1.0 convolution_bitcast_fusion.4
  136.4 0.9 dynamic-slice_bitcast_fusion.2
  138.1 1.0 convolution_bitcast_fusion.4
  148.4 0.9 dynamic-slice_bitcast_fusion.2
  150.1 1.0 convolution_bitcast_fusion.4
  160.5 0.9 dynamic-slice_bitcast_fusion.2
  162.2 1.0 convolution_bitcast_fusion.4
  172.6 0.9 dynamic-slice_bitcast_fusion.2
  174.3 1.0 convolution_bitcast_fusion.4
  186.4 1.0 convolution_bitcast_fusion.4
  198.5 1.0 convolution_bitcast_fusion.4
  210.5 1.0 convolution_bitcast_fusion.4
  222.6 1.0 convolution_bitcast_fusion.4
  234.7 1.0 convolution_bitcast_fusion.4
  246.8 1.0 convolution_bitcast_fusion.4
  258.8 1.0 convolution_bitcast_fusion.4
  270.9 1.0 convolution_bitcast_fusion.4
  283.0 1.0 convolution_bitcast_fusion.4
  295.1 1.0 convolution_bitcast_fusion.4
  301.4 1.0 broadcast_multiply_fusion.1
  302.4 1.3 iota_multiply_fusion
  303.7 1.2 iota_multiply_fusion.2
  307.0 66.4 %all-reduce.4.cloned.1.call-done = f32[3,4,128,128]{2,3,1,0:T(8,128)} async-done(((f32[3,4,128,128]{2,3,1,0:T(8,128)}), f32[3,4,128,128]{2,3,1,0:T(8,128)}) %all-reduce.4.cloned.1.call-update) | async-done | bytes 786448 | tf_op jit(solution)/shard_map/psum | solution.py:123
  373.4 1.1 slice_reduce_fusion
  374.8 1.5 fusion.59
  377.5 1.0 convolution_bitcast_fusion.1
  379.9 1.0 convolution_multiply_fusion
  380.9 1.5 fusion.74
  382.3 1.5 fusion.73
  383.9 1.0 fusion.31
  385.2 3.4 collective-permute-start.1
  388.7 8.0 %collective-permute-done.1 = f32[64,320]{1,0:T(8,128)S(1)} collective-permute-done((f32[64,320]{1,0:T(8,128)S(1)}, f32[64,320]{1,0:T(8,128)S(1)}, u32[]{:S(2)}, u32[]{:S(2)}) %collective-permute-start.1) | collective-permute-done | bytes 81952 | tf_op jit(solution)/shard_map/ppermute | solution.py:15
  (220 shorter events, 66.9 us)
Async XLA Ops:
  6.5 366.9 %all-reduce.4.cloned.1.call-start = ((), (), s32[]{:S(2)}) async-start(), calls=%async_computation | async-start | bytes 1572864 | tf_op jit(solution)/shard_map/psum | solution.py:123
  6.5 49.2 %collective-permute-start = (f32[20,64,320]{2,1,0:T(8,128)}, f32[20,64,320]{2,1,0:T(8,128)S(1)}, u32[]{:S(2)}, u32[]{:S(2)}) collective-permute-start(f32[20,64,320]{2,1,0:T(8,128)} %param.8), channel_id=1, source_target_pairs={{1,0},{2,1},{3,2},{4,3},{5,4},{6,5},{7,6},{8,7},{9,8},{10,9},{11,1... | collective-permute-start | bytes 4915208 | tf_op jit(solution)/shard_map/ppermute | solution.py:15
  376.7 4.1 %copy-start = (f32[3,4,128,128]{2,3,1,0:T(8,128)S(1)}, f32[3,4,128,128]{2,3,1,0:T(8,128)}, u32[]{:S(2)}) copy-start(f32[3,4,128,128]{2,3,1,0:T(8,128)} %all-reduce.4.cloned.1.call-done) | copy-start | bytes 2359300
  385.2 11.5 %collective-permute-start.1 = (f32[64,320]{1,0:T(8,128)S(1)}, f32[64,320]{1,0:T(8,128)S(1)}, u32[]{:S(2)}, u32[]{:S(2)}) collective-permute-start(f32[64,320]{1,0:T(8,128)S(1)} %copy.13), channel_id=1, source_target_pairs={{0,1},{1,2},{2,3},{3,4},{4,5},{5,6},{6,7},{7,8},{8,9},{9,10},{10,1... | collective-permute-start | bytes 245768 | tf_op jit(solution)/shard_map/ppermute | solution.py:15
Sparse Core Ops, SparseCore 0:
  302.5 70.8 all-reduce.3
where the time goes:
time: 407 us; the launch traced here: 404 us
  loops' own time  151 us (37%)
  waiting for transfers between devices  105 us (26%)
  other arithmetic  39.4 us (10%)
  matrix products  39.1 us (10%)
  local copies, waits for them, and re-layouts  34.9 us (9%)
  between operations  25.1 us (6%)
  starting transfers between devices  10.2 us (3%)
    another operation x1, loops' own time, on_device(): spectra_sum, unused = lax.scan(add_frame, initial, stacked)  151 us
    psum x1, waiting for transfers between devices, on_device(): summed = lax.psum(spectra, 'frames')  66.4 us
    ppermute x2, waiting for transfers between devices, from_behind(): return lax.ppermute(block, axis, route)  38.4 us
    dot_general x21, matrix products, forward_real(): jnp.einsum('ux,...xv->...uv', upright, right_part, precision=highest)  20.9 us
    squeeze x20, local copies, waits for them, and re-layouts, on_device(): spectra_sum, unused = lax.scan(add_frame, initial, stacked)  18.9 us
    another operation x40, other arithmetic, add_frame(): return (carry + jnp.stack(terms, axis=0), None)  13.8 us
    dot_general x21, matrix products, forward_real(): jnp.einsum('...xy,yv->...xv', values, stacked_table, precision=highest)  12 us
    another operation x20, local copies, waits for them, and re-layouts, add_frame(): jnp.roll(real_part, (-shifts[s, 0], -shifts[s, 1]), axis=(1, 2))  11.9 us
  transfers between devices with their start and end apart: 3, of which 3 were waited for; matrix products, arithmetic and copies ran while one was open for 1% of the time, Pallas kernels for 0%

commit v1 on v0

v1 whole, which is shorter than its diff:
```python
import functools

import jax
import jax.numpy as jnp
import ml_dtypes
import numpy as np
from jax import lax
from jax.experimental import pallas as pl
from jax.experimental.pallas import tpu as pltpu
from jax.sharding import PartitionSpec as P

ridge_term = 0.1
share_term = 0.0001
tiny_term = 1e-06

side = 128
half = 64
width = 320
pair_width = 2 * width
folded_rows = 200
total_frames = 80
float32 = jnp.float32
bfloat16 = jnp.bfloat16
vmem_limit = 48 * 1024 * 1024


def as_pieces(table):
    upper = table.astype(np.float32).astype(ml_dtypes.bfloat16)
    lower = (table - upper.astype(np.float64)).astype(np.float32).astype(ml_dtypes.bfloat16)
    return upper, lower


def complex_tables():
    index = np.arange(side)
    angle = 2.0 * np.pi * (index[:, None] * index[None, :] % side) / side
    cosine, sine = np.cos(angle), np.sin(angle)
    taper = np.sin(np.pi * (index + 0.5) / side) ** 2
    wc, ws = taper[:, None] * cosine, taper[:, None] * sine
    right_taper = np.block([[wc, -ws], [ws, wc]])
    left_taper = np.block([[wc.T, ws.T], [-ws.T, wc.T]])
    right = np.block([[cosine, -sine], [sine, cosine]])
    left = np.block([[cosine, sine], [-sine, cosine]])
    right_back = np.block([[cosine, sine], [-sine, cosine]])
    left_back = np.block([[cosine, -sine], [sine, cosine]])
    stacked = [as_pieces(t) for t in (right_taper, left_taper, right, left, right_back, left_back)]
    flip = np.zeros((side, side), ml_dtypes.bfloat16)
    flip[index, (-index) % side] = 1
    window = (taper[:, None] * taper[None, :] / side**2).astype(np.float32)
    return np.stack([np.stack(s) for s in stacked]), flip, window


def pieces(values):
    upper = values.astype(bfloat16)
    lower = (values - upper.astype(float32)).astype(bfloat16)
    return upper, lower


def product(a, b):
    return jnp.dot(a, b, preferred_element_type=float32)


def times_table(values, table_ref):
    upper, lower = pieces(values)
    high, low = table_ref[0], table_ref[1]
    return product(upper, high) + product(lower, high) + product(upper, low)


def table_times(table_ref, values):
    upper, lower = pieces(values)
    high, low = table_ref[0], table_ref[1]
    return product(high, upper) + product(high, lower) + product(low, upper)


def upright(g):
    return jnp.concatenate([g[:, :side], g[:, side:]], axis=0)


def moved(values, row_step, col_step):
    return pltpu.roll(pltpu.roll(values, side - col_step, 1), side - row_step, 0)


def moved_back(values, row_step, col_step):
    return pltpu.roll(pltpu.roll(values, col_step, 1), row_step, 0)


def mirrored(planes, flip_ref):
    flip = flip_ref[...]
    twice_down = jnp.concatenate([flip, flip], axis=0)
    twice_across = jnp.concatenate([flip, flip], axis=1)
    tall = jnp.concatenate(planes, axis=0)
    upper, lower = pieces(tall)
    tall = product(jnp.concatenate([upper, lower], axis=1), twice_down)
    wide = jnp.concatenate([tall[i * side : (i + 1) * side] for i in range(len(planes))], axis=1)
    upper, lower = pieces(wide)
    wide = product(twice_across, jnp.concatenate([upper, lower], axis=0))
    return [wide[:, i * side : (i + 1) * side] for i in range(len(planes))]


def pack_kernel(frames_ref, *out_refs):
    base = 0
    for out_ref in out_refs:
        count = out_ref.shape[0]

        def body(i, carry, base=base, out_ref=out_ref):
            f = 2 * (base + i)
            out_ref[i] = jnp.concatenate([frames_ref[f], frames_ref[f + 1]], axis=1)
            return carry

        lax.fori_loop(0, count, body, 0)
        base += count


def add_pair(upper, lower, row_step, col_step, right_ref, left_ref, out_ref, which):
    plane = jnp.concatenate([upper, lower], axis=0)
    shifted = plane[:, half : half + 512]
    first = [plane[:, 0:128], shifted[:, 0:128], plane[:, 128:256], shifted[:, 128:256]]
    second = [shifted[:, 256:384], plane[:, 384:512], shifted[:, 384:512], plane[:, 512:640]]
    stacked = jnp.concatenate([jnp.concatenate([a, b], axis=1) for a, b in zip(first, second)], axis=0)
    g = times_table(stacked, right_ref)
    for two in range(2):
        parts = [upright(g[(2 * two + j) * side : (2 * two + j + 1) * side]) for j in range(2)]
        z = table_times(left_ref, jnp.concatenate(parts, axis=1))
        for j in range(2):
            c = 2 * two + j
            zr = z[:side, j * side : (j + 1) * side]
            zi = z[side:, j * side : (j + 1) * side]
            out_ref[which, c, 0] += zr * zr + zi * zi
            out_ref[which, c, 1] += zi * moved(zr, 1, col_step) - zr * moved(zi, 1, col_step)
            out_ref[which, c, 2] += zi * moved(zr, row_step, 1) - zr * moved(zi, row_step, 1)


def add_chunk(scalars, own_l, halo_l, own_r, halo_r, right_ref, left_ref, acc):
    row_step, col_step = scalars[0], scalars[1]

    def body(i, carry):
        add_pair(own_l[i], halo_l[i], row_step, col_step, right_ref, left_ref, acc, 0)
        add_pair(halo_r[i], own_r[i], row_step, col_step, right_ref, left_ref, acc, 1)
        return carry

    lax.fori_loop(0, own_l.shape[0], body, 0)


def start_kernel(scalars, own_r0, own_r1, right_ref, left_ref, out_ref):
    out_ref[...] = jnp.zeros_like(out_ref)

    @pl.when(scalars[3] == 1)
    def last_tile():
        blank = jnp.zeros((half, pair_width), float32)
        for own in (own_r0, own_r1):

            def body(i, carry, own=own):
                add_pair(own[i], blank, scalars[0], scalars[1], right_ref, left_ref, out_ref, 0)
                return carry

            lax.fori_loop(0, own.shape[0], body, 0)


def middle_kernel(scalars, own_l, halo_l, own_r, halo_r, right_ref, left_ref, before, out_ref):
    out_ref[...] = before[...]
    add_chunk(scalars, own_l, halo_l, own_r, halo_r, right_ref, left_ref, out_ref)


def last_kernel(scalars, own_l, halo_l, own_r, halo_r, right_ref, left_ref, before, kept, sent, acc):
    acc[...] = before[...]
    add_chunk(scalars, own_l, halo_l, own_r, halo_r, right_ref, left_ref, acc)
    lower_core = scalars[2] == 0
    for which in range(2):
        for j in range(2):
            for k in range(3):
                one, two = acc[which, j, k], acc[which, 2 + j, k]
                kept[which, j, k] = jnp.where(lower_core, one, two)
                sent[which, j, k] = jnp.where(lower_core, two, one)


def fold_kernel(scalars, kept, got, flip_ref, here_ref, there_ref):
    row_step, col_step = scalars[0], scalars[1]
    lanes = lax.broadcasted_iota(jnp.int32, (half, side), 1)
    for which, out_ref in enumerate((here_ref, there_ref)):
        planes = [kept[which, j, k] + got[which, j, k] for j in range(2) for k in range(3)]
        mirror = mirrored(planes, flip_ref)
        for j in range(2):
            power, cross_a, cross_b = planes[3 * j : 3 * j + 3]
            flip_power, flip_a, flip_b = mirror[3 * j : 3 * j + 3]
            cross_a = cross_a + moved(flip_a, 1, col_step)
            cross_b = cross_b + moved(flip_b, row_step, 1)
            out_ref[j, 0:half] = cross_a[:half]
            out_ref[j, half:side] = jnp.where(lanes < half, cross_b[:half], pltpu.roll(cross_b[half:], half, 1))
            out_ref[j, side:folded_rows] = (power + flip_power)[: folded_rows - side]


def solve_kernel(
    scalars, factors, here, there, flip_ref, right, left, right_back, left_back, inverse_eigen, window, upper_ref, lower_ref
):
    row_step, col_step = scalars[0], scalars[1]
    lanes = lax.broadcasted_iota(jnp.int32, (side, side), 1)
    blank = jnp.zeros((half, side), float32)
    planes = []
    for j in range(2):
        both = here[j] + there[j]
        crowded = both[half:side]
        planes.append(jnp.concatenate([both[side:], blank[: 2 * side - folded_rows]], axis=0))
        planes.append(jnp.concatenate([both[:half], blank], axis=0))
        spread = jnp.concatenate([crowded, pltpu.roll(crowded, half, 1)], axis=0)
        planes.append(jnp.where(lanes < half, spread, 0.0))
    mirror = mirrored(planes, flip_ref)
    scale = 0.5 / total_frames
    targets, amplitudes = [], []
    for j in range(2):
        power = jnp.concatenate([planes[3 * j][: folded_rows - side], mirror[3 * j][folded_rows - side :]], axis=0)
        power = power * scale
        cross_a = (planes[3 * j + 1] + moved(mirror[3 * j + 1], 1, col_step)) * scale
        cross_b = (planes[3 * j + 2] + moved(mirror[3 * j + 2], row_step, 1)) * scale
        level = jnp.sum(jnp.sum(power, axis=0, keepdims=True), axis=1, keepdims=True) * (1.0 / (side * side))
        floor = share_term * level * level
        target = jnp.zeros((side, side), float32)
        for cross, rows, cols in ((cross_a, 1, col_step), (cross_b, row_step, 1)):
            partner = moved(power, rows, cols)
            coherence = cross / (jnp.sqrt(power * partner + floor) + tiny_term)
            target = target + coherence - moved_back(coherence, rows, cols)
        targets.append(target)
        amplitudes.append(jnp.sqrt(power))
    z = table_times(left, upright(times_table(jnp.concatenate(targets, axis=1), right)))
    zr = z[:side] * inverse_eigen[...]
    zi = z[side:] * inverse_eigen[...]
    phase = table_times(left_back, upright(times_table(jnp.concatenate([zr, zi], axis=1), right_back)))
    cosine, sine = jnp.cos(phase), jnp.sin(phase)
    first, second = amplitudes
    wr = first * cosine[:side] - second * sine[side:]
    wi = first * sine[:side] + second * cosine[side:]
    rebuilt = table_times(left_back, upright(times_table(jnp.concatenate([wr, wi], axis=1), right_back)))
    first = rebuilt[:side] * (window[...] * factors[0])
    second = pltpu.roll(rebuilt[side:] * (window[...] * factors[1]), half, 1)
    left_part = first + jnp.where(lanes >= half, second, 0.0)
    right_part = jnp.where(lanes < half, second, 0.0)
    block = jnp.concatenate([left_part, right_part], axis=1)
    upper_ref[...] = block[:half]
    lower_ref[...] = block[half:]


def join_kernel(scalars, upper_own, upper_other, lower_own, lower_other, out_ref):
    own = upper_own[...] + lower_own[...]
    other = upper_other[...] + lower_other[...]
    lower_core = scalars[2] == 0
    left = jnp.where(lower_core, own, other)
    right = jnp.where(lower_core, other, own)
    out_ref[:, 0:128] = left[:, :128]
    out_ref[:, 128:256] = left[:, 128:] + right[:, :128]
    out_ref[:, 256:320] = right[:, 128:192]


def inverse_eigen_of(shifts):
    frequency = jnp.arange(side, dtype=jnp.int32)
    total = jnp.full((side, side), ridge_term, float32)
    for s in range(shifts.shape[0]):
        angle = (frequency[:, None] * shifts[s, 0] + frequency[None, :] * shifts[s, 1]) % side
        total = total + 2.0 - 2.0 * jnp.cos(2.0 * jnp.pi * angle.astype(float32) / side)
    return 1.0 / (total * (side * side))


smem = pl.BlockSpec(memory_space=pltpu.SMEM)
vmem = pl.BlockSpec(memory_space=pltpu.VMEM)


def call(kernel, shapes, scalar_count, array_count, scratch=(), flops=0, moved_bytes=0):
    return pl.pallas_call(
        kernel,
        out_shape=[jax.ShapeDtypeStruct(s, float32) for s in shapes],
        in_specs=[smem] * scalar_count + [vmem] * array_count,
        out_specs=[vmem] * len(shapes),
        scratch_shapes=list(scratch),
        compiler_params=pltpu.CompilerParams(vmem_limit_bytes=vmem_limit),
        cost_estimate=pl.CostEstimate(flops=flops, bytes_accessed=moved_bytes, transcendentals=0),
    )


def on_device(frames, live_first, live_count, shifts):
    pairs = frames.shape[0] // 2
    tiles = lax.axis_size("tiles")
    tile = lax.axis_index("tiles")
    core = lax.axis_index("frames") % 2
    tables, flip, window = complex_tables()
    right_taper, left_taper, right, left, right_back, left_back = [jnp.asarray(t) for t in tables]
    flip, window = jnp.asarray(flip), jnp.asarray(window)
    scalars = jnp.stack([shifts[1, 0], shifts[0, 1], core.astype(jnp.int32), (tile == tiles - 1).astype(jnp.int32)])
    columns = 2 * core + jnp.arange(2, dtype=jnp.int32)
    live = (columns >= live_first[0]) & (columns < live_first[0] + live_count[0])
    factors = live.astype(float32)

    each = pairs // 2
    tail = 1
    body = each - tail
    own_l0, own_l1, own_r0, own_r1 = call(
        pack_kernel, [(n, half, pair_width) for n in (body, tail, body, tail)], 0, 1, moved_bytes=4 * 2**20
    )(frames)
    to_left = [(i, i - 1) for i in range(1, tiles)]
    to_right = [(i, i + 1) for i in range(tiles - 1)]
    halo_l0 = lax.ppermute(own_l0, "tiles", to_left)
    halo_r0 = lax.ppermute(own_r0, "tiles", to_right)
    halo_l1 = lax.ppermute(own_l1, "tiles", to_left)
    halo_r1 = lax.ppermute(own_r1, "tiles", to_right)

    sums = (2, 4, 3, side, side)
    (before,) = call(start_kernel, [sums], 1, 4, moved_bytes=2**20)(scalars, own_r0, own_r1, right_taper, left_taper)
    (before,) = call(middle_kernel, [sums], 1, 7, flops=2 * 10**9, moved_bytes=8 * 2**20)(
        scalars, own_l0, halo_l0, own_r0, halo_r0, right_taper, left_taper, before
    )
    parted = (2, 2, 3, side, side)
    kept, sent = call(
        last_kernel, [parted, parted], 1, 7, scratch=[pltpu.VMEM(sums, float32)], flops=10**9, moved_bytes=4 * 2**20
    )(scalars, own_l1, halo_l1, own_r1, halo_r1, right_taper, left_taper, before)

    other_core = [(g, g ^ 1) for g in range(4)]
    other_half = [(g, g ^ 2) for g in range(4)]
    got = lax.ppermute(sent, "frames", other_core)
    folded = (2, folded_rows, side)
    here, there = call(fold_kernel, [folded, folded], 1, 3, flops=10**9, moved_bytes=4 * 2**20)(scalars, kept, got, flip)
    here = here + lax.ppermute(there, "tiles", to_left)
    there = lax.ppermute(here, "frames", other_half)

    block = (half, 2 * side)
    upper, lower = call(solve_kernel, [block, block], 2, 9, flops=10**9, moved_bytes=4 * 2**20)(
        scalars,
        factors,
        here,
        there,
        flip,
        right,
        left,
        right_back,
        left_back,
        inverse_eigen_of(shifts),
        window,
    )
    below_other = [(g * tiles + i, (g ^ 1) * tiles + i + 1) for g in range(4) for i in range(tiles - 1)]
    upper_other = lax.ppermute(upper, "frames", other_core)
    lower_own = lax.ppermute(lower, "tiles", to_right)
    lower_other = lax.ppermute(lower, ("frames", "tiles"), below_other)
    (image,) = call(join_kernel, [(half, width)], 1, 4)(scalars, upper, upper_other, lower_own, lower_other)
    return image


def solution(mesh):
    placed = (P("frames", "tiles", None), P("tiles"), P("tiles"), P())
    return jax.shard_map(on_device, mesh=mesh, in_specs=placed, out_specs=P("tiles", None), check_vma=False)
```

time: 407 us -> 102 us (0.25)
  the two profiles are of different devices: /device:TPU:64 before, /device:TPU:253 now
where the time goes in v1:
time: 102 us; the launch traced here: 101 us
  starting transfers between devices  41.4 us (41%)
  waiting for transfers between devices  31.8 us (31%)
  Pallas kernels  18.6 us (18%)
  other arithmetic  4.26 us (4%)
  local copies, waits for them, and re-layouts  3.36 us (3%)
  between operations  1.56 us (2%)
    ppermute x1, starting transfers between devices, on_device(): lower_own = lax.ppermute(lower, 'tiles', to_right)  13.6 us
    ppermute x1, waiting for transfers between devices, on_device(): here = here + lax.ppermute(there, 'tiles', to_left)  11.9 us
    ppermute x1, waiting for transfers between devices, on_device(): there = lax.ppermute(here, 'frames', other_half)  9.33 us
    pallas_call x1, Pallas kernels, on_device(): call(middle_kernel, [sums], 1, 7, flops=2 * 10 ** 9, moved_bytes=8 * 2 **...  8.34 us
    ppermute x1, starting transfers between devices, on_device(): halo_r1 = lax.ppermute(own_r1, 'tiles', to_right)  6.95 us
    ppermute x1, waiting for transfers between devices, on_device(): halo_l0 = lax.ppermute(own_l0, 'tiles', to_left)  6.56 us
    ppermute x1, starting transfers between devices, on_device(): got = lax.ppermute(sent, 'frames', other_core)  4.6 us
    ppermute x1, waiting for transfers between devices, on_device(): lower_other = lax.ppermute(lower, ('frames', 'tiles'), below_other)  3.94 us
  transfers between devices with their start and end apart: 10, of which 4 were waited for; matrix products, arithmetic and copies ran while one was open for 5% of the time, Pallas kernels for 9%

profile of v1, /device:TPU:253, one launch (start us, length us, event | category | flops | bytes accessed | tf_op | source)
XLA Modules:
  0.0 101.1 jit_solution(10350054229876003334)
XLA Ops:
  0.0 0.0 copy-start
  0.0 1.5 %copy-done = f32[20,64,320]{2,1,0:T(8,128)S(1)} copy-done((f32[20,64,320]{2,1,0:T(8,128)S(1)}, f32[20,64,320]{2,1,0:T(8,128)}, u32[]{:S(2)}) %copy-start) | copy-done | bytes 1638424
  1.5 0.0 copy-start.2
  1.6 0.9 shard_map.118
  2.4 2.8 %collective-permute-start.3 = (f32[4,64,640]{2,1,0:T(8,128)S(1)}, f32[4,64,640]{2,1,0:T(8,128)S(1)}, u32[]{:S(2)}, u32[]{:S(2)}) collective-permute-start(f32[4,64,640]{2,1,0:T(8,128)S(1)} %get-tuple-element.18.own_r0.own_r), channel_id=1, source_target_pairs={{0,1},{1,2},{2,3},{3,4},{4,5},{5,6},{6,7},{7,8},{8,9},{9,10},{10,1... | collective-permute-start | bytes 1966088 | tf_op jit(solution)/shard_map/ppermute | solution.py:298
  5.3 2.5 %collective-permute-start.2 = (f32[4,64,640]{2,1,0:T(8,128)S(1)}, f32[4,64,640]{2,1,0:T(8,128)S(1)}, u32[]{:S(2)}, u32[]{:S(2)}) collective-permute-start(f32[4,64,640]{2,1,0:T(8,128)S(1)} %get-tuple-element.17.own_l), channel_id=1, source_target_pairs={{1,0},{2,1},{3,2},{4,3},{5,4},{6,5},{7,6},{8,7},{9,8},{10,9},{11,1... | collective-permute-start | bytes 1966088 | tf_op jit(solution)/shard_map/ppermute | solution.py:297
  7.7 6.9 %collective-permute-start.1 = (f32[1,64,640]{2,1,0:T(8,128)S(1)}, f32[1,64,640]{2,1,0:T(8,128)}, u32[]{:S(2)}, u32[]{:S(2)}) collective-permute-start(f32[1,64,640]{2,1,0:T(8,128)S(1)} %get-tuple-element.16.own_r1.own_r), channel_id=1, source_target_pairs={{0,1},{1,2},{2,3},{3,4},{4,5},{5,6},{6,7},{7,8},{8,9},{9,10},{10,1... | collective-permute-start | bytes 491528 | tf_op jit(solution)/shard_map/ppermute | solution.py:300
  14.7 1.9 %collective-permute-start = (f32[1,64,640]{2,1,0:T(8,128)S(1)}, f32[1,64,640]{2,1,0:T(8,128)}, u32[]{:S(2)}, u32[]{:S(2)}) collective-permute-start(f32[1,64,640]{2,1,0:T(8,128)S(1)} %get-tuple-element.15.own_l), channel_id=1, source_target_pairs={{1,0},{2,1},{3,2},{4,3},{5,4},{6,5},{7,6},{8,7},{9,8},{10,9},{11,1... | collective-permute-start | bytes 491528 | tf_op jit(solution)/shard_map/ppermute | solution.py:299
  16.6 0.0 copy-done.8
  16.6 0.6 fusion.14
  17.2 1.2 %pad_add_fusion.scalars = s32[4]{0:T(128)S(1)} fusion(s32[1]{0:T(128)} %bitcast.3, s32[1]{0:T(128)} %bitcast.2, s32[1]{0:T(128)} %bitcast.1, s32[1]{0:T(128)} %bitcast), kind=kLoop, calls=%fused_computation.25 | loop fusion | flops 12 | bytes 32 | tf_op jit(solution)/shard_map/stack | solution.py:284
  18.5 0.0 copy-done.2
  18.5 0.0 copy-done.3
  18.5 0.6 shard_map.119.before
  19.1 0.0 copy-start.1
  19.1 1.2 %copy-done.1 = f32[2,4,3,128,128]{4,3,2,1,0:T(8,128)} copy-done((f32[2,4,3,128,128]{4,3,2,1,0:T(8,128)}, f32[2,4,3,128,128]{4,3,2,1,0:T(8,128)S(1)}, u32[]{:S(2)}) %copy-start.1) | copy-done | bytes 1572888
  20.3 0.0 collective-permute-done.3.halo_r
  20.3 6.6 %collective-permute-done.2.halo_l = f32[4,64,640]{2,1,0:T(8,128)S(1)} collective-permute-done((f32[4,64,640]{2,1,0:T(8,128)S(1)}, f32[4,64,640]{2,1,0:T(8,128)S(1)}, u32[]{:S(2)}, u32[]{:S(2)}) %collective-permute-start.2) | collective-permute-done | bytes 655392 | tf_op jit(solution)/shard_map/ppermute | solution.py:297
  26.9 8.3 %shard_map.120.before = f32[2,4,3,128,128]{4,3,2,1,0:T(8,128)S(1)} custom-call(s32[4]{0:T(128)S(1)} %pad_add_fusion.scalars, f32[4,64,640]{2,1,0:T(8,128)S(1)} %get-tuple-element.17.own_l, f32[4,64,640]{2,1,0:T(8,128)S(1)} %collective-permute-done.2.halo_l, f32[4,64,640]{2,1,0:T(8,128)S(1)} %get-tuple-element.18.own_r0.own_r, ...), custom_call_target="tpu_custom_call" | custom-call | flops 2000000000 | bytes 8388608 | tf_op jit(solution)/shard_map/pallas_call | solution.py:304
  35.2 0.0 copy-start.7
  35.2 0.0 collective-permute-done.1.halo_r
  35.2 0.0 collective-permute-done.halo_l
  35.2 2.8 %shard_map.121 = (f32[2,2,3,128,128]{4,3,2,1,0:T(8,128)S(1)}, f32[2,2,3,128,128]{4,3,2,1,0:T(8,128)S(1)}) custom-call(s32[4]{0:T(128)S(1)} %pad_add_fusion.scalars, f32[1,64,640]{2,1,0:T(8,128)S(1)} %get-tuple-element.15.own_l, f32[1,64,640]{2,1,0:T(8,128)} %collective-permute-done.halo_l, f32[1,64,640]{2,1,0:T(8,128)S(1)} %get-tuple-element.16.own_r1.own_r, ...), custom_call_target="tpu_custom_call" | custom-call | flops 1000000000 | bytes 4194304 | tf_op jit(solution)/shard_map/pallas_call | solution.py:308
  38.0 4.6 %collective-permute-start.4 = (f32[2,2,3,128,128]{4,3,2,1,0:T(8,128)S(1)}, f32[2,2,3,128,128]{4,3,2,1,0:T(8,128)S(1)}, u32[]{:S(2)}, u32[]{:S(2)}) collective-permute-start(f32[2,2,3,128,128]{4,3,2,1,0:T(8,128)S(1)} %get-tuple-element.20), channel_id=1, source_target_pairs={{0,128},{128,0},{256,384},{384,256},{1,129},{129,1},{257,385},{385... | collective-permute-start | bytes 2359304 | tf_op jit(solution)/shard_map/ppermute | solution.py:314
  43.9 1.2 %iota_multiply_fusion = (s32[128]{0:T(128)S(1)}, s32[128]{0:T(128)S(1)}) fusion(s32[]{:T(128)} %bitcast.9, s32[]{:T(128)} %bitcast.8), kind=kLoop, calls=%fused_computation.26 | loop fusion | flops 256 | bytes 1032 | tf_op jit(solution)/shard_map/mul | solution.py:255
  45.1 0.0 collective-permute-done.4.got
  45.1 0.0 copy-done.7
  45.1 0.0 copy-start.4
  45.2 0.0 copy-start.5
  45.2 0.0 copy-start.6
  45.2 1.6 %shard_map.122 = (f32[2,200,128]{2,1,0:T(8,128)S(1)}, f32[2,200,128]{2,1,0:T(8,128)S(1)}) custom-call(s32[4]{0:T(128)S(1)} %pad_add_fusion.scalars, f32[2,2,3,128,128]{4,3,2,1,0:T(8,128)S(1)} %get-tuple-element.19.kept, f32[2,2,3,128,128]{4,3,2,1,0:T(8,128)S(1)} %collective-permute-done.4.got, bf16[128,128]{1,0:T(8,128)(2,1)S(1)} %copy-done.7), custom_call_target="tpu_custom_call" | custom-call | flops 1000000000 | bytes 4194304 | tf_op jit(solution)/shard_map/pallas_call | solution.py:316
  46.8 1.9 %collective-permute-start.5 = (f32[2,200,128]{2,1,0:T(8,128)S(1)}, f32[2,200,128]{2,1,0:T(8,128)S(1)}, u32[]{:S(2)}, u32[]{:S(2)}) collective-permute-start(f32[2,200,128]{2,1,0:T(8,128)S(1)} %get-tuple-element.22), channel_id=1, source_target_pairs={{1,0},{2,1},{3,2},{4,3},{5,4},{6,5},{7,6},{8,7},{9,8},{10,9},{11,1... | collective-permute-start | bytes 614408 | tf_op jit(solution)/shard_map/ppermute | solution.py:317
  48.7 1.2 %iota_multiply_fusion.2 = (s32[128]{0:T(128)S(1)}, s32[128]{0:T(128)S(1)}) fusion(s32[]{:T(128)} %bitcast.7, s32[]{:T(128)} %bitcast.6), kind=kLoop, calls=%fused_computation.28 | loop fusion | flops 256 | bytes 1032 | tf_op jit(solution)/shard_map/mul | solution.py:255
  50.0 11.9 %collective-permute-done.5 = f32[2,200,128]{2,1,0:T(8,128)S(1)} collective-permute-done((f32[2,200,128]{2,1,0:T(8,128)S(1)}, f32[2,200,128]{2,1,0:T(8,128)S(1)}, u32[]{:S(2)}, u32[]{:S(2)}) %collective-permute-start.5) | collective-permute-done | bytes 204832 | tf_op jit(solution)/shard_map/ppermute | solution.py:317
  61.9 1.9 %collective-permute-start.6 = (f32[2,200,128]{2,1,0:T(8,128)S(1)}, f32[2,200,128]{2,1,0:T(8,128)S(1)}, u32[]{:S(2)}, u32[]{:S(2)}) collective-permute-start(f32[2,200,128]{2,1,0:T(8,128)S(1)} %add.63.here), channel_id=1, source_target_pairs={{0,256},{128,384},{256,0},{384,128},{1,257},{129,385},{257,1},{385... | collective-permute-start | bytes 614408 | tf_op jit(solution)/shard_map/ppermute | solution.py:318
  63.8 0.6 fusion.7.inverse_eigen
  64.4 9.3 %collective-permute-done.6.there = f32[2,200,128]{2,1,0:T(8,128)S(1)} collective-permute-done((f32[2,200,128]{2,1,0:T(8,128)S(1)}, f32[2,200,128]{2,1,0:T(8,128)S(1)}, u32[]{:S(2)}, u32[]{:S(2)}) %collective-permute-start.6) | collective-permute-done | bytes 204832 | tf_op jit(solution)/shard_map/ppermute | solution.py:318
  73.8 0.0 copy-done.4
  73.8 0.0 copy-done.5
  73.8 0.0 copy-done.6
  73.8 3.3 %shard_map.123 = (f32[64,256]{1,0:T(8,128)S(1)}, f32[64,256]{1,0:T(8,128)S(1)}) custom-call(s32[4]{0:T(128)S(1)} %pad_add_fusion.scalars, f32[2]{0:T(128)S(1)} %and_convert_fusion.factors, f32[2,200,128]{2,1,0:T(8,128)S(1)} %add.63.here, f32[2,200,128]{2,1,0:T(8,128)S(1)} %collective-permute-done.6.there, bf16[128,128]{1,0:T(8,128)(2,1)S(1)} %copy-done.7, ...), custom_call_target="tpu_custom_call" | custom-call | flops 1000000000 | bytes 4194304 | tf_op jit(solution)/shard_map/pallas_call | solution.py:321
  77.0 3.4 %collective-permute-start.7 = (f32[64,256]{1,0:T(8,128)S(1)}, f32[64,256]{1,0:T(8,128)S(1)}, u32[]{:S(2)}, u32[]{:S(2)}) collective-permute-start(f32[64,256]{1,0:T(8,128)S(1)} %get-tuple-element.23.upper_own), channel_id=1, source_target_pairs={{0,128},{128,0},{256,384},{384,256},{1,129},{129,1},{257,385},{385... | collective-permute-start | bytes 196616 | tf_op jit(solution)/shard_map/ppermute | solution.py:335
  80.4 13.6 %collective-permute-start.8 = (f32[64,256]{1,0:T(8,128)S(1)}, f32[64,256]{1,0:T(8,128)S(1)}, u32[]{:S(2)}, u32[]{:S(2)}) collective-permute-start(f32[64,256]{1,0:T(8,128)S(1)} %get-tuple-element.24), channel_id=1, source_target_pairs={{0,1},{1,2},{2,3},{3,4},{4,5},{5,6},{6,7},{7,8},{8,9},{9,10},{10,1... | collective-permute-start | bytes 196616 | tf_op jit(solution)/shard_map/ppermute | solution.py:336
  94.0 1.9 %collective-permute-start.9 = (f32[64,256]{1,0:T(8,128)S(1)}, f32[64,256]{1,0:T(8,128)S(1)}, u32[]{:S(2)}, u32[]{:S(2)}) collective-permute-start(f32[64,256]{1,0:T(8,128)S(1)} %get-tuple-element.24), channel_id=1, source_target_pairs={{0,129},{1,130},{2,131},{3,132},{4,133},{5,134},{6,135},{7,136},{8... | collective-permute-start | bytes 196616 | tf_op jit(solution)/shard_map/ppermute | solution.py:337
  95.9 0.0 collective-permute-done.7.upper_other
  95.9 0.0 collective-permute-done.8.lower_own
  95.9 3.9 %collective-permute-done.9.lower_other = f32[64,256]{1,0:T(8,128)S(1)} collective-permute-done((f32[64,256]{1,0:T(8,128)S(1)}, f32[64,256]{1,0:T(8,128)S(1)}, u32[]{:S(2)}, u32[]{:S(2)}) %collective-permute-start.9) | collective-permute-done | bytes 65568 | tf_op jit(solution)/shard_map/ppermute | solution.py:337
  99.9 1.2 %shard_map.124 = f32[64,320]{1,0:T(8,128)} custom-call(s32[4]{0:T(128)S(1)} %pad_add_fusion.scalars, f32[64,256]{1,0:T(8,128)S(1)} %get-tuple-element.23.upper_own, f32[64,256]{1,0:T(8,128)S(1)} %collective-permute-done.7.upper_other, f32[64,256]{1,0:T(8,128)S(1)} %collective-permute-done.8.lower_own, f32[64,256]{1,0:T(8,128)S(1)} %collective-permute-done.9.lower_other), custom_call_target="tpu_custom_call" | custom-call | tf_op jit(solution)/shard_map/pallas_call | solution.py:338
  (4 shorter events, 0.0 us)
Async XLA Ops:
  0.0 1.5 %copy-start = (f32[20,64,320]{2,1,0:T(8,128)S(1)}, f32[20,64,320]{2,1,0:T(8,128)}, u32[]{:S(2)}) copy-start(f32[20,64,320]{2,1,0:T(8,128)} %frames_ref.1) | copy-start | bytes 4915204
  1.5 15.1 %copy-start.8 = (s32[2,2]{1,0:T(2,128)S(1)}, s32[2,2]{1,0:T(2,128)}, u32[]{:S(2)}) copy-start(s32[2,2]{1,0:T(2,128)} %param.15) | copy-start | bytes 52
  1.5 16.9 %copy-start.2 = (bf16[2,256,256]{2,1,0:T(8,128)(2,1)S(1)}, bf16[2,256,256]{2,1,0:T(8,128)(2,1)}, u32[]{:S(2)}) copy-start(bf16[2,256,256]{2,1,0:T(8,128)(2,1)} %constant.70.clone.right_ref) | copy-start | bytes 786436
  1.6 16.9 %copy-start.3 = (bf16[2,256,256]{2,1,0:T(8,128)(2,1)S(1)}, bf16[2,256,256]{2,1,0:T(8,128)(2,1)}, u32[]{:S(2)}) copy-start(bf16[2,256,256]{2,1,0:T(8,128)(2,1)} %constant.71.clone.left_ref) | copy-start | bytes 786436
  2.4 17.9 %collective-permute-start.3 = (f32[4,64,640]{2,1,0:T(8,128)S(1)}, f32[4,64,640]{2,1,0:T(8,128)S(1)}, u32[]{:S(2)}, u32[]{:S(2)}) collective-permute-start(f32[4,64,640]{2,1,0:T(8,128)S(1)} %get-tuple-element.18.own_r0.own_r), channel_id=1, source_target_pairs={{0,1},{1,2},{2,3},{3,4},{4,5},{5,6},{6,7},{7,8},{8,9},{9,10},{10,1... | collective-permute-start | bytes 1966088 | tf_op jit(solution)/shard_map/ppermute | solution.py:298
  5.3 21.6 %collective-permute-start.2 = (f32[4,64,640]{2,1,0:T(8,128)S(1)}, f32[4,64,640]{2,1,0:T(8,128)S(1)}, u32[]{:S(2)}, u32[]{:S(2)}) collective-permute-start(f32[4,64,640]{2,1,0:T(8,128)S(1)} %get-tuple-element.17.own_l), channel_id=1, source_target_pairs={{1,0},{2,1},{3,2},{4,3},{5,4},{6,5},{7,6},{8,7},{9,8},{10,9},{11,1... | collective-permute-start | bytes 1966088 | tf_op jit(solution)/shard_map/ppermute | solution.py:297
  7.7 27.5 %collective-permute-start.1 = (f32[1,64,640]{2,1,0:T(8,128)S(1)}, f32[1,64,640]{2,1,0:T(8,128)}, u32[]{:S(2)}, u32[]{:S(2)}) collective-permute-start(f32[1,64,640]{2,1,0:T(8,128)S(1)} %get-tuple-element.16.own_r1.own_r), channel_id=1, source_target_pairs={{0,1},{1,2},{2,3},{3,4},{4,5},{5,6},{6,7},{7,8},{8,9},{9,10},{10,1... | collective-permute-start | bytes 491528 | tf_op jit(solution)/shard_map/ppermute | solution.py:300
  14.7 20.6 %collective-permute-start = (f32[1,64,640]{2,1,0:T(8,128)S(1)}, f32[1,64,640]{2,1,0:T(8,128)}, u32[]{:S(2)}, u32[]{:S(2)}) collective-permute-start(f32[1,64,640]{2,1,0:T(8,128)S(1)} %get-tuple-element.15.own_l), channel_id=1, source_target_pairs={{1,0},{2,1},{3,2},{4,3},{5,4},{6,5},{7,6},{8,7},{9,8},{10,9},{11,1... | collective-permute-start | bytes 491528 | tf_op jit(solution)/shard_map/ppermute | solution.py:299
  19.1 1.2 %copy-start.1 = (f32[2,4,3,128,128]{4,3,2,1,0:T(8,128)}, f32[2,4,3,128,128]{4,3,2,1,0:T(8,128)S(1)}, u32[]{:S(2)}) copy-start(f32[2,4,3,128,128]{4,3,2,1,0:T(8,128)S(1)} %shard_map.119.before) | copy-start | bytes 4718596
  35.2 9.9 %copy-start.7 = (bf16[128,128]{1,0:T(8,128)(2,1)S(1)}, bf16[128,128]{1,0:T(8,128)(2,1)}, u32[]{:S(2)}) copy-start(bf16[128,128]{1,0:T(8,128)(2,1)} %constant.74.clone.flip_ref) | copy-start | bytes 98308
  38.0 7.1 %collective-permute-start.4 = (f32[2,2,3,128,128]{4,3,2,1,0:T(8,128)S(1)}, f32[2,2,3,128,128]{4,3,2,1,0:T(8,128)S(1)}, u32[]{:S(2)}, u32[]{:S(2)}) collective-permute-start(f32[2,2,3,128,128]{4,3,2,1,0:T(8,128)S(1)} %get-tuple-element.20), channel_id=1, source_target_pairs={{0,128},{128,0},{256,384},{384,256},{1,129},{129,1},{257,385},{385... | collective-permute-start | bytes 2359304 | tf_op jit(solution)/shard_map/ppermute | solution.py:314
  45.1 28.6 %copy-start.4 = (bf16[2,256,256]{2,1,0:T(8,128)(2,1)S(1)}, bf16[2,256,256]{2,1,0:T(8,128)(2,1)}, u32[]{:S(2)}) copy-start(bf16[2,256,256]{2,1,0:T(8,128)(2,1)} %constant.72.clone.right.left_back) | copy-start | bytes 786436
  45.2 28.6 %copy-start.5 = (bf16[2,256,256]{2,1,0:T(8,128)(2,1)S(1)}, bf16[2,256,256]{2,1,0:T(8,128)(2,1)}, u32[]{:S(2)}) copy-start(bf16[2,256,256]{2,1,0:T(8,128)(2,1)} %constant.73.clone.left.right_back) | copy-start | bytes 786436
  45.2 28.6 %copy-start.6 = (f32[128,128]{1,0:T(8,128)S(1)}, f32[128,128]{1,0:T(8,128)}, u32[]{:S(2)}) copy-start(f32[128,128]{1,0:T(8,128)} %constant.75.clone.window) | copy-start | bytes 196612
  46.8 15.1 %collective-permute-start.5 = (f32[2,200,128]{2,1,0:T(8,128)S(1)}, f32[2,200,128]{2,1,0:T(8,128)S(1)}, u32[]{:S(2)}, u32[]{:S(2)}) collective-permute-start(f32[2,200,128]{2,1,0:T(8,128)S(1)} %get-tuple-element.22), channel_id=1, source_target_pairs={{1,0},{2,1},{3,2},{4,3},{5,4},{6,5},{7,6},{8,7},{9,8},{10,9},{11,1... | collective-permute-start | bytes 614408 | tf_op jit(solution)/shard_map/ppermute | solution.py:317
  61.9 11.8 %collective-permute-start.6 = (f32[2,200,128]{2,1,0:T(8,128)S(1)}, f32[2,200,128]{2,1,0:T(8,128)S(1)}, u32[]{:S(2)}, u32[]{:S(2)}) collective-permute-start(f32[2,200,128]{2,1,0:T(8,128)S(1)} %add.63.here), channel_id=1, source_target_pairs={{0,256},{128,384},{256,0},{384,128},{1,257},{129,385},{257,1},{385... | collective-permute-start | bytes 614408 | tf_op jit(solution)/shard_map/ppermute | solution.py:318
  77.0 18.9 %collective-permute-start.7 = (f32[64,256]{1,0:T(8,128)S(1)}, f32[64,256]{1,0:T(8,128)S(1)}, u32[]{:S(2)}, u32[]{:S(2)}) collective-permute-start(f32[64,256]{1,0:T(8,128)S(1)} %get-tuple-element.23.upper_own), channel_id=1, source_target_pairs={{0,128},{128,0},{256,384},{384,256},{1,129},{129,1},{257,385},{385... | collective-permute-start | bytes 196616 | tf_op jit(solution)/shard_map/ppermute | solution.py:335
  80.4 15.5 %collective-permute-start.8 = (f32[64,256]{1,0:T(8,128)S(1)}, f32[64,256]{1,0:T(8,128)S(1)}, u32[]{:S(2)}, u32[]{:S(2)}) collective-permute-start(f32[64,256]{1,0:T(8,128)S(1)} %get-tuple-element.24), channel_id=1, source_target_pairs={{0,1},{1,2},{2,3},{3,4},{4,5},{5,6},{6,7},{7,8},{8,9},{9,10},{10,1... | collective-permute-start | bytes 196616 | tf_op jit(solution)/shard_map/ppermute | solution.py:336
  94.0 5.9 %collective-permute-start.9 = (f32[64,256]{1,0:T(8,128)S(1)}, f32[64,256]{1,0:T(8,128)S(1)}, u32[]{:S(2)}, u32[]{:S(2)}) collective-permute-start(f32[64,256]{1,0:T(8,128)S(1)} %get-tuple-element.24), channel_id=1, source_target_pairs={{0,129},{1,130},{2,131},{3,132},{4,133},{5,134},{6,135},{7,136},{8... | collective-permute-start | bytes 196616 | tf_op jit(solution)/shard_map/ppermute | solution.py:337

commit v2 on v1

v2 whole, which is shorter than its diff:
```python
import jax
import jax.numpy as jnp
import ml_dtypes
import numpy as np
from jax import lax
from jax.experimental import pallas as pl
from jax.experimental.pallas import tpu as pltpu
from jax.sharding import PartitionSpec as P

ridge_term = 0.1
share_term = 0.0001
tiny_term = 1e-06

side = 128
half = 64
width = 320
quad_width = 4 * width
folded_rows = 200
total_frames = 80
float32 = jnp.float32
bfloat16 = jnp.bfloat16
vmem_limit = 48 * 1024 * 1024


def as_pieces(table):
    upper = table.astype(np.float32).astype(ml_dtypes.bfloat16)
    lower = (table - upper.astype(np.float64)).astype(np.float32).astype(ml_dtypes.bfloat16)
    return upper, lower


def complex_tables():
    index = np.arange(side)
    angle = 2.0 * np.pi * (index[:, None] * index[None, :] % side) / side
    cosine, sine = np.cos(angle), np.sin(angle)
    taper = np.sin(np.pi * (index + 0.5) / side) ** 2
    wc, ws = taper[:, None] * cosine, taper[:, None] * sine
    right_taper = np.block([[wc, -ws], [ws, wc]])
    left_taper = np.block([[wc.T, ws.T], [-ws.T, wc.T]])
    right = np.block([[cosine, -sine], [sine, cosine]])
    left = np.block([[cosine, sine], [-sine, cosine]])
    right_back = np.block([[cosine, sine], [-sine, cosine]])
    left_back = np.block([[cosine, -sine], [sine, cosine]])
    window = (taper[:, None] * taper[None, :] / side**2).astype(np.float32)
    exact = np.stack([right, left, right_back, left_back]).astype(np.float32)
    return [deep(right_taper), wide(left_taper), exact, deep(right_back), wide(left_back), window]


def deep(table):
    upper, lower = as_pieces(table)
    return np.concatenate([upper, upper, lower], axis=0)


def wide(table):
    upper, lower = as_pieces(table)
    return np.concatenate([upper, upper, lower], axis=1)


def pieces(values):
    upper = values.astype(bfloat16)
    lower = (values - upper.astype(float32)).astype(bfloat16)
    return upper, lower


def product(a, b):
    return jnp.dot(a, b, preferred_element_type=float32)


def times_table(values, table):
    upper, lower = pieces(values)
    return product(jnp.concatenate([upper, lower, upper], axis=1), table)


def table_times(table, values):
    upper, lower = pieces(values)
    return product(table, jnp.concatenate([upper, lower, upper], axis=0))


def exactly(a, b):
    return jnp.dot(a, b, precision=lax.Precision.HIGHEST, preferred_element_type=float32)


def upright(g):
    return jnp.concatenate([g[:, :side], g[:, side:]], axis=0)


def moved(values, row_step, col_step):
    return pltpu.roll(pltpu.roll(values, side - col_step, 1), side - row_step, 0)


def moved_back(values, row_step, col_step):
    return pltpu.roll(pltpu.roll(values, col_step, 1), row_step, 0)


def negation(step, twice_axis):
    down = lax.broadcasted_iota(jnp.int32, (side, side), 0)
    across = lax.broadcasted_iota(jnp.int32, (side, side), 1)
    once = jnp.where(((down + across + step) & (side - 1)) == 0, 1.0, 0.0).astype(bfloat16)
    return jnp.concatenate([once, once], axis=twice_axis)


def mirrored(planes, row_step, col_step, rows=side):
    upper, lower = pieces(jnp.concatenate(planes, axis=0))
    tall = product(jnp.concatenate([upper, lower], axis=1), negation(col_step, 0))
    across = jnp.concatenate([tall[i * side : (i + 1) * side] for i in range(len(planes))], axis=1)
    upper, lower = pieces(across)
    across = product(negation(row_step, 1)[:rows], jnp.concatenate([upper, lower], axis=0))
    return [across[:, i * side : (i + 1) * side] for i in range(len(planes))]


def pack_kernel(frames_ref, *out_refs):
    f = 0
    for out_ref in out_refs:
        for quad in range(out_ref.shape[0]):
            for j in range(2):
                one, two = frames_ref[f + j], frames_ref[f + 2 + j]
                base = 2 * width * j
                out_ref[quad, :, base : base + 256] = one[:, :256]
                out_ref[quad, :, base + 256 : base + 512] = two[:, :256]
                out_ref[quad, :, base + 512 : base + 640] = jnp.concatenate([one[:, 256:], two[:, 256:]], axis=1)
            f += 4


def add_quad(upper, lower, row_step, col_step, left, right, spectrum, acc):
    cut = 2 * width
    high, low = pieces(jnp.concatenate([upper[:, :cut], lower[:, :cut], upper[:, cut:], lower[:, cut:]], axis=0))
    g = product(left, jnp.concatenate([high, low, high], axis=0))
    places = []
    for piece in pieces(g):
        column = []
        for p in range(2):
            base = 256 * p
            last = 512 + half * p
            column.append(piece[:, base : base + 128])
            column.append(piece[:, base + half : base + half + 128])
            column.append(piece[:, base + 128 : base + 256])
            column.append(jnp.concatenate([piece[:, base + 192 : base + 256], piece[:, last : last + half]], axis=1))
        places.append(jnp.concatenate([jnp.concatenate([c[:side], c[side:]], axis=1) for c in column], axis=0))
    high, low = places
    z = product(jnp.concatenate([high, low, high], axis=1), right)
    for k in range(8):
        for part in range(2):
            plane = z[k * side : (k + 1) * side, part * side : (part + 1) * side]
            spectrum[k, part, 0:side] = plane
            spectrum[k, part, side : side + half] = plane[:half]
    for c in range(4):
        power, cross_a, cross_b = acc[c, 0], acc[c, 1], acc[c, 2]
        for k in (c, 4 + c):
            zr = z[k * side : (k + 1) * side, :side]
            zi = z[k * side : (k + 1) * side, side:]
            power = power + (zr * zr + zi * zi)
            yr = pltpu.roll(spectrum[k, 0, pl.ds(1, side)], side - col_step, 1)
            yi = pltpu.roll(spectrum[k, 1, pl.ds(1, side)], side - col_step, 1)
            cross_a = cross_a + (zi * yr - zr * yi)
            yr = pltpu.roll(spectrum[k, 0, pl.ds(row_step, side)], side - 1, 1)
            yi = pltpu.roll(spectrum[k, 1, pl.ds(row_step, side)], side - 1, 1)
            cross_b = cross_b + (zi * yr - zr * yi)
        acc[c, 0], acc[c, 1], acc[c, 2] = power, cross_a, cross_b


def number(numbers, i):
    return numbers[i][0, 0]


def fold(acc, row_step, col_step, lower_core, kept, sent):
    lanes = lax.broadcasted_iota(jnp.int32, (half, side), 1)
    top = folded_rows - side
    power = mirrored([acc[c, 0] for c in range(4)], 0, 0, 80)
    cross_a = mirrored([acc[c, 1] for c in range(4)], 1, col_step, half)
    cross_b = mirrored([acc[c, 2] for c in range(4)], row_step, 1)
    planes = []
    for c in range(4):
        total = acc[c, 2] + cross_b[c]
        total = jnp.where(lanes < half, total[:half], pltpu.roll(total[half:], half, 1))
        planes.append((acc[c, 1, :half] + cross_a[c], total, acc[c, 0, :top] + power[c][:top]))
    for j in range(2):
        for one, two, at in zip(planes[j], planes[2 + j], ((0, half), (half, side), (side, folded_rows))):
            kept[j, at[0] : at[1]] = jnp.where(lower_core, one, two)
            sent[j, at[0] : at[1]] = jnp.where(lower_core, two, one)


def start_kernel(numbers, own_r, right_ref, left_ref, out_ref, eigen_ref, spectrum):
    row_step, col_step = number(numbers, 0), number(numbers, 1)
    down = lax.broadcasted_iota(jnp.int32, (side, side), 0)
    across = lax.broadcasted_iota(jnp.int32, (side, side), 1)
    total = jnp.full((side, side), ridge_term, float32)
    for rows, cols in ((1, col_step), (row_step, 1)):
        angle = (down * rows + across * cols) & (side - 1)
        total = total + 2.0 - 2.0 * jnp.cos(angle.astype(float32) * (2.0 * np.pi / side))
    eigen_ref[...] = 1.0 / (total * (side * side))
    out_ref[...] = jnp.zeros_like(out_ref)

    @pl.when(number(numbers, 3) == 1)
    def last_tile():
        blank = jnp.zeros((half, quad_width), float32)

        def body(i, carry):
            add_quad(own_r[i], blank, row_step, col_step, left_ref[...], right_ref[...], spectrum, out_ref)
            return carry

        lax.fori_loop(0, own_r.shape[0], body, 0)


def sum_kernel(numbers, uppers, lowers, right_ref, left_ref, *refs):
    kept, sent, acc, spectrum = refs[-4:]
    row_step, col_step = number(numbers, 0), number(numbers, 1)
    acc[...] = refs[1][...] if len(refs) == 6 else jnp.zeros_like(acc)

    for i in range(uppers.shape[0]):
        add_quad(uppers[i], lowers[i], row_step, col_step, left_ref[...], right_ref[...], spectrum.at[i % 2], acc)
    fold(acc, row_step, col_step, number(numbers, 2) == 0, kept, sent)


def solve_kernel(numbers, here, there, exact, right_back, left_back, inverse_eigen, window, upper_ref, lower_ref):
    row_step, col_step = number(numbers, 0), number(numbers, 1)
    lower_core = number(numbers, 2) == 0
    live_first, live_last = number(numbers, 4), number(numbers, 4) + number(numbers, 5)
    lanes = lax.broadcasted_iota(jnp.int32, (side, side), 1)
    blank = jnp.zeros((half, side), float32)
    powers, crosses_a, crosses_b = [], [], []
    for j in range(2):
        both = here[j] + there[j]
        crowded = both[half:side]
        powers.append(jnp.concatenate([both[side:], blank[: 2 * side - folded_rows]], axis=0))
        crosses_a.append(jnp.concatenate([both[:half], blank], axis=0))
        spread = jnp.concatenate([crowded, pltpu.roll(crowded, half, 1)], axis=0)
        crosses_b.append(jnp.where(lanes < half, spread, 0.0))
    far_powers = mirrored(powers, 0, 0)
    far_a = mirrored(crosses_a, 1, col_step)
    far_b = mirrored(crosses_b, row_step, 1)
    scale = 0.5 / total_frames
    targets, amplitudes = [], []
    for j in range(2):
        power = jnp.concatenate([powers[j][: folded_rows - side], far_powers[j][folded_rows - side :]], axis=0)
        power = power * scale
        cross_a = (crosses_a[j] + far_a[j]) * scale
        cross_b = (crosses_b[j] + far_b[j]) * scale
        level = jnp.sum(jnp.sum(power, axis=0, keepdims=True), axis=1, keepdims=True) * (1.0 / (side * side))
        floor = share_term * level * level
        target = jnp.zeros((side, side), float32)
        for cross, rows, cols in ((cross_a, 1, col_step), (cross_b, row_step, 1)):
            partner = moved(power, rows, cols)
            coherence = cross / (jnp.sqrt(power * partner + floor) + tiny_term)
            target = target + coherence - moved_back(coherence, rows, cols)
        targets.append(target)
        amplitudes.append(jnp.sqrt(power))
    z = exactly(exact[1], upright(exactly(jnp.concatenate(targets, axis=1), exact[0])))
    zr = z[:side] * inverse_eigen[...]
    zi = z[side:] * inverse_eigen[...]
    phase = table_times(left_back[...], upright(times_table(jnp.concatenate([zr, zi], axis=1), right_back[...])))
    cosine, sine = jnp.cos(phase), jnp.sin(phase)
    first, second = amplitudes
    wr = first * cosine[:side] - second * sine[side:]
    wi = first * sine[:side] + second * cosine[side:]
    rebuilt = exactly(exact[3], upright(exactly(jnp.concatenate([wr, wi], axis=1), exact[2])))
    live = []
    for j in range(2):
        c = 2 * number(numbers, 2) + j
        live.append(jnp.where((c >= live_first) & (c < live_last), 1.0, 0.0).astype(float32))
    first = rebuilt[:side] * (window[...] * live[0])
    second = pltpu.roll(rebuilt[side:] * (window[...] * live[1]), half, 1)
    left_part = first + jnp.where(lanes >= half, second, 0.0)
    right_part = jnp.where(lanes < half, second, 0.0)
    for at, part in ((0, left_part), (side, right_part)):
        lower_ref[:, at : at + side] = part[half:]
    place(lower_core, left_part[:half], right_part[:half], upper_ref)


def place(lower_core, left, right, out_ref):
    out_ref[:, 0:128] = jnp.where(lower_core, left, 0.0)
    out_ref[:, 128:256] = jnp.where(lower_core, right, left)
    out_ref[:, 256:320] = jnp.where(lower_core, 0.0, right)[:, :half]


def receive_kernel(numbers, upper, lower, out_ref):
    place(number(numbers, 2) == 0, lower[:, :side], lower[:, side:], out_ref)
    out_ref[...] += upper[...]


vmem = pl.BlockSpec(memory_space=pltpu.VMEM)


def shape_of(dims, dtype=float32):
    return jax.ShapeDtypeStruct(dims, dtype)


def call(kernel, shapes, array_count, scratch=(), flops=0, moved_bytes=0):
    return pl.pallas_call(
        kernel,
        out_shape=shapes,
        in_specs=[vmem] * array_count,
        out_specs=[vmem] * len(shapes),
        scratch_shapes=list(scratch),
        compiler_params=pltpu.CompilerParams(vmem_limit_bytes=vmem_limit),
        cost_estimate=pl.CostEstimate(flops=flops, bytes_accessed=moved_bytes, transcendentals=0),
    )


def on_device(frames, live_first, live_count, shifts):
    tiles = lax.axis_size("tiles")
    tile = lax.axis_index("tiles")
    core = lax.axis_index("frames") % 2
    right_taper, left_taper, exact, right_back, left_back, window = [jnp.asarray(t) for t in complex_tables()]
    numbers = jnp.stack([shifts[1, 0], shifts[0, 1], core, tile == tiles - 1, live_first[0], live_count[0]])
    numbers = jnp.broadcast_to(numbers.astype(jnp.int32)[:, None, None], (6, 8, side))

    to_left = [(i, i - 1) for i in range(1, tiles)]
    to_right = [(i, i + 1) for i in range(tiles - 1)]
    other_core = [(g, g ^ 1) for g in range(4)]
    other_half = [(g, g ^ 2) for g in range(4)]
    count_r = 8
    count_l = frames.shape[0] - count_r
    packed = [shape_of((n // 4, half, quad_width)) for n in (count_l, count_r)]
    own_l, own_r = call(pack_kernel, packed, 1)(frames)
    halo_l = lax.ppermute(own_l, "tiles", to_left)
    halo_r = lax.ppermute(own_r, "tiles", to_right)

    sums, folded = (4, 3, side, side), shape_of((2, folded_rows, side))
    spectrum = pltpu.VMEM((8, 2, side + half, side), float32)
    scratch = [pltpu.VMEM(sums, float32), pltpu.VMEM((2, 8, 2, side + half, side), float32)]
    before, inverse_eigen = call(start_kernel, [shape_of(sums), shape_of((side, side))], 4, [spectrum], 16 * 10**9)(
        numbers, own_r, right_taper, left_taper
    )
    kept, sent = call(sum_kernel, [folded, folded], 6, scratch)(
        numbers, halo_r, own_r, right_taper, left_taper, inverse_eigen
    )
    away = kept + lax.ppermute(sent, "frames", other_core)
    back = lax.ppermute(away, "tiles", to_left)
    kept, sent = call(sum_kernel, [folded, folded], 7, scratch)(
        numbers, own_l, halo_l, right_taper, left_taper, away, before
    )
    here = kept + back + lax.ppermute(sent, "frames", other_core)
    there = lax.ppermute(here, "frames", other_half)

    block = shape_of((half, width))
    upper, lower = call(solve_kernel, [block, shape_of((half, 2 * side))], 8)(
        numbers, here, there, exact, right_back, left_back, inverse_eigen, window
    )
    lower = lax.ppermute(lower, "tiles", to_right)
    (own,) = call(receive_kernel, [block], 3)(numbers, upper, lower)
    return own + lax.ppermute(own, "frames", other_core)


def solution(mesh):
    placed = (P("frames", "tiles", None), P("tiles"), P("tiles"), P())
    return jax.shard_map(on_device, mesh=mesh, in_specs=placed, out_specs=P("tiles", None), check_vma=False)
```

time: 102 us -> 81.9 us (0.80)
  the two profiles are of different devices: /device:TPU:253 before, /device:TPU:257 now
where the time goes in v2:
time: 81.9 us; the launch traced here: 81.5 us
  starting transfers between devices  34.6 us (42%)
  waiting for transfers between devices  27.9 us (34%)
  Pallas kernels  13.2 us (16%)
  local copies, waits for them, and re-layouts  3.53 us (4%)
  between operations  1.5 us (2%)
    ppermute x1, waiting for transfers between devices, on_device(): there = lax.ppermute(here, 'frames', other_half)  9.23 us
    ppermute x1, waiting for transfers between devices, on_device(): halo_r = lax.ppermute(own_r, 'tiles', to_right)  8.44 us
    ppermute x1, starting transfers between devices, on_device(): halo_l = lax.ppermute(own_l, 'tiles', to_left)  8.18 us
    ppermute x1, starting transfers between devices, on_device(): there = lax.ppermute(here, 'frames', other_half)  7.63 us
    ppermute x1, waiting for transfers between devices, on_device(): lower = lax.ppermute(lower, 'tiles', to_right)  7.23 us
    pallas_call x1, Pallas kernels, on_device(): call(sum_kernel, [folded, folded], 6, scratch)  4.56 us
    pallas_call x1, Pallas kernels, on_device(): call(sum_kernel, [folded, folded], 7, scratch)  4.34 us
    ppermute x1, starting transfers between devices, on_device(): return own + lax.ppermute(own, 'frames', other_core)  4.1 us
  transfers between devices with their start and end apart: 8, of which 6 were waited for; matrix products, arithmetic and copies ran while one was open for 2% of the time, Pallas kernels for 12%

profile of v2, /device:TPU:257, one launch (start us, length us, event | category | flops | bytes accessed | tf_op | source)
XLA Modules:
  0.0 81.5 jit_solution(12727978583726911475)
XLA Ops:
  0.0 0.0 copy-start
  0.0 1.5 %copy-done = f32[20,64,320]{2,1,0:T(8,128)S(1)} copy-done((f32[20,64,320]{2,1,0:T(8,128)S(1)}, f32[20,64,320]{2,1,0:T(8,128)}, u32[]{:S(2)}) %copy-start) | copy-done | bytes 1638424
  1.5 0.0 copy-start.7
  1.5 0.0 copy-start.1
  1.6 0.0 copy-start.2
  1.6 0.2 shard_map.100
  1.7 3.3 %collective-permute-start.1 = (f32[2,64,1280]{2,1,0:T(8,128)S(1)}, f32[2,64,1280]{2,1,0:T(8,128)}, u32[]{:S(2)}, u32[]{:S(2)}) collective-permute-start(f32[2,64,1280]{2,1,0:T(8,128)S(1)} %get-tuple-element.16.own_r.lowers), channel_id=1, source_target_pairs={{0,1},{1,2},{2,3},{3,4},{4,5},{5,6},{6,7},{7,8},{8,9},{9,10},{10,1... | collective-permute-start | bytes 1966088 | tf_op jit(solution)/shard_map/ppermute | solution.py:315
  5.0 8.2 %collective-permute-start = (f32[3,64,1280]{2,1,0:T(8,128)S(1)}, f32[3,64,1280]{2,1,0:T(8,128)S(1)}, u32[]{:S(2)}, u32[]{:S(2)}) collective-permute-start(f32[3,64,1280]{2,1,0:T(8,128)S(1)} %get-tuple-element.15.uppers), channel_id=1, source_target_pairs={{1,0},{2,1},{3,2},{4,3},{5,4},{6,5},{7,6},{8,7},{9,8},{10,9},{11,1... | collective-permute-start | bytes 2949128 | tf_op jit(solution)/shard_map/ppermute | solution.py:314
  13.2 0.0 copy-done.7
  13.2 0.6 fusion
  15.1 1.3 %stack.15 = s32[6]{0:T(128)S(1)} concatenate(s32[1]{0:T(128)} %bitcast, s32[1]{0:T(128)} %bitcast.1, s32[1]{0:T(128)} %bitcast.2, s32[1]{0:T(128)} %bitcast.3, s32[1]{0:T(128)S(6)} %copy.11, s32[1]{0:T(128)S(6)} %copy.12), dimensions={0} | concatenate | bytes 48 | tf_op jit(solution)/shard_map/stack | solution.py:303
  16.4 0.1 broadcast_in_dim.2.numbers
  16.5 0.0 copy-done.1
  16.5 0.0 copy-done.2
  16.5 0.6 shard_map.101
  17.0 8.4 %collective-permute-done.1.uppers = f32[2,64,1280]{2,1,0:T(8,128)} collective-permute-done((f32[2,64,1280]{2,1,0:T(8,128)S(1)}, f32[2,64,1280]{2,1,0:T(8,128)}, u32[]{:S(2)}, u32[]{:S(2)}) %collective-permute-start.1) | collective-permute-done | bytes 655392 | tf_op jit(solution)/shard_map/ppermute | solution.py:315
  25.5 4.6 %shard_map.102 = (f32[2,200,128]{2,1,0:T(8,128)S(1)}, f32[2,200,128]{2,1,0:T(8,128)S(1)}) custom-call(s32[6,8,128]{2,1,0:T(8,128)S(1)} %broadcast_in_dim.2.numbers, f32[2,64,1280]{2,1,0:T(8,128)} %collective-permute-done.1.uppers, f32[2,64,1280]{2,1,0:T(8,128)S(1)} %get-tuple-element.16.own_r.lowers, bf16[768,256]{1,0:T(8,128)(2,1)S(1)} %copy-done.1, ...), custom_call_target="tpu_custom_call" | custom-call | tf_op jit(solution)/shard_map/pallas_call | solution.py:323
  30.0 3.4 %collective-permute-start.2 = (f32[2,200,128]{2,1,0:T(8,128)S(1)}, f32[2,200,128]{2,1,0:T(8,128)S(1)}, u32[]{:S(2)}, u32[]{:S(2)}) collective-permute-start(f32[2,200,128]{2,1,0:T(8,128)S(1)} %get-tuple-element.19), channel_id=1, source_target_pairs={{0,128},{128,0},{256,384},{384,256},{1,129},{129,1},{257,385},{385... | collective-permute-start | bytes 614408 | tf_op jit(solution)/shard_map/ppermute | solution.py:326
  33.5 1.1 %collective-permute-done.2 = f32[2,200,128]{2,1,0:T(8,128)S(1)} collective-permute-done((f32[2,200,128]{2,1,0:T(8,128)S(1)}, f32[2,200,128]{2,1,0:T(8,128)S(1)}, u32[]{:S(2)}, u32[]{:S(2)}) %collective-permute-start.2) | collective-permute-done | bytes 204832 | tf_op jit(solution)/shard_map/ppermute | solution.py:326
  34.6 1.9 %collective-permute-start.3 = (f32[2,200,128]{2,1,0:T(8,128)S(1)}, f32[2,200,128]{2,1,0:T(8,128)S(1)}, u32[]{:S(2)}, u32[]{:S(2)}) collective-permute-start(f32[2,200,128]{2,1,0:T(8,128)S(1)} %add.17.refs_0_), channel_id=1, source_target_pairs={{1,0},{2,1},{3,2},{4,3},{5,4},{6,5},{7,6},{8,7},{9,8},{10,9},{11,1... | collective-permute-start | bytes 614408 | tf_op jit(solution)/shard_map/ppermute | solution.py:327
  36.5 0.0 collective-permute-done.lowers
  36.5 0.0 copy-start.3
  36.5 0.0 copy-start.4
  36.6 0.0 copy-start.5
  36.6 0.0 copy-start.6
  36.6 4.3 %shard_map.103 = (f32[2,200,128]{2,1,0:T(8,128)S(1)}, f32[2,200,128]{2,1,0:T(8,128)S(1)}) custom-call(s32[6,8,128]{2,1,0:T(8,128)S(1)} %broadcast_in_dim.2.numbers, f32[3,64,1280]{2,1,0:T(8,128)S(1)} %get-tuple-element.15.uppers, f32[3,64,1280]{2,1,0:T(8,128)S(1)} %collective-permute-done.lowers, bf16[768,256]{1,0:T(8,128)(2,1)S(1)} %copy-done.1, ...), custom_call_target="tpu_custom_call" | custom-call | tf_op jit(solution)/shard_map/pallas_call | solution.py:328
  40.9 2.3 %collective-permute-start.4 = (f32[2,200,128]{2,1,0:T(8,128)S(1)}, f32[2,200,128]{2,1,0:T(8,128)S(1)}, u32[]{:S(2)}, u32[]{:S(2)}) collective-permute-start(f32[2,200,128]{2,1,0:T(8,128)S(1)} %get-tuple-element.22), channel_id=1, source_target_pairs={{0,128},{128,0},{256,384},{384,256},{1,129},{129,1},{257,385},{385... | collective-permute-start | bytes 614408 | tf_op jit(solution)/shard_map/ppermute | solution.py:331
  43.2 0.0 collective-permute-done.3
  43.2 1.0 %collective-permute-done.4 = f32[2,200,128]{2,1,0:T(8,128)S(1)} collective-permute-done((f32[2,200,128]{2,1,0:T(8,128)S(1)}, f32[2,200,128]{2,1,0:T(8,128)S(1)}, u32[]{:S(2)}, u32[]{:S(2)}) %collective-permute-start.4) | collective-permute-done | bytes 204832 | tf_op jit(solution)/shard_map/ppermute | solution.py:331
  44.3 7.6 %collective-permute-start.5 = (f32[2,200,128]{2,1,0:T(8,128)S(1)}, f32[2,200,128]{2,1,0:T(8,128)S(1)}, u32[]{:S(2)}, u32[]{:S(2)}) collective-permute-start(f32[2,200,128]{2,1,0:T(8,128)S(1)} %add_add_fusion.here), channel_id=1, source_target_pairs={{0,256},{128,384},{256,0},{384,128},{1,257},{129,385},{257,1},{385... | collective-permute-start | bytes 614408 | tf_op jit(solution)/shard_map/ppermute | solution.py:332
  52.0 9.2 %collective-permute-done.5.there = f32[2,200,128]{2,1,0:T(8,128)S(1)} collective-permute-done((f32[2,200,128]{2,1,0:T(8,128)S(1)}, f32[2,200,128]{2,1,0:T(8,128)S(1)}, u32[]{:S(2)}, u32[]{:S(2)}) %collective-permute-start.5) | collective-permute-done | bytes 204832 | tf_op jit(solution)/shard_map/ppermute | solution.py:332
  61.2 0.0 copy-done.3
  61.2 0.0 copy-done.4
  61.2 0.0 copy-done.5
  61.2 0.0 copy-done.6
  61.2 3.5 %shard_map.104 = (f32[64,320]{1,0:T(8,128)S(1)}, f32[64,256]{1,0:T(8,128)S(1)}) custom-call(s32[6,8,128]{2,1,0:T(8,128)S(1)} %broadcast_in_dim.2.numbers, f32[2,200,128]{2,1,0:T(8,128)S(1)} %add_add_fusion.here, f32[2,200,128]{2,1,0:T(8,128)S(1)} %collective-permute-done.5.there, f32[4,256,256]{2,1,0:T(8,128)S(1)} %copy-done.3, ...), custom_call_target="tpu_custom_call" | custom-call | tf_op jit(solution)/shard_map/pallas_call | solution.py:335
  64.7 3.8 %collective-permute-start.6 = (f32[64,256]{1,0:T(8,128)S(1)}, f32[64,256]{1,0:T(8,128)S(1)}, u32[]{:S(2)}, u32[]{:S(2)}) collective-permute-start(f32[64,256]{1,0:T(8,128)S(1)} %get-tuple-element.24), channel_id=1, source_target_pairs={{0,1},{1,2},{2,3},{3,4},{4,5},{5,6},{6,7},{7,8},{8,9},{9,10},{10,1... | collective-permute-start | bytes 196616 | tf_op jit(solution)/shard_map/ppermute | solution.py:338
  68.5 7.2 %collective-permute-done.6.lower = f32[64,256]{1,0:T(8,128)S(1)} collective-permute-done((f32[64,256]{1,0:T(8,128)S(1)}, f32[64,256]{1,0:T(8,128)S(1)}, u32[]{:S(2)}, u32[]{:S(2)}) %collective-permute-start.6) | collective-permute-done | bytes 65568 | tf_op jit(solution)/shard_map/ppermute | solution.py:338
  75.7 0.1 shard_map.105
  75.8 4.1 %collective-permute-start.7 = (f32[64,320]{1,0:T(8,128)S(1)}, f32[64,320]{1,0:T(8,128)S(1)}, u32[]{:S(2)}, u32[]{:S(2)}) collective-permute-start(f32[64,320]{1,0:T(8,128)S(1)} %shard_map.105), channel_id=1, source_target_pairs={{0,128},{128,0},{256,384},{384,256},{1,129},{129,1},{257,385},{385... | collective-permute-start | bytes 245768 | tf_op jit(solution)/shard_map/ppermute | solution.py:340
  79.9 0.9 %collective-permute-done.7 = f32[64,320]{1,0:T(8,128)S(1)} collective-permute-done((f32[64,320]{1,0:T(8,128)S(1)}, f32[64,320]{1,0:T(8,128)S(1)}, u32[]{:S(2)}, u32[]{:S(2)}) %collective-permute-start.7) | collective-permute-done | bytes 81952 | tf_op jit(solution)/shard_map/ppermute | solution.py:340
  80.8 0.7 add.20
  (2 shorter events, 0.1 us)
Async XLA Ops:
  0.0 1.5 %copy-start = (f32[20,64,320]{2,1,0:T(8,128)S(1)}, f32[20,64,320]{2,1,0:T(8,128)}, u32[]{:S(2)}) copy-start(f32[20,64,320]{2,1,0:T(8,128)} %frames_ref.1) | copy-start | bytes 4915204
  1.5 11.6 %copy-start.7 = (s32[2,2]{1,0:T(2,128)S(1)}, s32[2,2]{1,0:T(2,128)}, u32[]{:S(2)}) copy-start(s32[2,2]{1,0:T(2,128)} %param.13) | copy-start | bytes 52
  1.5 14.9 %copy-start.1 = (bf16[768,256]{1,0:T(8,128)(2,1)S(1)}, bf16[768,256]{1,0:T(8,128)(2,1)}, u32[]{:S(2)}) copy-start(bf16[768,256]{1,0:T(8,128)(2,1)} %constant.36.clone.right_ref) | copy-start | bytes 1179652
  1.6 14.9 %copy-start.2 = (bf16[256,768]{1,0:T(8,128)(2,1)S(1)}, bf16[256,768]{1,0:T(8,128)(2,1)}, u32[]{:S(2)}) copy-start(bf16[256,768]{1,0:T(8,128)(2,1)} %constant.37.clone.left_ref) | copy-start | bytes 1179652
  1.7 23.7 %collective-permute-start.1 = (f32[2,64,1280]{2,1,0:T(8,128)S(1)}, f32[2,64,1280]{2,1,0:T(8,128)}, u32[]{:S(2)}, u32[]{:S(2)}) collective-permute-start(f32[2,64,1280]{2,1,0:T(8,128)S(1)} %get-tuple-element.16.own_r.lowers), channel_id=1, source_target_pairs={{0,1},{1,2},{2,3},{3,4},{4,5},{5,6},{6,7},{7,8},{8,9},{9,10},{10,1... | collective-permute-start | bytes 1966088 | tf_op jit(solution)/shard_map/ppermute | solution.py:315
  5.0 31.5 %collective-permute-start = (f32[3,64,1280]{2,1,0:T(8,128)S(1)}, f32[3,64,1280]{2,1,0:T(8,128)S(1)}, u32[]{:S(2)}, u32[]{:S(2)}) collective-permute-start(f32[3,64,1280]{2,1,0:T(8,128)S(1)} %get-tuple-element.15.uppers), channel_id=1, source_target_pairs={{1,0},{2,1},{3,2},{4,3},{5,4},{6,5},{7,6},{8,7},{9,8},{10,9},{11,1... | collective-permute-start | bytes 2949128 | tf_op jit(solution)/shard_map/ppermute | solution.py:314
  30.0 4.5 %collective-permute-start.2 = (f32[2,200,128]{2,1,0:T(8,128)S(1)}, f32[2,200,128]{2,1,0:T(8,128)S(1)}, u32[]{:S(2)}, u32[]{:S(2)}) collective-permute-start(f32[2,200,128]{2,1,0:T(8,128)S(1)} %get-tuple-element.19), channel_id=1, source_target_pairs={{0,128},{128,0},{256,384},{384,256},{1,129},{129,1},{257,385},{385... | collective-permute-start | bytes 614408 | tf_op jit(solution)/shard_map/ppermute | solution.py:326
  34.6 8.6 %collective-permute-start.3 = (f32[2,200,128]{2,1,0:T(8,128)S(1)}, f32[2,200,128]{2,1,0:T(8,128)S(1)}, u32[]{:S(2)}, u32[]{:S(2)}) collective-permute-start(f32[2,200,128]{2,1,0:T(8,128)S(1)} %add.17.refs_0_), channel_id=1, source_target_pairs={{1,0},{2,1},{3,2},{4,3},{5,4},{6,5},{7,6},{8,7},{9,8},{10,9},{11,1... | collective-permute-start | bytes 614408 | tf_op jit(solution)/shard_map/ppermute | solution.py:327
  36.5 24.7 %copy-start.3 = (f32[4,256,256]{2,1,0:T(8,128)S(1)}, f32[4,256,256]{2,1,0:T(8,128)}, u32[]{:S(2)}) copy-start(f32[4,256,256]{2,1,0:T(8,128)} %constant.38.clone.exact) | copy-start | bytes 3145732
  36.5 24.7 %copy-start.4 = (bf16[768,256]{1,0:T(8,128)(2,1)S(1)}, bf16[768,256]{1,0:T(8,128)(2,1)}, u32[]{:S(2)}) copy-start(bf16[768,256]{1,0:T(8,128)(2,1)} %constant.39.clone.right_back) | copy-start | bytes 1179652
  36.6 24.7 %copy-start.5 = (bf16[256,768]{1,0:T(8,128)(2,1)S(1)}, bf16[256,768]{1,0:T(8,128)(2,1)}, u32[]{:S(2)}) copy-start(bf16[256,768]{1,0:T(8,128)(2,1)} %constant.40.clone.left_back) | copy-start | bytes 1179652
  36.6 24.6 %copy-start.6 = (f32[128,128]{1,0:T(8,128)S(1)}, f32[128,128]{1,0:T(8,128)}, u32[]{:S(2)}) copy-start(f32[128,128]{1,0:T(8,128)} %constant.41.clone.window) | copy-start | bytes 196612
  40.9 3.3 %collective-permute-start.4 = (f32[2,200,128]{2,1,0:T(8,128)S(1)}, f32[2,200,128]{2,1,0:T(8,128)S(1)}, u32[]{:S(2)}, u32[]{:S(2)}) collective-permute-start(f32[2,200,128]{2,1,0:T(8,128)S(1)} %get-tuple-element.22), channel_id=1, source_target_pairs={{0,128},{128,0},{256,384},{384,256},{1,129},{129,1},{257,385},{385... | collective-permute-start | bytes 614408 | tf_op jit(solution)/shard_map/ppermute | solution.py:331
  44.3 16.9 %collective-permute-start.5 = (f32[2,200,128]{2,1,0:T(8,128)S(1)}, f32[2,200,128]{2,1,0:T(8,128)S(1)}, u32[]{:S(2)}, u32[]{:S(2)}) collective-permute-start(f32[2,200,128]{2,1,0:T(8,128)S(1)} %add_add_fusion.here), channel_id=1, source_target_pairs={{0,256},{128,384},{256,0},{384,128},{1,257},{129,385},{257,1},{385... | collective-permute-start | bytes 614408 | tf_op jit(solution)/shard_map/ppermute | solution.py:332
  64.7 11.0 %collective-permute-start.6 = (f32[64,256]{1,0:T(8,128)S(1)}, f32[64,256]{1,0:T(8,128)S(1)}, u32[]{:S(2)}, u32[]{:S(2)}) collective-permute-start(f32[64,256]{1,0:T(8,128)S(1)} %get-tuple-element.24), channel_id=1, source_target_pairs={{0,1},{1,2},{2,3},{3,4},{4,5},{5,6},{6,7},{7,8},{8,9},{9,10},{10,1... | collective-permute-start | bytes 196616 | tf_op jit(solution)/shard_map/ppermute | solution.py:338
  75.8 5.0 %collective-permute-start.7 = (f32[64,320]{1,0:T(8,128)S(1)}, f32[64,320]{1,0:T(8,128)S(1)}, u32[]{:S(2)}, u32[]{:S(2)}) collective-permute-start(f32[64,320]{1,0:T(8,128)S(1)} %shard_map.105), channel_id=1, source_target_pairs={{0,128},{128,0},{256,384},{384,256},{1,129},{129,1},{257,385},{385... | collective-permute-start | bytes 245768 | tf_op jit(solution)/shard_map/ppermute | solution.py:340

commit v3 on v2

--- a/solution.py
+++ b/solution.py
@@ -42,7 +42,9 @@
     left_back = np.block([[cosine, -sine], [sine, cosine]])
     window = (taper[:, None] * taper[None, :] / side**2).astype(np.float32)
     exact = np.stack([right, left, right_back, left_back]).astype(np.float32)
-    return [deep(right_taper), wide(left_taper), exact, deep(right_back), wide(left_back), window]
+    rows = np.concatenate([index[:half], side + index[:half]])
+    tapers = [deep(right_taper), wide(left_taper[:, rows]), wide(left_taper[:, rows + half])]
+    return [*tapers, exact, deep(right_back), wide(left_back), window]
 
 
 def deep(table):
@@ -120,10 +122,12 @@
             f += 4
 
 
-def add_quad(upper, lower, row_step, col_step, left, right, spectrum, acc):
-    cut = 2 * width
-    high, low = pieces(jnp.concatenate([upper[:, :cut], lower[:, :cut], upper[:, cut:], lower[:, cut:]], axis=0))
-    g = product(left, jnp.concatenate([high, low, high], axis=0))
+def rows_of(block, table):
+    high, low = pieces(jnp.concatenate([block[:, : 2 * width], block[:, 2 * width :]], axis=0))
+    return product(table, jnp.concatenate([high, low, high], axis=0))
+
+
+def add_quad(g, row_step, col_step, right, spectrum, acc):
     places = []
     for piece in pieces(g):
         column = []
@@ -178,7 +182,9 @@
             sent[j, at[0] : at[1]] = jnp.where(lower_core, two, one)
 
 
-def start_kernel(numbers, own_r, right_ref, left_ref, out_ref, eigen_ref, spectrum):
+def start_kernel(
+    numbers, own_l, own_r, right_ref, upper_ref, lower_ref, out_ref, eigen_ref, rows_l_ref, rows_r_ref, spectrum
+):
     row_step, col_step = number(numbers, 0), number(numbers, 1)
     down = lax.broadcasted_iota(jnp.int32, (side, side), 0)
     across = lax.broadcasted_iota(jnp.int32, (side, side), 1)
@@ -188,26 +194,45 @@
         total = total + 2.0 - 2.0 * jnp.cos(angle.astype(float32) * (2.0 * np.pi / side))
     eigen_ref[...] = 1.0 / (total * (side * side))
     out_ref[...] = jnp.zeros_like(out_ref)
+    for i in range(own_l.shape[0]):
+        rows_l_ref[i] = rows_of(own_l[i], upper_ref[...])
+    for i in range(own_r.shape[0]):
+        rows_r_ref[i] = rows_of(own_r[i], lower_ref[...])
 
     @pl.when(number(numbers, 3) == 1)
     def last_tile():
-        blank = jnp.zeros((half, quad_width), float32)
-
         def body(i, carry):
-            add_quad(own_r[i], blank, row_step, col_step, left_ref[...], right_ref[...], spectrum, out_ref)
+            add_quad(rows_of(own_r[i], upper_ref[...]), row_step, col_step, right_ref[...], spectrum, out_ref)
             return carry
 
         lax.fori_loop(0, own_r.shape[0], body, 0)
 
 
-def sum_kernel(numbers, uppers, lowers, right_ref, left_ref, *refs):
+def sum_kernel(numbers, own, halo, right_ref, left_ref, *refs):
     kept, sent, acc, spectrum = refs[-4:]
     row_step, col_step = number(numbers, 0), number(numbers, 1)
     acc[...] = refs[1][...] if len(refs) == 6 else jnp.zeros_like(acc)
-
-    for i in range(uppers.shape[0]):
-        add_quad(uppers[i], lowers[i], row_step, col_step, left_ref[...], right_ref[...], spectrum.at[i % 2], acc)
+    for i in range(halo.shape[0]):
+        g = own[i] + rows_of(halo[i], left_ref[...])
+        add_quad(g, row_step, col_step, right_ref[...], spectrum.at[i % 2], acc)
     fold(acc, row_step, col_step, number(numbers, 2) == 0, kept, sent)
+
+
+def wave(angle):
+    turns = jnp.floor(angle * (2.0 / np.pi) + 0.5)
+    rest = angle - turns * np.float32(1.5703125)
+    rest = rest - turns * np.float32(4.837512969970703125e-4)
+    rest = rest - turns * np.float32(7.549789948768648e-8)
+    square = rest * rest
+    sine = rest + rest * square * (-1.6666654611e-1 + square * (8.3321608736e-3 - square * 1.9515295891e-4))
+    cosine = 1.0 - 0.5 * square + square * square * (4.166664568298827e-2 + square * (-1.388731625493765e-3 + square * 2.443315711809948e-5))
+    quarter = turns.astype(jnp.int32)
+    odd = (quarter & 1) == 1
+    first = jnp.where(odd, sine, cosine)
+    second = jnp.where(odd, cosine, sine)
+    first = jnp.where(((quarter + 1) & 2) == 2, -first, first)
+    second = jnp.where((quarter & 2) == 2, -second, second)
+    return first, second
 
 
 def solve_kernel(numbers, here, there, exact, right_back, left_back, inverse_eigen, window, upper_ref, lower_ref):
@@ -247,7 +272,7 @@
     zr = z[:side] * inverse_eigen[...]
     zi = z[side:] * inverse_eigen[...]
     phase = table_times(left_back[...], upright(times_table(jnp.concatenate([zr, zi], axis=1), right_back[...])))
-    cosine, sine = jnp.cos(phase), jnp.sin(phase)
+    cosine, sine = wave(phase)
     first, second = amplitudes
     wr = first * cosine[:side] - second * sine[side:]
     wi = first * sine[:side] + second * cosine[side:]
@@ -299,7 +324,7 @@
     tiles = lax.axis_size("tiles")
     tile = lax.axis_index("tiles")
     core = lax.axis_index("frames") % 2
-    right_taper, left_taper, exact, right_back, left_back, window = [jnp.asarray(t) for t in complex_tables()]
+    right_taper, upper_taper, lower_taper, exact, right_back, left_back, window = [jnp.asarray(t) for t in complex_tables()]
     numbers = jnp.stack([shifts[1, 0], shifts[0, 1], core, tile == tiles - 1, live_first[0], live_count[0]])
     numbers = jnp.broadcast_to(numbers.astype(jnp.int32)[:, None, None], (6, 8, side))
 
@@ -317,16 +342,18 @@
     sums, folded = (4, 3, side, side), shape_of((2, folded_rows, side))
     spectrum = pltpu.VMEM((8, 2, side + half, side), float32)
     scratch = [pltpu.VMEM(sums, float32), pltpu.VMEM((2, 8, 2, side + half, side), float32)]
-    before, inverse_eigen = call(start_kernel, [shape_of(sums), shape_of((side, side))], 4, [spectrum], 16 * 10**9)(
-        numbers, own_r, right_taper, left_taper
+    tables = [shape_of(sums), shape_of((side, side))]
+    tables += [shape_of((n // 4, 2 * side, 2 * width)) for n in (count_l, count_r)]
+    before, inverse_eigen, rows_l, rows_r = call(start_kernel, tables, 6, [spectrum], 16 * 10**9)(
+        numbers, own_l, own_r, right_taper, upper_taper, lower_taper
     )
     kept, sent = call(sum_kernel, [folded, folded], 6, scratch)(
-        numbers, halo_r, own_r, right_taper, left_taper, inverse_eigen
+        numbers, rows_r, halo_r, right_taper, upper_taper, inverse_eigen
     )
     away = kept + lax.ppermute(sent, "frames", other_core)
     back = lax.ppermute(away, "tiles", to_left)
     kept, sent = call(sum_kernel, [folded, folded], 7, scratch)(
-        numbers, own_l, halo_l, right_taper, left_taper, away, before
+        numbers, rows_l, halo_l, right_taper, lower_taper, away, before
     )
     here = kept + back + lax.ppermute(sent, "frames", other_core)
     there = lax.ppermute(here, "frames", other_half)

time: 81.9 us -> 80.2 us (0.979)
  waiting for transfers between devices: 27.9 us -> 24.8 us
  Pallas kernels: 13.2 us -> 14.9 us
    pallas_call x1, Pallas kernels: 0.57 us -> 3.89 us  [on_device(): call(start_kernel, tables, 6, [spectrum], 16 * 10 ** 9)]
    ppermute x1, waiting for transfers between devices: 8.44 us -> 5.16 us  [on_device(): halo_r = lax.ppermute(own_r, 'tiles', to_right)]
    pallas_call x1, Pallas kernels: 4.56 us -> 2.86 us  [on_device(): call(sum_kernel, [folded, folded], 6, scratch)]
    pallas_call x1, Pallas kernels: 0.17 us -> 1 us  [on_device(): own_l, own_r = call(pack_kernel, packed, 1)(frames)]
  transfers between devices with their start and end apart: 8 -> 8, of which waited for: 6 -> 6; matrix products, arithmetic and copies ran while one was open for 2% -> 3% of each run, Pallas kernels for 12% -> 13%
where the time goes in v3:
time: 80.2 us; the launch traced here: 79.8 us
  starting transfers between devices  34.3 us (43%)
  waiting for transfers between devices  24.8 us (31%)
  Pallas kernels  14.9 us (19%)
  local copies, waits for them, and re-layouts  3.6 us (4%)
  between operations  1.5 us (2%)
    ppermute x1, waiting for transfers between devices, on_device(): there = lax.ppermute(here, 'frames', other_half)  9.41 us
    ppermute x1, starting transfers between devices, on_device(): halo_l = lax.ppermute(own_l, 'tiles', to_left)  8.18 us
    ppermute x1, starting transfers between devices, on_device(): there = lax.ppermute(here, 'frames', other_half)  7.45 us
    ppermute x1, waiting for transfers between devices, on_device(): lower = lax.ppermute(lower, 'tiles', to_right)  7.24 us
    ppermute x1, waiting for transfers between devices, on_device(): halo_r = lax.ppermute(own_r, 'tiles', to_right)  5.16 us
    ppermute x1, starting transfers between devices, on_device(): return own + lax.ppermute(own, 'frames', other_core)  4.09 us
    pallas_call x1, Pallas kernels, on_device(): call(start_kernel, tables, 6, [spectrum], 16 * 10 ** 9)  3.89 us
    pallas_call x1, Pallas kernels, on_device(): call(sum_kernel, [folded, folded], 7, scratch)  3.88 us
  transfers between devices with their start and end apart: 8, of which 6 were waited for; matrix products, arithmetic and copies ran while one was open for 3% of the time, Pallas kernels for 13%

profile of v3, /device:TPU:257, one launch (start us, length us, event | category | flops | bytes accessed | tf_op | source)
XLA Modules:
  0.0 79.8 jit_solution(11915219665668514817)
XLA Ops:
  0.0 0.0 copy-start
  0.0 1.5 %copy-done = f32[20,64,320]{2,1,0:T(8,128)S(1)} copy-done((f32[20,64,320]{2,1,0:T(8,128)S(1)}, f32[20,64,320]{2,1,0:T(8,128)}, u32[]{:S(2)}) %copy-start) | copy-done | bytes 1638424
  1.5 0.0 copy-start.9
  1.5 0.0 copy-start.2
  1.6 0.0 copy-start.6
  1.6 0.0 copy-start.7
  1.6 1.0 %shard_map.109 = (f32[3,64,1280]{2,1,0:T(8,128)S(1)}, f32[2,64,1280]{2,1,0:T(8,128)}) custom-call(f32[20,64,320]{2,1,0:T(8,128)S(1)} %copy-done), custom_call_target="tpu_custom_call" | custom-call | tf_op jit(solution)/shard_map/pallas_call | solution.py:338
  2.6 3.1 %collective-permute-start.1 = (f32[2,64,1280]{2,1,0:T(8,128)}, f32[2,64,1280]{2,1,0:T(8,128)S(1)}, u32[]{:S(2)}, u32[]{:S(2)}) collective-permute-start(f32[2,64,1280]{2,1,0:T(8,128)} %get-tuple-element.18.own_r), channel_id=1, source_target_pairs={{0,1},{1,2},{2,3},{3,4},{4,5},{5,6},{6,7},{7,8},{8,9},{9,10},{10,1... | collective-permute-start | bytes 1966088 | tf_op jit(solution)/shard_map/ppermute | solution.py:340
  5.7 8.2 %collective-permute-start = (f32[3,64,1280]{2,1,0:T(8,128)S(1)}, f32[3,64,1280]{2,1,0:T(8,128)S(1)}, u32[]{:S(2)}, u32[]{:S(2)}) collective-permute-start(f32[3,64,1280]{2,1,0:T(8,128)S(1)} %get-tuple-element.17.own_l), channel_id=1, source_target_pairs={{1,0},{2,1},{3,2},{4,3},{5,4},{6,5},{7,6},{8,7},{9,8},{10,9},{11,1... | collective-permute-start | bytes 2949128 | tf_op jit(solution)/shard_map/ppermute | solution.py:339
  13.9 0.0 copy-done.9
  13.9 0.6 fusion
  15.8 1.4 %stack.15 = s32[6]{0:T(128)S(1)} concatenate(s32[1]{0:T(128)} %bitcast, s32[1]{0:T(128)} %bitcast.1, s32[1]{0:T(128)} %bitcast.2, s32[1]{0:T(128)} %bitcast.3, s32[1]{0:T(128)S(6)} %copy.12, s32[1]{0:T(128)S(6)} %copy.13), dimensions={0} | concatenate | bytes 48 | tf_op jit(solution)/shard_map/stack | solution.py:328
  17.1 0.1 broadcast_in_dim.2.numbers
  17.2 0.0 copy-done.2
  17.2 0.0 copy-done.6
  17.2 0.0 copy-done.7
  17.2 3.9 %shard_map.110 = (f32[4,3,128,128]{3,2,1,0:T(8,128)S(1)}, f32[128,128]{1,0:T(8,128)S(1)}, f32[3,256,640]{2,1,0:T(8,128)}, f32[2,256,640]{2,1,0:T(8,128)S(1)}) custom-call(s32[6,8,128]{2,1,0:T(8,128)S(1)} %broadcast_in_dim.2.numbers, f32[3,64,1280]{2,1,0:T(8,128)S(1)} %get-tuple-element.17.own_l, f32[2,64,1280]{2,1,0:T(8,128)} %get-tuple-element.18.own_r, ...), custom_call_target="tpu_custom_call" | custom-call | flops 16000000000 | tf_op jit(solution)/shard_map/pallas_call | solution.py:347
  21.1 0.0 copy-start.1
  21.1 5.2 %collective-permute-done.1.halo = f32[2,64,1280]{2,1,0:T(8,128)S(1)} collective-permute-done((f32[2,64,1280]{2,1,0:T(8,128)}, f32[2,64,1280]{2,1,0:T(8,128)S(1)}, u32[]{:S(2)}, u32[]{:S(2)}) %collective-permute-start.1) | collective-permute-done | bytes 655392 | tf_op jit(solution)/shard_map/ppermute | solution.py:340
  26.3 2.9 %shard_map.111 = (f32[2,200,128]{2,1,0:T(8,128)S(1)}, f32[2,200,128]{2,1,0:T(8,128)S(1)}) custom-call(s32[6,8,128]{2,1,0:T(8,128)S(1)} %broadcast_in_dim.2.numbers, f32[2,256,640]{2,1,0:T(8,128)S(1)} %get-tuple-element.20.own, f32[2,64,1280]{2,1,0:T(8,128)S(1)} %collective-permute-done.1.halo, bf16[768,256]{1,0:T(8,128)(2,1)S(1)} %copy-done.2, ...), custom_call_target="tpu_custom_call" | custom-call | tf_op jit(solution)/shard_map/pallas_call | solution.py:350
  29.1 3.5 %collective-permute-start.2 = (f32[2,200,128]{2,1,0:T(8,128)S(1)}, f32[2,200,128]{2,1,0:T(8,128)S(1)}, u32[]{:S(2)}, u32[]{:S(2)}) collective-permute-start(f32[2,200,128]{2,1,0:T(8,128)S(1)} %get-tuple-element.23), channel_id=1, source_target_pairs={{0,128},{128,0},{256,384},{384,256},{1,129},{129,1},{257,385},{385... | collective-permute-start | bytes 614408 | tf_op jit(solution)/shard_map/ppermute | solution.py:353
  32.6 1.1 %collective-permute-done.2 = f32[2,200,128]{2,1,0:T(8,128)S(1)} collective-permute-done((f32[2,200,128]{2,1,0:T(8,128)S(1)}, f32[2,200,128]{2,1,0:T(8,128)S(1)}, u32[]{:S(2)}, u32[]{:S(2)}) %collective-permute-start.2) | collective-permute-done | bytes 204832 | tf_op jit(solution)/shard_map/ppermute | solution.py:353
  33.7 1.9 %collective-permute-start.3 = (f32[2,200,128]{2,1,0:T(8,128)S(1)}, f32[2,200,128]{2,1,0:T(8,128)S(1)}, u32[]{:S(2)}, u32[]{:S(2)}) collective-permute-start(f32[2,200,128]{2,1,0:T(8,128)S(1)} %add.17.refs_0_), channel_id=1, source_target_pairs={{1,0},{2,1},{3,2},{4,3},{5,4},{6,5},{7,6},{8,7},{9,8},{10,9},{11,1... | collective-permute-start | bytes 614408 | tf_op jit(solution)/shard_map/ppermute | solution.py:354
  35.6 0.0 collective-permute-done.halo
  35.6 0.0 copy-done.1
  35.6 0.0 copy-start.3
  35.6 0.0 copy-start.4
  35.7 0.0 copy-start.5
  35.7 0.0 copy-start.8
  35.7 3.9 %shard_map.112 = (f32[2,200,128]{2,1,0:T(8,128)S(1)}, f32[2,200,128]{2,1,0:T(8,128)S(1)}) custom-call(s32[6,8,128]{2,1,0:T(8,128)S(1)} %broadcast_in_dim.2.numbers, f32[3,256,640]{2,1,0:T(8,128)S(1)} %copy-done.1, f32[3,64,1280]{2,1,0:T(8,128)S(1)} %collective-permute-done.halo, bf16[768,256]{1,0:T(8,128)(2,1)S(1)} %copy-done.2, ...), custom_call_target="tpu_custom_call" | custom-call | tf_op jit(solution)/shard_map/pallas_call | solution.py:355
  39.6 2.3 %collective-permute-start.4 = (f32[2,200,128]{2,1,0:T(8,128)S(1)}, f32[2,200,128]{2,1,0:T(8,128)S(1)}, u32[]{:S(2)}, u32[]{:S(2)}) collective-permute-start(f32[2,200,128]{2,1,0:T(8,128)S(1)} %get-tuple-element.26), channel_id=1, source_target_pairs={{0,128},{128,0},{256,384},{384,256},{1,129},{129,1},{257,385},{385... | collective-permute-start | bytes 614408 | tf_op jit(solution)/shard_map/ppermute | solution.py:358
  41.9 0.0 collective-permute-done.3
  41.9 1.0 %collective-permute-done.4 = f32[2,200,128]{2,1,0:T(8,128)S(1)} collective-permute-done((f32[2,200,128]{2,1,0:T(8,128)S(1)}, f32[2,200,128]{2,1,0:T(8,128)S(1)}, u32[]{:S(2)}, u32[]{:S(2)}) %collective-permute-start.4) | collective-permute-done | bytes 204832 | tf_op jit(solution)/shard_map/ppermute | solution.py:358
  43.0 7.5 %collective-permute-start.5 = (f32[2,200,128]{2,1,0:T(8,128)S(1)}, f32[2,200,128]{2,1,0:T(8,128)S(1)}, u32[]{:S(2)}, u32[]{:S(2)}) collective-permute-start(f32[2,200,128]{2,1,0:T(8,128)S(1)} %add_add_fusion.here), channel_id=1, source_target_pairs={{0,256},{128,384},{256,0},{384,128},{1,257},{129,385},{257,1},{385... | collective-permute-start | bytes 614408 | tf_op jit(solution)/shard_map/ppermute | solution.py:359
  50.4 9.4 %collective-permute-done.5.there = f32[2,200,128]{2,1,0:T(8,128)S(1)} collective-permute-done((f32[2,200,128]{2,1,0:T(8,128)S(1)}, f32[2,200,128]{2,1,0:T(8,128)S(1)}, u32[]{:S(2)}, u32[]{:S(2)}) %collective-permute-start.5) | collective-permute-done | bytes 204832 | tf_op jit(solution)/shard_map/ppermute | solution.py:359
  59.8 0.0 copy-done.3
  59.8 0.0 copy-done.4
  59.8 0.0 copy-done.5
  59.8 0.0 copy-done.8
  59.8 3.2 %shard_map.113 = (f32[64,320]{1,0:T(8,128)S(1)}, f32[64,256]{1,0:T(8,128)S(1)}) custom-call(s32[6,8,128]{2,1,0:T(8,128)S(1)} %broadcast_in_dim.2.numbers, f32[2,200,128]{2,1,0:T(8,128)S(1)} %add_add_fusion.here, f32[2,200,128]{2,1,0:T(8,128)S(1)} %collective-permute-done.5.there, f32[4,256,256]{2,1,0:T(8,128)S(1)} %copy-done.3, ...), custom_call_target="tpu_custom_call" | custom-call | tf_op jit(solution)/shard_map/pallas_call | solution.py:362
  63.0 3.8 %collective-permute-start.6 = (f32[64,256]{1,0:T(8,128)S(1)}, f32[64,256]{1,0:T(8,128)S(1)}, u32[]{:S(2)}, u32[]{:S(2)}) collective-permute-start(f32[64,256]{1,0:T(8,128)S(1)} %get-tuple-element.28), channel_id=1, source_target_pairs={{0,1},{1,2},{2,3},{3,4},{4,5},{5,6},{6,7},{7,8},{8,9},{9,10},{10,1... | collective-permute-start | bytes 196616 | tf_op jit(solution)/shard_map/ppermute | solution.py:365
  66.8 7.2 %collective-permute-done.6.lower = f32[64,256]{1,0:T(8,128)S(1)} collective-permute-done((f32[64,256]{1,0:T(8,128)S(1)}, f32[64,256]{1,0:T(8,128)S(1)}, u32[]{:S(2)}, u32[]{:S(2)}) %collective-permute-start.6) | collective-permute-done | bytes 65568 | tf_op jit(solution)/shard_map/ppermute | solution.py:365
  74.1 0.1 shard_map.114
  74.1 4.1 %collective-permute-start.7 = (f32[64,320]{1,0:T(8,128)S(1)}, f32[64,320]{1,0:T(8,128)S(1)}, u32[]{:S(2)}, u32[]{:S(2)}) collective-permute-start(f32[64,320]{1,0:T(8,128)S(1)} %shard_map.114), channel_id=1, source_target_pairs={{0,128},{128,0},{256,384},{384,256},{1,129},{129,1},{257,385},{385... | collective-permute-start | bytes 245768 | tf_op jit(solution)/shard_map/ppermute | solution.py:367
  78.2 0.9 %collective-permute-done.7 = f32[64,320]{1,0:T(8,128)S(1)} collective-permute-done((f32[64,320]{1,0:T(8,128)S(1)}, f32[64,320]{1,0:T(8,128)S(1)}, u32[]{:S(2)}, u32[]{:S(2)}) %collective-permute-start.7) | collective-permute-done | bytes 81952 | tf_op jit(solution)/shard_map/ppermute | solution.py:367
  79.2 0.7 add.20
  (2 shorter events, 0.1 us)
Async XLA Ops:
  0.0 1.5 %copy-start = (f32[20,64,320]{2,1,0:T(8,128)S(1)}, f32[20,64,320]{2,1,0:T(8,128)}, u32[]{:S(2)}) copy-start(f32[20,64,320]{2,1,0:T(8,128)} %frames_ref.1) | copy-start | bytes 4915204
  1.5 12.3 %copy-start.9 = (s32[2,2]{1,0:T(2,128)S(1)}, s32[2,2]{1,0:T(2,128)}, u32[]{:S(2)}) copy-start(s32[2,2]{1,0:T(2,128)} %param.14) | copy-start | bytes 52
  1.5 15.7 %copy-start.2 = (bf16[768,256]{1,0:T(8,128)(2,1)S(1)}, bf16[768,256]{1,0:T(8,128)(2,1)}, u32[]{:S(2)}) copy-start(bf16[768,256]{1,0:T(8,128)(2,1)} %constant.38.clone.right_ref) | copy-start | bytes 1179652
  1.6 15.7 %copy-start.6 = (bf16[256,384]{1,0:T(8,128)(2,1)S(1)}, bf16[256,384]{1,0:T(8,128)(2,1)}, u32[]{:S(2)}) copy-start(bf16[256,384]{1,0:T(8,128)(2,1)} %constant.40.clone.lower_ref.left_ref) | copy-start | bytes 589828
  1.6 15.7 %copy-start.7 = (bf16[256,384]{1,0:T(8,128)(2,1)S(1)}, bf16[256,384]{1,0:T(8,128)(2,1)}, u32[]{:S(2)}) copy-start(bf16[256,384]{1,0:T(8,128)(2,1)} %constant.39.clone.upper_ref.left_ref) | copy-start | bytes 589828
  2.6 23.7 %collective-permute-start.1 = (f32[2,64,1280]{2,1,0:T(8,128)}, f32[2,64,1280]{2,1,0:T(8,128)S(1)}, u32[]{:S(2)}, u32[]{:S(2)}) collective-permute-start(f32[2,64,1280]{2,1,0:T(8,128)} %get-tuple-element.18.own_r), channel_id=1, source_target_pairs={{0,1},{1,2},{2,3},{3,4},{4,5},{5,6},{6,7},{7,8},{8,9},{9,10},{10,1... | collective-permute-start | bytes 1966088 | tf_op jit(solution)/shard_map/ppermute | solution.py:340
  5.7 29.9 %collective-permute-start = (f32[3,64,1280]{2,1,0:T(8,128)S(1)}, f32[3,64,1280]{2,1,0:T(8,128)S(1)}, u32[]{:S(2)}, u32[]{:S(2)}) collective-permute-start(f32[3,64,1280]{2,1,0:T(8,128)S(1)} %get-tuple-element.17.own_l), channel_id=1, source_target_pairs={{1,0},{2,1},{3,2},{4,3},{5,4},{6,5},{7,6},{8,7},{9,8},{10,9},{11,1... | collective-permute-start | bytes 2949128 | tf_op jit(solution)/shard_map/ppermute | solution.py:339
  21.1 14.5 %copy-start.1 = (f32[3,256,640]{2,1,0:T(8,128)S(1)}, f32[3,256,640]{2,1,0:T(8,128)}, u32[]{:S(2)}) copy-start(f32[3,256,640]{2,1,0:T(8,128)} %get-tuple-element.19.own) | copy-start | bytes 5898244
  29.1 4.5 %collective-permute-start.2 = (f32[2,200,128]{2,1,0:T(8,128)S(1)}, f32[2,200,128]{2,1,0:T(8,128)S(1)}, u32[]{:S(2)}, u32[]{:S(2)}) collective-permute-start(f32[2,200,128]{2,1,0:T(8,128)S(1)} %get-tuple-element.23), channel_id=1, source_target_pairs={{0,128},{128,0},{256,384},{384,256},{1,129},{129,1},{257,385},{385... | collective-permute-start | bytes 614408 | tf_op jit(solution)/shard_map/ppermute | solution.py:353
  33.7 8.2 %collective-permute-start.3 = (f32[2,200,128]{2,1,0:T(8,128)S(1)}, f32[2,200,128]{2,1,0:T(8,128)S(1)}, u32[]{:S(2)}, u32[]{:S(2)}) collective-permute-start(f32[2,200,128]{2,1,0:T(8,128)S(1)} %add.17.refs_0_), channel_id=1, source_target_pairs={{1,0},{2,1},{3,2},{4,3},{5,4},{6,5},{7,6},{8,7},{9,8},{10,9},{11,1... | collective-permute-start | bytes 614408 | tf_op jit(solution)/shard_map/ppermute | solution.py:354
  35.6 24.2 %copy-start.3 = (f32[4,256,256]{2,1,0:T(8,128)S(1)}, f32[4,256,256]{2,1,0:T(8,128)}, u32[]{:S(2)}) copy-start(f32[4,256,256]{2,1,0:T(8,128)} %constant.41.clone.exact) | copy-start | bytes 3145732
  35.6 24.2 %copy-start.4 = (bf16[768,256]{1,0:T(8,128)(2,1)S(1)}, bf16[768,256]{1,0:T(8,128)(2,1)}, u32[]{:S(2)}) copy-start(bf16[768,256]{1,0:T(8,128)(2,1)} %constant.42.clone.right_back) | copy-start | bytes 1179652
  35.7 24.2 %copy-start.5 = (bf16[256,768]{1,0:T(8,128)(2,1)S(1)}, bf16[256,768]{1,0:T(8,128)(2,1)}, u32[]{:S(2)}) copy-start(bf16[256,768]{1,0:T(8,128)(2,1)} %constant.43.clone.left_back) | copy-start | bytes 1179652
  35.7 24.2 %copy-start.8 = (f32[128,128]{1,0:T(8,128)S(1)}, f32[128,128]{1,0:T(8,128)}, u32[]{:S(2)}) copy-start(f32[128,128]{1,0:T(8,128)} %constant.44.clone.window) | copy-start | bytes 196612
  39.6 3.4 %collective-permute-start.4 = (f32[2,200,128]{2,1,0:T(8,128)S(1)}, f32[2,200,128]{2,1,0:T(8,128)S(1)}, u32[]{:S(2)}, u32[]{:S(2)}) collective-permute-start(f32[2,200,128]{2,1,0:T(8,128)S(1)} %get-tuple-element.26), channel_id=1, source_target_pairs={{0,128},{128,0},{256,384},{384,256},{1,129},{129,1},{257,385},{385... | collective-permute-start | bytes 614408 | tf_op jit(solution)/shard_map/ppermute | solution.py:358
  43.0 16.9 %collective-permute-start.5 = (f32[2,200,128]{2,1,0:T(8,128)S(1)}, f32[2,200,128]{2,1,0:T(8,128)S(1)}, u32[]{:S(2)}, u32[]{:S(2)}) collective-permute-start(f32[2,200,128]{2,1,0:T(8,128)S(1)} %add_add_fusion.here), channel_id=1, source_target_pairs={{0,256},{128,384},{256,0},{384,128},{1,257},{129,385},{257,1},{385... | collective-permute-start | bytes 614408 | tf_op jit(solution)/shard_map/ppermute | solution.py:359
  63.0 11.0 %collective-permute-start.6 = (f32[64,256]{1,0:T(8,128)S(1)}, f32[64,256]{1,0:T(8,128)S(1)}, u32[]{:S(2)}, u32[]{:S(2)}) collective-permute-start(f32[64,256]{1,0:T(8,128)S(1)} %get-tuple-element.28), channel_id=1, source_target_pairs={{0,1},{1,2},{2,3},{3,4},{4,5},{5,6},{6,7},{7,8},{8,9},{9,10},{10,1... | collective-permute-start | bytes 196616 | tf_op jit(solution)/shard_map/ppermute | solution.py:365
  74.1 5.0 %collective-permute-start.7 = (f32[64,320]{1,0:T(8,128)S(1)}, f32[64,320]{1,0:T(8,128)S(1)}, u32[]{:S(2)}, u32[]{:S(2)}) collective-permute-start(f32[64,320]{1,0:T(8,128)S(1)} %shard_map.114), channel_id=1, source_target_pairs={{0,128},{128,0},{256,384},{384,256},{1,129},{129,1},{257,385},{385... | collective-permute-start | bytes 245768 | tf_op jit(solution)/shard_map/ppermute | solution.py:367

commit v4 on v3

--- a/solution.py
+++ b/solution.py
@@ -19,7 +19,7 @@
 total_frames = 80
 float32 = jnp.float32
 bfloat16 = jnp.bfloat16
-vmem_limit = 48 * 1024 * 1024
+vmem_limit = 24 * 1024 * 1024
 
 
 def as_pieces(table):
@@ -235,7 +235,14 @@
     return first, second
 
 
-def solve_kernel(numbers, here, there, exact, right_back, left_back, inverse_eigen, window, upper_ref, lower_ref):
+def total_kernel(numbers, both, *refs):
+    total = jnp.where(number(numbers, 2) == 0, both[1], both[0])
+    for ref in refs[:-1]:
+        total = total + ref[...]
+    refs[-1][...] = total
+
+
+def solve_kernel(numbers, halves, exact, right_back, left_back, inverse_eigen, window, upper_ref, lower_ref):
     row_step, col_step = number(numbers, 0), number(numbers, 1)
     lower_core = number(numbers, 2) == 0
     live_first, live_last = number(numbers, 4), number(numbers, 4) + number(numbers, 5)
@@ -243,7 +250,7 @@
     blank = jnp.zeros((half, side), float32)
     powers, crosses_a, crosses_b = [], [], []
     for j in range(2):
-        both = here[j] + there[j]
+        both = halves[0, j] + halves[1, j]
         crowded = both[half:side]
         powers.append(jnp.concatenate([both[side:], blank[: 2 * side - folded_rows]], axis=0))
         crosses_a.append(jnp.concatenate([both[:half], blank], axis=0))
@@ -330,8 +337,7 @@
 
     to_left = [(i, i - 1) for i in range(1, tiles)]
     to_right = [(i, i + 1) for i in range(tiles - 1)]
-    other_core = [(g, g ^ 1) for g in range(4)]
-    other_half = [(g, g ^ 2) for g in range(4)]
+    cores, halves = [[0, 1], [2, 3]], [[0, 2], [1, 3]]
     count_r = 8
     count_l = frames.shape[0] - count_r
     packed = [shape_of((n // 4, half, quad_width)) for n in (count_l, count_r)]
@@ -350,21 +356,24 @@
     kept, sent = call(sum_kernel, [folded, folded], 6, scratch)(
         numbers, rows_r, halo_r, right_taper, upper_taper, inverse_eigen
     )
-    away = kept + lax.ppermute(sent, "frames", other_core)
+    both = lax.all_gather(sent, "frames", axis_index_groups=cores)
+    (away,) = call(total_kernel, [folded], 3)(numbers, both, kept)
     back = lax.ppermute(away, "tiles", to_left)
     kept, sent = call(sum_kernel, [folded, folded], 7, scratch)(
         numbers, rows_l, halo_l, right_taper, lower_taper, away, before
     )
-    here = kept + back + lax.ppermute(sent, "frames", other_core)
-    there = lax.ppermute(here, "frames", other_half)
+    both = lax.all_gather(sent, "frames", axis_index_groups=cores)
+    (here,) = call(total_kernel, [folded], 4)(numbers, both, kept, back)
+    both = lax.all_gather(here, "frames", axis_index_groups=halves)
 
     block = shape_of((half, width))
-    upper, lower = call(solve_kernel, [block, shape_of((half, 2 * side))], 8)(
-        numbers, here, there, exact, right_back, left_back, inverse_eigen, window
+    upper, lower = call(solve_kernel, [block, shape_of((half, 2 * side))], 7)(
+        numbers, both, exact, right_back, left_back, inverse_eigen, window
     )
     lower = lax.ppermute(lower, "tiles", to_right)
     (own,) = call(receive_kernel, [block], 3)(numbers, upper, lower)
-    return own + lax.ppermute(own, "frames", other_core)
+    own = lax.all_gather(own, "frames", axis_index_groups=cores)
+    return own[0] + own[1]
 
 
 def solution(mesh):

time: 80.2 us -> 76.5 us (0.954)
  blocking collectives: 0 us -> 25.9 us
  starting transfers between devices: 34.3 us -> 15.6 us
  waiting for transfers between devices: 24.8 us -> 15.1 us
  Pallas kernels: 14.9 us -> 13.9 us
    all_gather x0 -> x4, blocking collectives: none -> 25.9 us  [the longest x1 15.8 us: on_device(): both = lax.all_gather(here, 'frames', axis_index_groups=halves)]
    ppermute x4 -> x0, starting transfers between devices: 17.3 us -> none  [the longest x1 7.45 us: on_device(): there = lax.ppermute(here, 'frames', other_half)]
    ppermute x4 -> x0, waiting for transfers between devices: 12.4 us -> none  [the longest x1 9.41 us: on_device(): there = lax.ppermute(here, 'frames', other_half)]
    ppermute x1, waiting for transfers between devices: 7.24 us -> 8.61 us  [on_device(): lower = lax.ppermute(lower, 'tiles', to_right)]
    ppermute x1, starting transfers between devices: 3.78 us -> 2.41 us  [on_device(): lower = lax.ppermute(lower, 'tiles', to_right)]
    pallas_call x1, Pallas kernels: 3.89 us -> 2.6 us  [on_device(): call(start_kernel, tables, 6, [spectrum], 16 * 10 ** 9)]
    ppermute x1, waiting for transfers between devices: 5.16 us -> 6.44 us  [on_device(): halo_r = lax.ppermute(own_r, 'tiles', to_right)]
    pallas_call x1 -> x3, Pallas kernels: 3.2 us -> 3.33 us  [the longest x1 3.19 us: on_device(): call(solve_kernel, [block, shape_of((half, 2 * side))], 7)]
  transfers between devices with their start and end apart: 8 -> 4, of which waited for: 6 -> 2; matrix products, arithmetic and copies ran while one was open for 3% -> 3% of each run, Pallas kernels for 13% -> 13%
where the time goes in v4:
time: 76.5 us; the launch traced here: 76.2 us
  blocking collectives  25.9 us (34%)
  starting transfers between devices  15.6 us (20%)
  waiting for transfers between devices  15.1 us (20%)
  Pallas kernels  13.9 us (18%)
  local copies, waits for them, and re-layouts  3.61 us (5%)
  between operations  1.47 us (2%)
    all_gather x1, blocking collectives, on_device(): both = lax.all_gather(here, 'frames', axis_index_groups=halves)  15.8 us
    ppermute x1, waiting for transfers between devices, on_device(): lower = lax.ppermute(lower, 'tiles', to_right)  8.61 us
    ppermute x1, starting transfers between devices, on_device(): halo_l = lax.ppermute(own_l, 'tiles', to_left)  8.18 us
    all_gather x2, blocking collectives, on_device(): both = lax.all_gather(sent, 'frames', axis_index_groups=cores)  6.96 us
    ppermute x1, waiting for transfers between devices, on_device(): halo_r = lax.ppermute(own_r, 'tiles', to_right)  6.44 us
    pallas_call x1, Pallas kernels, on_device(): call(sum_kernel, [folded, folded], 7, scratch)  4.01 us
    all_gather x1, blocking collectives, on_device(): own = lax.all_gather(own, 'frames', axis_index_groups=cores)  3.2 us
    pallas_call x1, Pallas kernels, on_device(): call(solve_kernel, [block, shape_of((half, 2 * side))], 7)  3.19 us
  transfers between devices with their start and end apart: 4, of which 2 were waited for; matrix products, arithmetic and copies ran while one was open for 3% of the time, Pallas kernels for 13%

profile of v4, /device:TPU:257, one launch (start us, length us, event | category | flops | bytes accessed | tf_op | source)
XLA Modules:
  0.0 76.2 jit_solution(10534789280939250624)
XLA Ops:
  0.0 0.0 copy-start
  0.0 1.5 %copy-done = f32[20,64,320]{2,1,0:T(8,128)S(1)} copy-done((f32[20,64,320]{2,1,0:T(8,128)S(1)}, f32[20,64,320]{2,1,0:T(8,128)}, u32[]{:S(2)}) %copy-start) | copy-done | bytes 1638424
  1.5 0.0 copy-start.8
  1.5 0.0 copy-start.1
  1.6 0.0 copy-start.5
  1.6 0.0 copy-start.6
  1.6 1.0 %shard_map.109 = (f32[3,64,1280]{2,1,0:T(8,128)S(1)}, f32[2,64,1280]{2,1,0:T(8,128)}) custom-call(f32[20,64,320]{2,1,0:T(8,128)S(1)} %copy-done), custom_call_target="tpu_custom_call" | custom-call | tf_op jit(solution)/shard_map/pallas_call | solution.py:344
  2.6 3.1 %collective-permute-start.1 = (f32[2,64,1280]{2,1,0:T(8,128)}, f32[2,64,1280]{2,1,0:T(8,128)S(1)}, u32[]{:S(2)}, u32[]{:S(2)}) collective-permute-start(f32[2,64,1280]{2,1,0:T(8,128)} %get-tuple-element.18.own_r), channel_id=1, source_target_pairs={{0,1},{1,2},{2,3},{3,4},{4,5},{5,6},{6,7},{7,8},{8,9},{9,10},{10,1... | collective-permute-start | bytes 1966088 | tf_op jit(solution)/shard_map/ppermute | solution.py:346
  5.7 8.2 %collective-permute-start = (f32[3,64,1280]{2,1,0:T(8,128)S(1)}, f32[3,64,1280]{2,1,0:T(8,128)S(1)}, u32[]{:S(2)}, u32[]{:S(2)}) collective-permute-start(f32[3,64,1280]{2,1,0:T(8,128)S(1)} %get-tuple-element.17.own_l), channel_id=1, source_target_pairs={{1,0},{2,1},{3,2},{4,3},{5,4},{6,5},{7,6},{8,7},{9,8},{10,9},{11,1... | collective-permute-start | bytes 2949128 | tf_op jit(solution)/shard_map/ppermute | solution.py:345
  13.9 0.0 copy-done.8
  13.9 0.6 fusion
  15.8 1.4 %stack.15 = s32[6]{0:T(128)S(1)} concatenate(s32[1]{0:T(128)} %bitcast, s32[1]{0:T(128)} %bitcast.1, s32[1]{0:T(128)} %bitcast.2, s32[1]{0:T(128)} %bitcast.3, s32[1]{0:T(128)S(6)} %copy.12, s32[1]{0:T(128)S(6)} %copy.13), dimensions={0} | concatenate | bytes 48 | tf_op jit(solution)/shard_map/stack | solution.py:335
  17.2 0.1 broadcast_in_dim.2.numbers
  17.2 0.0 copy-done.1
  17.2 0.0 copy-done.5
  17.2 0.0 copy-done.6
  17.2 2.6 %shard_map.110 = (f32[4,3,128,128]{3,2,1,0:T(8,128)S(1)}, f32[128,128]{1,0:T(8,128)S(1)}, f32[3,256,640]{2,1,0:T(8,128)S(1)}, f32[2,256,640]{2,1,0:T(8,128)S(1)}) custom-call(s32[6,8,128]{2,1,0:T(8,128)S(1)} %broadcast_in_dim.2.numbers, f32[3,64,1280]{2,1,0:T(8,128)S(1)} %get-tuple-element.17.own_l, f32[2,64,1280]{2,1,0:T(8,128)} %get-tuple-element.18.own_r, ...), custom_call_target="tpu_custom_call" | custom-call | flops 16000000000 | tf_op jit(solution)/shard_map/pallas_call | solution.py:353
  19.8 6.4 %collective-permute-done.1.halo = f32[2,64,1280]{2,1,0:T(8,128)S(1)} collective-permute-done((f32[2,64,1280]{2,1,0:T(8,128)}, f32[2,64,1280]{2,1,0:T(8,128)S(1)}, u32[]{:S(2)}, u32[]{:S(2)}) %collective-permute-start.1) | collective-permute-done | bytes 655392 | tf_op jit(solution)/shard_map/ppermute | solution.py:346
  26.3 2.9 %shard_map.111 = (f32[2,200,128]{2,1,0:T(8,128)S(1)}, f32[2,200,128]{2,1,0:T(8,128)S(1)}) custom-call(s32[6,8,128]{2,1,0:T(8,128)S(1)} %broadcast_in_dim.2.numbers, f32[2,256,640]{2,1,0:T(8,128)S(1)} %get-tuple-element.20.own, f32[2,64,1280]{2,1,0:T(8,128)S(1)} %collective-permute-done.1.halo, bf16[768,256]{1,0:T(8,128)(2,1)S(1)} %copy-done.1, ...), custom_call_target="tpu_custom_call" | custom-call | tf_op jit(solution)/shard_map/pallas_call | solution.py:356
  29.2 3.3 %all-gather = f32[4,200,128]{2,1,0:T(8,128)S(1)} all-gather(f32[2,200,128]{2,1,0:T(8,128)S(1)} %get-tuple-element.22), channel_id=2, replica_groups={{0,128},{256,384},{1,129},{257,385},{2,130},{258,386},{3,131},{259,387}..., dimensions={0}, use_global_device_ids=true | all-gather | bytes 614400 | tf_op jit(solution)/shard_map/all_gather | solution.py:359
  32.4 0.1 shard_map.112.refs_0_
  32.5 1.9 %collective-permute-start.2 = (f32[2,200,128]{2,1,0:T(8,128)S(1)}, f32[2,200,128]{2,1,0:T(8,128)S(1)}, u32[]{:S(2)}, u32[]{:S(2)}) collective-permute-start(f32[2,200,128]{2,1,0:T(8,128)S(1)} %shard_map.112.refs_0_), channel_id=1, source_target_pairs={{1,0},{2,1},{3,2},{4,3},{5,4},{6,5},{7,6},{8,7},{9,8},{10,9},{11,1... | collective-permute-start | bytes 614408 | tf_op jit(solution)/shard_map/ppermute | solution.py:361
  34.4 0.0 collective-permute-done.halo
  34.4 4.0 %shard_map.113 = (f32[2,200,128]{2,1,0:T(8,128)S(1)}, f32[2,200,128]{2,1,0:T(8,128)S(1)}) custom-call(s32[6,8,128]{2,1,0:T(8,128)S(1)} %broadcast_in_dim.2.numbers, f32[3,256,640]{2,1,0:T(8,128)S(1)} %get-tuple-element.19.own, f32[3,64,1280]{2,1,0:T(8,128)S(1)} %collective-permute-done.halo, bf16[768,256]{1,0:T(8,128)(2,1)S(1)} %copy-done.1, ...), custom_call_target="tpu_custom_call" | custom-call | tf_op jit(solution)/shard_map/pallas_call | solution.py:362
  38.4 0.0 copy-start.2
  38.5 0.0 copy-start.3
  38.5 0.0 copy-start.4
  38.5 0.0 copy-start.7
  38.5 3.7 %all-gather.1 = f32[4,200,128]{2,1,0:T(8,128)S(1)} all-gather(f32[2,200,128]{2,1,0:T(8,128)S(1)} %get-tuple-element.25), channel_id=3, replica_groups={{0,128},{256,384},{1,129},{257,385},{2,130},{258,386},{3,131},{259,387}..., dimensions={0}, use_global_device_ids=true | all-gather | bytes 614400 | tf_op jit(solution)/shard_map/all_gather | solution.py:365
  42.2 0.0 collective-permute-done.2.refs_1_
  42.2 0.1 shard_map.114
  42.3 15.8 %all-gather.2 = f32[4,200,128]{2,1,0:T(8,128)S(1)} all-gather(f32[2,200,128]{2,1,0:T(8,128)S(1)} %shard_map.114), channel_id=4, replica_groups={{0,256},{128,384},{1,257},{129,385},{2,258},{130,386},{3,259},{131,387}..., dimensions={0}, use_global_device_ids=true | all-gather | bytes 614400 | tf_op jit(solution)/shard_map/all_gather | solution.py:367
  58.0 0.0 copy-done.2
  58.0 0.0 copy-done.3
  58.0 0.0 copy-done.4
  58.0 0.0 copy-done.7
  58.1 3.2 %shard_map.115 = (f32[64,320]{1,0:T(8,128)S(1)}, f32[64,256]{1,0:T(8,128)S(1)}) custom-call(s32[6,8,128]{2,1,0:T(8,128)S(1)} %broadcast_in_dim.2.numbers, f32[2,2,200,128]{3,2,1,0:T(8,128)S(1)} %bitcast.7, f32[4,256,256]{2,1,0:T(8,128)S(1)} %copy-done.2, bf16[768,256]{1,0:T(8,128)(2,1)S(1)} %copy-done.3, bf16[256,768]{1,0:T(8,128)(2,1)S(1)} %copy-done.4, ...), custom_call_target="tpu_custom_call" | custom-call | tf_op jit(solution)/shard_map/pallas_call | solution.py:370
  61.3 2.4 %collective-permute-start.3 = (f32[64,256]{1,0:T(8,128)S(1)}, f32[64,256]{1,0:T(8,128)S(1)}, u32[]{:S(2)}, u32[]{:S(2)}) collective-permute-start(f32[64,256]{1,0:T(8,128)S(1)} %get-tuple-element.28), channel_id=1, source_target_pairs={{0,1},{1,2},{2,3},{3,4},{4,5},{5,6},{6,7},{7,8},{8,9},{9,10},{10,1... | collective-permute-start | bytes 196616 | tf_op jit(solution)/shard_map/ppermute | solution.py:373
  63.7 8.6 %collective-permute-done.3.lower = f32[64,256]{1,0:T(8,128)S(1)} collective-permute-done((f32[64,256]{1,0:T(8,128)S(1)}, f32[64,256]{1,0:T(8,128)S(1)}, u32[]{:S(2)}, u32[]{:S(2)}) %collective-permute-start.3) | collective-permute-done | bytes 65568 | tf_op jit(solution)/shard_map/ppermute | solution.py:373
  72.3 0.1 shard_map.116
  72.3 3.2 %all-gather.3 = f32[128,320]{1,0:T(8,128)S(1)} all-gather(f32[64,320]{1,0:T(8,128)S(1)} %shard_map.116), channel_id=5, replica_groups={{0,128},{256,384},{1,129},{257,385},{2,130},{258,386},{3,131},{259,387}..., dimensions={0}, use_global_device_ids=true | all-gather | bytes 245760 | tf_op jit(solution)/shard_map/all_gather | solution.py:375
  75.5 0.7 slice_add_fusion
Async XLA Ops:
  0.0 1.5 %copy-start = (f32[20,64,320]{2,1,0:T(8,128)S(1)}, f32[20,64,320]{2,1,0:T(8,128)}, u32[]{:S(2)}) copy-start(f32[20,64,320]{2,1,0:T(8,128)} %frames_ref.1) | copy-start | bytes 4915204
  1.5 12.3 %copy-start.8 = (s32[2,2]{1,0:T(2,128)S(1)}, s32[2,2]{1,0:T(2,128)}, u32[]{:S(2)}) copy-start(s32[2,2]{1,0:T(2,128)} %param.14) | copy-start | bytes 52
  1.5 15.7 %copy-start.1 = (bf16[768,256]{1,0:T(8,128)(2,1)S(1)}, bf16[768,256]{1,0:T(8,128)(2,1)}, u32[]{:S(2)}) copy-start(bf16[768,256]{1,0:T(8,128)(2,1)} %constant.38.clone.right_ref) | copy-start | bytes 1179652
  1.6 15.7 %copy-start.5 = (bf16[256,384]{1,0:T(8,128)(2,1)S(1)}, bf16[256,384]{1,0:T(8,128)(2,1)}, u32[]{:S(2)}) copy-start(bf16[256,384]{1,0:T(8,128)(2,1)} %constant.40.clone.lower_ref.left_ref) | copy-start | bytes 589828
  1.6 15.7 %copy-start.6 = (bf16[256,384]{1,0:T(8,128)(2,1)S(1)}, bf16[256,384]{1,0:T(8,128)(2,1)}, u32[]{:S(2)}) copy-start(bf16[256,384]{1,0:T(8,128)(2,1)} %constant.39.clone.upper_ref.left_ref) | copy-start | bytes 589828
  2.6 23.7 %collective-permute-start.1 = (f32[2,64,1280]{2,1,0:T(8,128)}, f32[2,64,1280]{2,1,0:T(8,128)S(1)}, u32[]{:S(2)}, u32[]{:S(2)}) collective-permute-start(f32[2,64,1280]{2,1,0:T(8,128)} %get-tuple-element.18.own_r), channel_id=1, source_target_pairs={{0,1},{1,2},{2,3},{3,4},{4,5},{5,6},{6,7},{7,8},{8,9},{9,10},{10,1... | collective-permute-start | bytes 1966088 | tf_op jit(solution)/shard_map/ppermute | solution.py:346
  5.7 28.7 %collective-permute-start = (f32[3,64,1280]{2,1,0:T(8,128)S(1)}, f32[3,64,1280]{2,1,0:T(8,128)S(1)}, u32[]{:S(2)}, u32[]{:S(2)}) collective-permute-start(f32[3,64,1280]{2,1,0:T(8,128)S(1)} %get-tuple-element.17.own_l), channel_id=1, source_target_pairs={{1,0},{2,1},{3,2},{4,3},{5,4},{6,5},{7,6},{8,7},{9,8},{10,9},{11,1... | collective-permute-start | bytes 2949128 | tf_op jit(solution)/shard_map/ppermute | solution.py:345
  32.5 9.7 %collective-permute-start.2 = (f32[2,200,128]{2,1,0:T(8,128)S(1)}, f32[2,200,128]{2,1,0:T(8,128)S(1)}, u32[]{:S(2)}, u32[]{:S(2)}) collective-permute-start(f32[2,200,128]{2,1,0:T(8,128)S(1)} %shard_map.112.refs_0_), channel_id=1, source_target_pairs={{1,0},{2,1},{3,2},{4,3},{5,4},{6,5},{7,6},{8,7},{9,8},{10,9},{11,1... | collective-permute-start | bytes 614408 | tf_op jit(solution)/shard_map/ppermute | solution.py:361
  38.4 19.6 %copy-start.2 = (f32[4,256,256]{2,1,0:T(8,128)S(1)}, f32[4,256,256]{2,1,0:T(8,128)}, u32[]{:S(2)}) copy-start(f32[4,256,256]{2,1,0:T(8,128)} %constant.41.clone.exact) | copy-start | bytes 3145732
  38.5 19.6 %copy-start.3 = (bf16[768,256]{1,0:T(8,128)(2,1)S(1)}, bf16[768,256]{1,0:T(8,128)(2,1)}, u32[]{:S(2)}) copy-start(bf16[768,256]{1,0:T(8,128)(2,1)} %constant.42.clone.right_back) | copy-start | bytes 1179652
  38.5 19.6 %copy-start.4 = (bf16[256,768]{1,0:T(8,128)(2,1)S(1)}, bf16[256,768]{1,0:T(8,128)(2,1)}, u32[]{:S(2)}) copy-start(bf16[256,768]{1,0:T(8,128)(2,1)} %constant.43.clone.left_back) | copy-start | bytes 1179652
  38.5 19.6 %copy-start.7 = (f32[128,128]{1,0:T(8,128)S(1)}, f32[128,128]{1,0:T(8,128)}, u32[]{:S(2)}) copy-start(f32[128,128]{1,0:T(8,128)} %constant.44.clone.window) | copy-start | bytes 196612
  61.3 11.0 %collective-permute-start.3 = (f32[64,256]{1,0:T(8,128)S(1)}, f32[64,256]{1,0:T(8,128)S(1)}, u32[]{:S(2)}, u32[]{:S(2)}) collective-permute-start(f32[64,256]{1,0:T(8,128)S(1)} %get-tuple-element.28), channel_id=1, source_target_pairs={{0,1},{1,2},{2,3},{3,4},{4,5},{5,6},{6,7},{7,8},{8,9},{9,10},{10,1... | collective-permute-start | bytes 196616 | tf_op jit(solution)/shard_map/ppermute | solution.py:373

commit v5 on v4

--- a/solution.py
+++ b/solution.py
@@ -211,7 +211,7 @@
 def sum_kernel(numbers, own, halo, right_ref, left_ref, *refs):
     kept, sent, acc, spectrum = refs[-4:]
     row_step, col_step = number(numbers, 0), number(numbers, 1)
-    acc[...] = refs[1][...] if len(refs) == 6 else jnp.zeros_like(acc)
+    acc[...] = refs[1][...] if len(refs) == 7 else jnp.zeros_like(acc)
     for i in range(halo.shape[0]):
         g = own[i] + rows_of(halo[i], left_ref[...])
         add_quad(g, row_step, col_step, right_ref[...], spectrum.at[i % 2], acc)
@@ -244,7 +244,6 @@
 
 def solve_kernel(numbers, halves, exact, right_back, left_back, inverse_eigen, window, upper_ref, lower_ref):
     row_step, col_step = number(numbers, 0), number(numbers, 1)
-    lower_core = number(numbers, 2) == 0
     live_first, live_last = number(numbers, 4), number(numbers, 4) + number(numbers, 5)
     lanes = lax.broadcasted_iota(jnp.int32, (side, side), 1)
     blank = jnp.zeros((half, side), float32)
@@ -292,20 +291,21 @@
     second = pltpu.roll(rebuilt[side:] * (window[...] * live[1]), half, 1)
     left_part = first + jnp.where(lanes >= half, second, 0.0)
     right_part = jnp.where(lanes < half, second, 0.0)
-    for at, part in ((0, left_part), (side, right_part)):
-        lower_ref[:, at : at + side] = part[half:]
-    place(lower_core, left_part[:half], right_part[:half], upper_ref)
-
-
-def place(lower_core, left, right, out_ref):
-    out_ref[:, 0:128] = jnp.where(lower_core, left, 0.0)
-    out_ref[:, 128:256] = jnp.where(lower_core, right, left)
-    out_ref[:, 256:320] = jnp.where(lower_core, 0.0, right)[:, :half]
-
-
-def receive_kernel(numbers, upper, lower, out_ref):
-    place(number(numbers, 2) == 0, lower[:, :side], lower[:, side:], out_ref)
-    out_ref[...] += upper[...]
+    for out_ref, at in ((upper_ref, 0), (lower_ref, half)):
+        rest = right_part[at : at + half, :half]
+        out_ref[:half] = left_part[at : at + half]
+        out_ref[half:] = jnp.concatenate([rest[: half // 2], rest[half // 2 :]], axis=1)
+
+
+def join_kernel(cores_ref, out_ref):
+    lanes = lax.broadcasted_iota(jnp.int32, (half, side), 1)
+    rests = []
+    for core in range(2):
+        rest = cores_ref[core, half:]
+        rests.append(jnp.concatenate([rest, pltpu.roll(rest, half, 1)], axis=0))
+    out_ref[:, 0:128] = cores_ref[0, :half]
+    out_ref[:, 128:256] = cores_ref[1, :half] + jnp.where(lanes < half, rests[0], 0.0)
+    out_ref[:, 256:320] = rests[1][:, :half]
 
 
 vmem = pl.BlockSpec(memory_space=pltpu.VMEM)
@@ -354,26 +354,26 @@
         numbers, own_l, own_r, right_taper, upper_taper, lower_taper
     )
     kept, sent = call(sum_kernel, [folded, folded], 6, scratch)(
-        numbers, rows_r, halo_r, right_taper, upper_taper, inverse_eigen
+        numbers, rows_r, halo_r, right_taper, upper_taper, own_r
     )
     both = lax.all_gather(sent, "frames", axis_index_groups=cores)
     (away,) = call(total_kernel, [folded], 3)(numbers, both, kept)
     back = lax.ppermute(away, "tiles", to_left)
-    kept, sent = call(sum_kernel, [folded, folded], 7, scratch)(
-        numbers, rows_l, halo_l, right_taper, lower_taper, away, before
+    kept, sent = call(sum_kernel, [folded, folded], 8, scratch)(
+        numbers, rows_l, halo_l, right_taper, lower_taper, away, before, own_l
     )
     both = lax.all_gather(sent, "frames", axis_index_groups=cores)
     (here,) = call(total_kernel, [folded], 4)(numbers, both, kept, back)
     both = lax.all_gather(here, "frames", axis_index_groups=halves)
 
-    block = shape_of((half, width))
-    upper, lower = call(solve_kernel, [block, shape_of((half, 2 * side))], 7)(
+    block = shape_of((half + half // 2, side))
+    upper, lower = call(solve_kernel, [block, block], 7)(
         numbers, both, exact, right_back, left_back, inverse_eigen, window
     )
-    lower = lax.ppermute(lower, "tiles", to_right)
-    (own,) = call(receive_kernel, [block], 3)(numbers, upper, lower)
-    own = lax.all_gather(own, "frames", axis_index_groups=cores)
-    return own[0] + own[1]
+    own = upper + lax.ppermute(lower, "tiles", to_right)
+    both = lax.all_gather(own, "frames", axis_index_groups=cores)
+    (image,) = call(join_kernel, [shape_of((half, width))], 1)(both)
+    return image
 
 
 def solution(mesh):

time: 76.5 us -> 75.7 us (0.990)
  starting transfers between devices: 15.6 us -> 17.7 us
  waiting for transfers between devices: 15.1 us -> 14 us
  blocking collectives: 25.9 us -> 24.9 us
    ppermute x1, waiting for transfers between devices: 8.61 us -> 6.51 us  [on_device(): own = upper + lax.ppermute(lower, 'tiles', to_right)]
    ppermute x1, starting transfers between devices: 2.41 us -> 4.34 us  [on_device(): own = upper + lax.ppermute(lower, 'tiles', to_right)]
    all_gather x2, blocking collectives: 6.96 us -> 5.54 us  [on_device(): both = lax.all_gather(sent, 'frames', axis_index_groups=cores)]
    pallas_call x1, Pallas kernels: 2.6 us -> 1.47 us  [on_device(): call(start_kernel, tables, 6, [spectrum], 16 * 10 ** 9)]
    all_gather x1, blocking collectives: 3.2 us -> 4.29 us  [on_device(): both = lax.all_gather(own, 'frames', axis_index_groups=cores)]
    pallas_call x1, Pallas kernels: 2.87 us -> 3.95 us  [on_device(): call(sum_kernel, [folded, folded], 6, scratch)]
    ppermute x1, waiting for transfers between devices: 6.44 us -> 7.45 us  [on_device(): halo_r = lax.ppermute(own_r, 'tiles', to_right)]
    pallas_call x1, Pallas kernels: 1.02 us -> 0.17 us  [on_device(): own_l, own_r = call(pack_kernel, packed, 1)(frames)]
where the time goes in v5:
time: 75.7 us; the launch traced here: 75.3 us
  blocking collectives  24.9 us (33%)
  starting transfers between devices  17.7 us (23%)
  waiting for transfers between devices  14 us (18%)
  Pallas kernels  13.7 us (18%)
  local copies, waits for them, and re-layouts  3.61 us (5%)
  between operations  1.47 us (2%)
    all_gather x1, blocking collectives, on_device(): both = lax.all_gather(here, 'frames', axis_index_groups=halves)  15.1 us
    ppermute x1, starting transfers between devices, on_device(): halo_l = lax.ppermute(own_l, 'tiles', to_left)  8.18 us
    ppermute x1, waiting for transfers between devices, on_device(): halo_r = lax.ppermute(own_r, 'tiles', to_right)  7.45 us
    ppermute x1, waiting for transfers between devices, on_device(): own = upper + lax.ppermute(lower, 'tiles', to_right)  6.51 us
    all_gather x2, blocking collectives, on_device(): both = lax.all_gather(sent, 'frames', axis_index_groups=cores)  5.54 us
    ppermute x1, starting transfers between devices, on_device(): own = upper + lax.ppermute(lower, 'tiles', to_right)  4.34 us
    all_gather x1, blocking collectives, on_device(): both = lax.all_gather(own, 'frames', axis_index_groups=cores)  4.29 us
    pallas_call x1, Pallas kernels, on_device(): call(sum_kernel, [folded, folded], 8, scratch)  3.99 us
  transfers between devices with their start and end apart: 4, of which 2 were waited for; matrix products, arithmetic and copies ran while one was open for 3% of the time, Pallas kernels for 13%

profile of v5, /device:TPU:257, one launch (start us, length us, event | category | flops | bytes accessed | tf_op | source)
XLA Modules:
  0.0 75.3 jit_solution(7081389992089446759)
XLA Ops:
  0.0 0.0 copy-start
  0.0 1.5 %copy-done = f32[20,64,320]{2,1,0:T(8,128)S(1)} copy-done((f32[20,64,320]{2,1,0:T(8,128)S(1)}, f32[20,64,320]{2,1,0:T(8,128)}, u32[]{:S(2)}) %copy-start) | copy-done | bytes 1638424
  1.5 0.0 copy-start.8
  1.5 0.0 copy-start.1
  1.6 0.0 copy-start.5
  1.6 0.0 copy-start.6
  1.6 0.2 shard_map.109
  1.7 3.3 %collective-permute-start.1 = (f32[2,64,1280]{2,1,0:T(8,128)S(1)}, f32[2,64,1280]{2,1,0:T(8,128)}, u32[]{:S(2)}, u32[]{:S(2)}) collective-permute-start(f32[2,64,1280]{2,1,0:T(8,128)S(1)} %get-tuple-element.18.own_r.refs_0_), channel_id=1, source_target_pairs={{0,1},{1,2},{2,3},{3,4},{4,5},{5,6},{6,7},{7,8},{8,9},{9,10},{10,1... | collective-permute-start | bytes 1966088 | tf_op jit(solution)/shard_map/ppermute | solution.py:346
  5.0 8.2 %collective-permute-start = (f32[3,64,1280]{2,1,0:T(8,128)S(1)}, f32[3,64,1280]{2,1,0:T(8,128)S(1)}, u32[]{:S(2)}, u32[]{:S(2)}) collective-permute-start(f32[3,64,1280]{2,1,0:T(8,128)S(1)} %get-tuple-element.17.own_l.refs_2_), channel_id=1, source_target_pairs={{1,0},{2,1},{3,2},{4,3},{5,4},{6,5},{7,6},{8,7},{9,8},{10,9},{11,1... | collective-permute-start | bytes 2949128 | tf_op jit(solution)/shard_map/ppermute | solution.py:345
  13.2 0.0 copy-done.8
  13.2 0.6 fusion
  15.1 1.4 %stack.15 = s32[6]{0:T(128)S(1)} concatenate(s32[1]{0:T(128)} %bitcast, s32[1]{0:T(128)} %bitcast.1, s32[1]{0:T(128)} %bitcast.2, s32[1]{0:T(128)} %bitcast.3, s32[1]{0:T(128)S(6)} %copy.12, s32[1]{0:T(128)S(6)} %copy.13), dimensions={0} | concatenate | bytes 48 | tf_op jit(solution)/shard_map/stack | solution.py:335
  16.5 0.1 broadcast_in_dim.2.numbers
  16.5 0.0 copy-done.1
  16.5 0.0 copy-done.5
  16.5 0.0 copy-done.6
  16.6 1.5 %shard_map.110 = (f32[4,3,128,128]{3,2,1,0:T(8,128)S(1)}, f32[128,128]{1,0:T(8,128)S(1)}, f32[3,256,640]{2,1,0:T(8,128)S(1)}, f32[2,256,640]{2,1,0:T(8,128)S(1)}) custom-call(s32[6,8,128]{2,1,0:T(8,128)S(1)} %broadcast_in_dim.2.numbers, f32[3,64,1280]{2,1,0:T(8,128)S(1)} %get-tuple-element.17.own_l.refs_2_, ...), custom_call_target="tpu_custom_call" | custom-call | flops 16000000000 | tf_op jit(solution)/shard_map/pallas_call | solution.py:353
  18.0 7.5 %collective-permute-done.1.halo = f32[2,64,1280]{2,1,0:T(8,128)} collective-permute-done((f32[2,64,1280]{2,1,0:T(8,128)S(1)}, f32[2,64,1280]{2,1,0:T(8,128)}, u32[]{:S(2)}, u32[]{:S(2)}) %collective-permute-start.1) | collective-permute-done | bytes 655392 | tf_op jit(solution)/shard_map/ppermute | solution.py:346
  25.5 3.9 %shard_map.111 = (f32[2,200,128]{2,1,0:T(8,128)S(1)}, f32[2,200,128]{2,1,0:T(8,128)S(1)}) custom-call(s32[6,8,128]{2,1,0:T(8,128)S(1)} %broadcast_in_dim.2.numbers, f32[2,256,640]{2,1,0:T(8,128)S(1)} %get-tuple-element.20.own, f32[2,64,1280]{2,1,0:T(8,128)} %collective-permute-done.1.halo, bf16[768,256]{1,0:T(8,128)(2,1)S(1)} %copy-done.1, ...), custom_call_target="tpu_custom_call" | custom-call | tf_op jit(solution)/shard_map/pallas_call | solution.py:356
  29.4 3.3 %all-gather = f32[4,200,128]{2,1,0:T(8,128)S(1)} all-gather(f32[2,200,128]{2,1,0:T(8,128)S(1)} %get-tuple-element.21), channel_id=2, replica_groups={{0,128},{256,384},{1,129},{257,385},{2,130},{258,386},{3,131},{259,387}..., dimensions={0}, use_global_device_ids=true | all-gather | bytes 614400 | tf_op jit(solution)/shard_map/all_gather | solution.py:359
  32.7 0.1 shard_map.112.refs_0_
  32.8 1.9 %collective-permute-start.2 = (f32[2,200,128]{2,1,0:T(8,128)S(1)}, f32[2,200,128]{2,1,0:T(8,128)S(1)}, u32[]{:S(2)}, u32[]{:S(2)}) collective-permute-start(f32[2,200,128]{2,1,0:T(8,128)S(1)} %shard_map.112.refs_0_), channel_id=1, source_target_pairs={{1,0},{2,1},{3,2},{4,3},{5,4},{6,5},{7,6},{8,7},{9,8},{10,9},{11,1... | collective-permute-start | bytes 614408 | tf_op jit(solution)/shard_map/ppermute | solution.py:361
  34.7 0.0 collective-permute-done.halo
  34.7 4.0 %shard_map.113 = (f32[2,200,128]{2,1,0:T(8,128)S(1)}, f32[2,200,128]{2,1,0:T(8,128)S(1)}) custom-call(s32[6,8,128]{2,1,0:T(8,128)S(1)} %broadcast_in_dim.2.numbers, f32[3,256,640]{2,1,0:T(8,128)S(1)} %get-tuple-element.19.own, f32[3,64,1280]{2,1,0:T(8,128)S(1)} %collective-permute-done.halo, bf16[768,256]{1,0:T(8,128)(2,1)S(1)} %copy-done.1, ...), custom_call_target="tpu_custom_call" | custom-call | tf_op jit(solution)/shard_map/pallas_call | solution.py:362
  38.7 0.0 copy-start.2
  38.7 0.0 copy-start.3
  38.7 0.0 copy-start.4
  38.8 0.0 copy-start.7
  38.8 2.3 %all-gather.1 = f32[4,200,128]{2,1,0:T(8,128)S(1)} all-gather(f32[2,200,128]{2,1,0:T(8,128)S(1)} %get-tuple-element.24), channel_id=3, replica_groups={{0,128},{256,384},{1,129},{257,385},{2,130},{258,386},{3,131},{259,387}..., dimensions={0}, use_global_device_ids=true | all-gather | bytes 614400 | tf_op jit(solution)/shard_map/all_gather | solution.py:365
  41.0 0.0 collective-permute-done.2.refs_1_
  41.0 0.1 shard_map.114
  41.1 15.1 %all-gather.2 = f32[4,200,128]{2,1,0:T(8,128)S(1)} all-gather(f32[2,200,128]{2,1,0:T(8,128)S(1)} %shard_map.114), channel_id=4, replica_groups={{0,256},{128,384},{1,257},{129,385},{2,258},{130,386},{3,259},{131,387}..., dimensions={0}, use_global_device_ids=true | all-gather | bytes 614400 | tf_op jit(solution)/shard_map/all_gather | solution.py:367
  56.2 0.0 copy-done.2
  56.2 0.0 copy-done.3
  56.2 0.0 copy-done.4
  56.2 0.0 copy-done.7
  56.2 3.3 %shard_map.115 = (f32[96,128]{1,0:T(8,128)S(1)}, f32[96,128]{1,0:T(8,128)S(1)}) custom-call(s32[6,8,128]{2,1,0:T(8,128)S(1)} %broadcast_in_dim.2.numbers, f32[2,2,200,128]{3,2,1,0:T(8,128)S(1)} %bitcast.8, f32[4,256,256]{2,1,0:T(8,128)S(1)} %copy-done.2, bf16[768,256]{1,0:T(8,128)(2,1)S(1)} %copy-done.3, bf16[256,768]{1,0:T(8,128)(2,1)S(1)} %copy-done.4, ...), custom_call_target="tpu_custom_call" | custom-call | tf_op jit(solution)/shard_map/pallas_call | solution.py:370
  59.5 4.3 %collective-permute-start.3 = (f32[96,128]{1,0:T(8,128)S(1)}, f32[96,128]{1,0:T(8,128)S(1)}, u32[]{:S(2)}, u32[]{:S(2)}) collective-permute-start(f32[96,128]{1,0:T(8,128)S(1)} %get-tuple-element.28), channel_id=1, source_target_pairs={{0,1},{1,2},{2,3},{3,4},{4,5},{5,6},{6,7},{7,8},{8,9},{9,10},{10,1... | collective-permute-start | bytes 147464 | tf_op jit(solution)/shard_map/ppermute | solution.py:373
  63.8 6.5 %collective-permute-done.3 = f32[96,128]{1,0:T(8,128)S(1)} collective-permute-done((f32[96,128]{1,0:T(8,128)S(1)}, f32[96,128]{1,0:T(8,128)S(1)}, u32[]{:S(2)}, u32[]{:S(2)}) %collective-permute-start.3) | collective-permute-done | bytes 49184 | tf_op jit(solution)/shard_map/ppermute | solution.py:373
  70.3 4.3 %all-gather.3 = f32[192,128]{1,0:T(8,128)S(1)} all-gather(f32[96,128]{1,0:T(8,128)S(1)} %add.8), channel_id=5, replica_groups={{0,128},{256,384},{1,129},{257,385},{2,130},{258,386},{3,131},{259,387}..., dimensions={0}, use_global_device_ids=true | all-gather | bytes 147456 | tf_op jit(solution)/shard_map/all_gather | solution.py:374
  74.6 0.7 shard_map.116
  (1 shorter events, 0.0 us)
Async XLA Ops:
  0.0 1.5 %copy-start = (f32[20,64,320]{2,1,0:T(8,128)S(1)}, f32[20,64,320]{2,1,0:T(8,128)}, u32[]{:S(2)}) copy-start(f32[20,64,320]{2,1,0:T(8,128)} %frames_ref.1) | copy-start | bytes 4915204
  1.5 11.7 %copy-start.8 = (s32[2,2]{1,0:T(2,128)S(1)}, s32[2,2]{1,0:T(2,128)}, u32[]{:S(2)}) copy-start(s32[2,2]{1,0:T(2,128)} %param.14) | copy-start | bytes 52
  1.5 15.0 %copy-start.1 = (bf16[768,256]{1,0:T(8,128)(2,1)S(1)}, bf16[768,256]{1,0:T(8,128)(2,1)}, u32[]{:S(2)}) copy-start(bf16[768,256]{1,0:T(8,128)(2,1)} %constant.38.clone.right_ref) | copy-start | bytes 1179652
  1.6 15.0 %copy-start.5 = (bf16[256,384]{1,0:T(8,128)(2,1)S(1)}, bf16[256,384]{1,0:T(8,128)(2,1)}, u32[]{:S(2)}) copy-start(bf16[256,384]{1,0:T(8,128)(2,1)} %constant.40.clone.lower_ref.left_ref) | copy-start | bytes 589828
  1.6 15.0 %copy-start.6 = (bf16[256,384]{1,0:T(8,128)(2,1)S(1)}, bf16[256,384]{1,0:T(8,128)(2,1)}, u32[]{:S(2)}) copy-start(bf16[256,384]{1,0:T(8,128)(2,1)} %constant.39.clone.upper_ref.left_ref) | copy-start | bytes 589828
  1.7 23.7 %collective-permute-start.1 = (f32[2,64,1280]{2,1,0:T(8,128)S(1)}, f32[2,64,1280]{2,1,0:T(8,128)}, u32[]{:S(2)}, u32[]{:S(2)}) collective-permute-start(f32[2,64,1280]{2,1,0:T(8,128)S(1)} %get-tuple-element.18.own_r.refs_0_), channel_id=1, source_target_pairs={{0,1},{1,2},{2,3},{3,4},{4,5},{5,6},{6,7},{7,8},{8,9},{9,10},{10,1... | collective-permute-start | bytes 1966088 | tf_op jit(solution)/shard_map/ppermute | solution.py:346
  5.0 29.7 %collective-permute-start = (f32[3,64,1280]{2,1,0:T(8,128)S(1)}, f32[3,64,1280]{2,1,0:T(8,128)S(1)}, u32[]{:S(2)}, u32[]{:S(2)}) collective-permute-start(f32[3,64,1280]{2,1,0:T(8,128)S(1)} %get-tuple-element.17.own_l.refs_2_), channel_id=1, source_target_pairs={{1,0},{2,1},{3,2},{4,3},{5,4},{6,5},{7,6},{8,7},{9,8},{10,9},{11,1... | collective-permute-start | bytes 2949128 | tf_op jit(solution)/shard_map/ppermute | solution.py:345
  32.8 8.3 %collective-permute-start.2 = (f32[2,200,128]{2,1,0:T(8,128)S(1)}, f32[2,200,128]{2,1,0:T(8,128)S(1)}, u32[]{:S(2)}, u32[]{:S(2)}) collective-permute-start(f32[2,200,128]{2,1,0:T(8,128)S(1)} %shard_map.112.refs_0_), channel_id=1, source_target_pairs={{1,0},{2,1},{3,2},{4,3},{5,4},{6,5},{7,6},{8,7},{9,8},{10,9},{11,1... | collective-permute-start | bytes 614408 | tf_op jit(solution)/shard_map/ppermute | solution.py:361
  38.7 17.5 %copy-start.2 = (f32[4,256,256]{2,1,0:T(8,128)S(1)}, f32[4,256,256]{2,1,0:T(8,128)}, u32[]{:S(2)}) copy-start(f32[4,256,256]{2,1,0:T(8,128)} %constant.41.clone.exact) | copy-start | bytes 3145732
  38.7 17.5 %copy-start.3 = (bf16[768,256]{1,0:T(8,128)(2,1)S(1)}, bf16[768,256]{1,0:T(8,128)(2,1)}, u32[]{:S(2)}) copy-start(bf16[768,256]{1,0:T(8,128)(2,1)} %constant.42.clone.right_back) | copy-start | bytes 1179652
  38.7 17.4 %copy-start.4 = (bf16[256,768]{1,0:T(8,128)(2,1)S(1)}, bf16[256,768]{1,0:T(8,128)(2,1)}, u32[]{:S(2)}) copy-start(bf16[256,768]{1,0:T(8,128)(2,1)} %constant.43.clone.left_back) | copy-start | bytes 1179652
  38.8 17.4 %copy-start.7 = (f32[128,128]{1,0:T(8,128)S(1)}, f32[128,128]{1,0:T(8,128)}, u32[]{:S(2)}) copy-start(f32[128,128]{1,0:T(8,128)} %constant.44.clone.window) | copy-start | bytes 196612
  59.5 10.8 %collective-permute-start.3 = (f32[96,128]{1,0:T(8,128)S(1)}, f32[96,128]{1,0:T(8,128)S(1)}, u32[]{:S(2)}, u32[]{:S(2)}) collective-permute-start(f32[96,128]{1,0:T(8,128)S(1)} %get-tuple-element.28), channel_id=1, source_target_pairs={{0,1},{1,2},{2,3},{3,4},{4,5},{5,6},{6,7},{7,8},{8,9},{9,10},{10,1... | collective-permute-start | bytes 147464 | tf_op jit(solution)/shard_map/ppermute | solution.py:373

commit v6 on v5

--- a/solution.py
+++ b/solution.py
@@ -297,14 +297,16 @@
         out_ref[half:] = jnp.concatenate([rest[: half // 2], rest[half // 2 :]], axis=1)
 
 
-def join_kernel(cores_ref, out_ref):
+def join_kernel(uppers, lowers, out_ref):
     lanes = lax.broadcasted_iota(jnp.int32, (half, side), 1)
-    rests = []
+    firsts, rests = [], []
     for core in range(2):
-        rest = cores_ref[core, half:]
+        block = uppers[core] + lowers[core]
+        rest = block[half:]
+        firsts.append(block[:half])
         rests.append(jnp.concatenate([rest, pltpu.roll(rest, half, 1)], axis=0))
-    out_ref[:, 0:128] = cores_ref[0, :half]
-    out_ref[:, 128:256] = cores_ref[1, :half] + jnp.where(lanes < half, rests[0], 0.0)
+    out_ref[:, 0:128] = firsts[0]
+    out_ref[:, 128:256] = firsts[1] + jnp.where(lanes < half, rests[0], 0.0)
     out_ref[:, 256:320] = rests[1][:, :half]
 
 
@@ -370,9 +372,10 @@
     upper, lower = call(solve_kernel, [block, block], 7)(
         numbers, both, exact, right_back, left_back, inverse_eigen, window
     )
-    own = upper + lax.ppermute(lower, "tiles", to_right)
-    both = lax.all_gather(own, "frames", axis_index_groups=cores)
-    (image,) = call(join_kernel, [shape_of((half, width))], 1)(both)
+    lower = lax.ppermute(lower, "tiles", to_right)
+    uppers = lax.all_gather(upper, "frames", axis_index_groups=cores)
+    lowers = lax.all_gather(lower, "frames", axis_index_groups=cores)
+    (image,) = call(join_kernel, [shape_of((half, width))], 2)(uppers, lowers)
     return image
 
 

time: 75.7 us -> 75.7 us (level)
  waiting for transfers between devices: 14 us -> 11.7 us
  blocking collectives: 24.9 us -> 27.1 us
    ppermute x1, waiting for transfers between devices: 6.51 us -> 4.23 us  [on_device(): lower = lax.ppermute(lower, 'tiles', to_right)]
    all_gather x1 -> x2, blocking collectives: 4.29 us -> 6.55 us  [the longest x1 4.28 us: on_device(): lowers = lax.all_gather(lower, 'frames', axis_index_groups=cores)]
where the time goes in v6:
time: 75.7 us; the launch traced here: 75.3 us
  blocking collectives  27.1 us (36%)
  starting transfers between devices  17.7 us (23%)
  Pallas kernels  13.7 us (18%)
  waiting for transfers between devices  11.7 us (15%)
  local copies, waits for them, and re-layouts  3.61 us (5%)
  between operations  1.47 us (2%)
    all_gather x1, blocking collectives, on_device(): both = lax.all_gather(here, 'frames', axis_index_groups=halves)  15.1 us
    ppermute x1, starting transfers between devices, on_device(): halo_l = lax.ppermute(own_l, 'tiles', to_left)  8.18 us
    ppermute x1, waiting for transfers between devices, on_device(): halo_r = lax.ppermute(own_r, 'tiles', to_right)  7.45 us
    all_gather x2, blocking collectives, on_device(): both = lax.all_gather(sent, 'frames', axis_index_groups=cores)  5.52 us
    ppermute x1, starting transfers between devices, on_device(): lower = lax.ppermute(lower, 'tiles', to_right)  4.34 us
    all_gather x1, blocking collectives, on_device(): lowers = lax.all_gather(lower, 'frames', axis_index_groups=cores)  4.28 us
    ppermute x1, waiting for transfers between devices, on_device(): lower = lax.ppermute(lower, 'tiles', to_right)  4.23 us
    pallas_call x1, Pallas kernels, on_device(): call(sum_kernel, [folded, folded], 8, scratch)  4.01 us
  transfers between devices with their start and end apart: 4, of which 2 were waited for; matrix products, arithmetic and copies ran while one was open for 3% of the time, Pallas kernels for 13%

profile of v6, /device:TPU:257, one launch (start us, length us, event | category | flops | bytes accessed | tf_op | source)
XLA Modules:
  0.0 75.3 jit_solution(4096141030963048684)
XLA Ops:
  0.0 0.0 copy-start
  0.0 1.5 %copy-done = f32[20,64,320]{2,1,0:T(8,128)S(1)} copy-done((f32[20,64,320]{2,1,0:T(8,128)S(1)}, f32[20,64,320]{2,1,0:T(8,128)}, u32[]{:S(2)}) %copy-start) | copy-done | bytes 1638424
  1.5 0.0 copy-start.8
  1.5 0.0 copy-start.1
  1.6 0.0 copy-start.5
  1.6 0.0 copy-start.6
  1.6 0.2 shard_map.109
  1.7 3.3 %collective-permute-start.1 = (f32[2,64,1280]{2,1,0:T(8,128)S(1)}, f32[2,64,1280]{2,1,0:T(8,128)}, u32[]{:S(2)}, u32[]{:S(2)}) collective-permute-start(f32[2,64,1280]{2,1,0:T(8,128)S(1)} %get-tuple-element.18.own_r.refs_0_), channel_id=1, source_target_pairs={{0,1},{1,2},{2,3},{3,4},{4,5},{5,6},{6,7},{7,8},{8,9},{9,10},{10,1... | collective-permute-start | bytes 1966088 | tf_op jit(solution)/shard_map/ppermute | solution.py:348
  5.0 8.2 %collective-permute-start = (f32[3,64,1280]{2,1,0:T(8,128)S(1)}, f32[3,64,1280]{2,1,0:T(8,128)S(1)}, u32[]{:S(2)}, u32[]{:S(2)}) collective-permute-start(f32[3,64,1280]{2,1,0:T(8,128)S(1)} %get-tuple-element.17.own_l.refs_2_), channel_id=1, source_target_pairs={{1,0},{2,1},{3,2},{4,3},{5,4},{6,5},{7,6},{8,7},{9,8},{10,9},{11,1... | collective-permute-start | bytes 2949128 | tf_op jit(solution)/shard_map/ppermute | solution.py:347
  13.2 0.0 copy-done.8
  13.2 0.6 fusion
  15.1 1.4 %stack.15 = s32[6]{0:T(128)S(1)} concatenate(s32[1]{0:T(128)} %bitcast, s32[1]{0:T(128)} %bitcast.1, s32[1]{0:T(128)} %bitcast.2, s32[1]{0:T(128)} %bitcast.3, s32[1]{0:T(128)S(6)} %copy.12, s32[1]{0:T(128)S(6)} %copy.13), dimensions={0} | concatenate | bytes 48 | tf_op jit(solution)/shard_map/stack | solution.py:337
  16.5 0.1 broadcast_in_dim.2.numbers
  16.5 0.0 copy-done.1
  16.5 0.0 copy-done.5
  16.5 0.0 copy-done.6
  16.6 1.5 %shard_map.110 = (f32[4,3,128,128]{3,2,1,0:T(8,128)S(1)}, f32[128,128]{1,0:T(8,128)S(1)}, f32[3,256,640]{2,1,0:T(8,128)S(1)}, f32[2,256,640]{2,1,0:T(8,128)S(1)}) custom-call(s32[6,8,128]{2,1,0:T(8,128)S(1)} %broadcast_in_dim.2.numbers, f32[3,64,1280]{2,1,0:T(8,128)S(1)} %get-tuple-element.17.own_l.refs_2_, ...), custom_call_target="tpu_custom_call" | custom-call | flops 16000000000 | tf_op jit(solution)/shard_map/pallas_call | solution.py:355
  18.0 7.5 %collective-permute-done.1.halo = f32[2,64,1280]{2,1,0:T(8,128)} collective-permute-done((f32[2,64,1280]{2,1,0:T(8,128)S(1)}, f32[2,64,1280]{2,1,0:T(8,128)}, u32[]{:S(2)}, u32[]{:S(2)}) %collective-permute-start.1) | collective-permute-done | bytes 655392 | tf_op jit(solution)/shard_map/ppermute | solution.py:348
  25.5 4.0 %shard_map.111 = (f32[2,200,128]{2,1,0:T(8,128)S(1)}, f32[2,200,128]{2,1,0:T(8,128)S(1)}) custom-call(s32[6,8,128]{2,1,0:T(8,128)S(1)} %broadcast_in_dim.2.numbers, f32[2,256,640]{2,1,0:T(8,128)S(1)} %get-tuple-element.20.own, f32[2,64,1280]{2,1,0:T(8,128)} %collective-permute-done.1.halo, bf16[768,256]{1,0:T(8,128)(2,1)S(1)} %copy-done.1, ...), custom_call_target="tpu_custom_call" | custom-call | tf_op jit(solution)/shard_map/pallas_call | solution.py:358
  29.5 3.3 %all-gather = f32[4,200,128]{2,1,0:T(8,128)S(1)} all-gather(f32[2,200,128]{2,1,0:T(8,128)S(1)} %get-tuple-element.21), channel_id=2, replica_groups={{0,128},{256,384},{1,129},{257,385},{2,130},{258,386},{3,131},{259,387}..., dimensions={0}, use_global_device_ids=true | all-gather | bytes 614400 | tf_op jit(solution)/shard_map/all_gather | solution.py:361
  32.7 0.1 shard_map.112.refs_0_
  32.8 1.9 %collective-permute-start.2 = (f32[2,200,128]{2,1,0:T(8,128)S(1)}, f32[2,200,128]{2,1,0:T(8,128)S(1)}, u32[]{:S(2)}, u32[]{:S(2)}) collective-permute-start(f32[2,200,128]{2,1,0:T(8,128)S(1)} %shard_map.112.refs_0_), channel_id=1, source_target_pairs={{1,0},{2,1},{3,2},{4,3},{5,4},{6,5},{7,6},{8,7},{9,8},{10,9},{11,1... | collective-permute-start | bytes 614408 | tf_op jit(solution)/shard_map/ppermute | solution.py:363
  34.7 0.0 collective-permute-done.halo
  34.7 4.0 %shard_map.113 = (f32[2,200,128]{2,1,0:T(8,128)S(1)}, f32[2,200,128]{2,1,0:T(8,128)S(1)}) custom-call(s32[6,8,128]{2,1,0:T(8,128)S(1)} %broadcast_in_dim.2.numbers, f32[3,256,640]{2,1,0:T(8,128)S(1)} %get-tuple-element.19.own, f32[3,64,1280]{2,1,0:T(8,128)S(1)} %collective-permute-done.halo, bf16[768,256]{1,0:T(8,128)(2,1)S(1)} %copy-done.1, ...), custom_call_target="tpu_custom_call" | custom-call | tf_op jit(solution)/shard_map/pallas_call | solution.py:364
  38.8 0.0 copy-start.2
  38.8 0.0 copy-start.3
  38.8 0.0 copy-start.4
  38.8 0.0 copy-start.7
  38.8 2.2 %all-gather.1 = f32[4,200,128]{2,1,0:T(8,128)S(1)} all-gather(f32[2,200,128]{2,1,0:T(8,128)S(1)} %get-tuple-element.24), channel_id=3, replica_groups={{0,128},{256,384},{1,129},{257,385},{2,130},{258,386},{3,131},{259,387}..., dimensions={0}, use_global_device_ids=true | all-gather | bytes 614400 | tf_op jit(solution)/shard_map/all_gather | solution.py:367
  41.1 0.0 collective-permute-done.2.refs_1_
  41.1 0.1 shard_map.114
  41.1 15.1 %all-gather.2 = f32[4,200,128]{2,1,0:T(8,128)S(1)} all-gather(f32[2,200,128]{2,1,0:T(8,128)S(1)} %shard_map.114), channel_id=4, replica_groups={{0,256},{128,384},{1,257},{129,385},{2,258},{130,386},{3,259},{131,387}..., dimensions={0}, use_global_device_ids=true | all-gather | bytes 614400 | tf_op jit(solution)/shard_map/all_gather | solution.py:369
  56.2 0.0 copy-done.2
  56.2 0.0 copy-done.3
  56.2 0.0 copy-done.4
  56.2 0.0 copy-done.7
  56.2 3.3 %shard_map.115 = (f32[96,128]{1,0:T(8,128)S(1)}, f32[96,128]{1,0:T(8,128)S(1)}) custom-call(s32[6,8,128]{2,1,0:T(8,128)S(1)} %broadcast_in_dim.2.numbers, f32[2,2,200,128]{3,2,1,0:T(8,128)S(1)} %bitcast.9, f32[4,256,256]{2,1,0:T(8,128)S(1)} %copy-done.2, bf16[768,256]{1,0:T(8,128)(2,1)S(1)} %copy-done.3, bf16[256,768]{1,0:T(8,128)(2,1)S(1)} %copy-done.4, ...), custom_call_target="tpu_custom_call" | custom-call | tf_op jit(solution)/shard_map/pallas_call | solution.py:372
  59.5 4.3 %collective-permute-start.3 = (f32[96,128]{1,0:T(8,128)S(1)}, f32[96,128]{1,0:T(8,128)S(1)}, u32[]{:S(2)}, u32[]{:S(2)}) collective-permute-start(f32[96,128]{1,0:T(8,128)S(1)} %get-tuple-element.28), channel_id=1, source_target_pairs={{0,1},{1,2},{2,3},{3,4},{4,5},{5,6},{6,7},{7,8},{8,9},{9,10},{10,1... | collective-permute-start | bytes 147464 | tf_op jit(solution)/shard_map/ppermute | solution.py:375
  63.8 2.3 %all-gather.3 = f32[192,128]{1,0:T(8,128)S(1)} all-gather(f32[96,128]{1,0:T(8,128)S(1)} %get-tuple-element.27), channel_id=5, replica_groups={{0,128},{256,384},{1,129},{257,385},{2,130},{258,386},{3,131},{259,387}..., dimensions={0}, use_global_device_ids=true | all-gather | bytes 147456 | tf_op jit(solution)/shard_map/all_gather | solution.py:376
  66.1 4.2 %collective-permute-done.3 = f32[96,128]{1,0:T(8,128)S(1)} collective-permute-done((f32[96,128]{1,0:T(8,128)S(1)}, f32[96,128]{1,0:T(8,128)S(1)}, u32[]{:S(2)}, u32[]{:S(2)}) %collective-permute-start.3) | collective-permute-done | bytes 49184 | tf_op jit(solution)/shard_map/ppermute | solution.py:375
  70.3 4.3 %all-gather.4 = f32[192,128]{1,0:T(8,128)S(1)} all-gather(f32[96,128]{1,0:T(8,128)S(1)} %collective-permute-done.3), channel_id=6, replica_groups={{0,128},{256,384},{1,129},{257,385},{2,130},{258,386},{3,131},{259,387}..., dimensions={0}, use_global_device_ids=true | all-gather | bytes 147456 | tf_op jit(solution)/shard_map/all_gather | solution.py:377
  74.6 0.7 shard_map.116
Async XLA Ops:
  0.0 1.5 %copy-start = (f32[20,64,320]{2,1,0:T(8,128)S(1)}, f32[20,64,320]{2,1,0:T(8,128)}, u32[]{:S(2)}) copy-start(f32[20,64,320]{2,1,0:T(8,128)} %frames_ref.1) | copy-start | bytes 4915204
  1.5 11.7 %copy-start.8 = (s32[2,2]{1,0:T(2,128)S(1)}, s32[2,2]{1,0:T(2,128)}, u32[]{:S(2)}) copy-start(s32[2,2]{1,0:T(2,128)} %param.14) | copy-start | bytes 52
  1.5 15.0 %copy-start.1 = (bf16[768,256]{1,0:T(8,128)(2,1)S(1)}, bf16[768,256]{1,0:T(8,128)(2,1)}, u32[]{:S(2)}) copy-start(bf16[768,256]{1,0:T(8,128)(2,1)} %constant.38.clone.right_ref) | copy-start | bytes 1179652
  1.6 15.0 %copy-start.5 = (bf16[256,384]{1,0:T(8,128)(2,1)S(1)}, bf16[256,384]{1,0:T(8,128)(2,1)}, u32[]{:S(2)}) copy-start(bf16[256,384]{1,0:T(8,128)(2,1)} %constant.40.clone.lower_ref.left_ref) | copy-start | bytes 589828
  1.6 15.0 %copy-start.6 = (bf16[256,384]{1,0:T(8,128)(2,1)S(1)}, bf16[256,384]{1,0:T(8,128)(2,1)}, u32[]{:S(2)}) copy-start(bf16[256,384]{1,0:T(8,128)(2,1)} %constant.39.clone.upper_ref.left_ref) | copy-start | bytes 589828
  1.7 23.7 %collective-permute-start.1 = (f32[2,64,1280]{2,1,0:T(8,128)S(1)}, f32[2,64,1280]{2,1,0:T(8,128)}, u32[]{:S(2)}, u32[]{:S(2)}) collective-permute-start(f32[2,64,1280]{2,1,0:T(8,128)S(1)} %get-tuple-element.18.own_r.refs_0_), channel_id=1, source_target_pairs={{0,1},{1,2},{2,3},{3,4},{4,5},{5,6},{6,7},{7,8},{8,9},{9,10},{10,1... | collective-permute-start | bytes 1966088 | tf_op jit(solution)/shard_map/ppermute | solution.py:348
  5.0 29.7 %collective-permute-start = (f32[3,64,1280]{2,1,0:T(8,128)S(1)}, f32[3,64,1280]{2,1,0:T(8,128)S(1)}, u32[]{:S(2)}, u32[]{:S(2)}) collective-permute-start(f32[3,64,1280]{2,1,0:T(8,128)S(1)} %get-tuple-element.17.own_l.refs_2_), channel_id=1, source_target_pairs={{1,0},{2,1},{3,2},{4,3},{5,4},{6,5},{7,6},{8,7},{9,8},{10,9},{11,1... | collective-permute-start | bytes 2949128 | tf_op jit(solution)/shard_map/ppermute | solution.py:347
  32.8 8.3 %collective-permute-start.2 = (f32[2,200,128]{2,1,0:T(8,128)S(1)}, f32[2,200,128]{2,1,0:T(8,128)S(1)}, u32[]{:S(2)}, u32[]{:S(2)}) collective-permute-start(f32[2,200,128]{2,1,0:T(8,128)S(1)} %shard_map.112.refs_0_), channel_id=1, source_target_pairs={{1,0},{2,1},{3,2},{4,3},{5,4},{6,5},{7,6},{8,7},{9,8},{10,9},{11,1... | collective-permute-start | bytes 614408 | tf_op jit(solution)/shard_map/ppermute | solution.py:363
  38.8 17.5 %copy-start.2 = (f32[4,256,256]{2,1,0:T(8,128)S(1)}, f32[4,256,256]{2,1,0:T(8,128)}, u32[]{:S(2)}) copy-start(f32[4,256,256]{2,1,0:T(8,128)} %constant.41.clone.exact) | copy-start | bytes 3145732
  38.8 17.4 %copy-start.3 = (bf16[768,256]{1,0:T(8,128)(2,1)S(1)}, bf16[768,256]{1,0:T(8,128)(2,1)}, u32[]{:S(2)}) copy-start(bf16[768,256]{1,0:T(8,128)(2,1)} %constant.42.clone.right_back) | copy-start | bytes 1179652
  38.8 17.4 %copy-start.4 = (bf16[256,768]{1,0:T(8,128)(2,1)S(1)}, bf16[256,768]{1,0:T(8,128)(2,1)}, u32[]{:S(2)}) copy-start(bf16[256,768]{1,0:T(8,128)(2,1)} %constant.43.clone.left_back) | copy-start | bytes 1179652
  38.8 17.4 %copy-start.7 = (f32[128,128]{1,0:T(8,128)S(1)}, f32[128,128]{1,0:T(8,128)}, u32[]{:S(2)}) copy-start(f32[128,128]{1,0:T(8,128)} %constant.44.clone.window) | copy-start | bytes 196612
  59.5 10.8 %collective-permute-start.3 = (f32[96,128]{1,0:T(8,128)S(1)}, f32[96,128]{1,0:T(8,128)S(1)}, u32[]{:S(2)}, u32[]{:S(2)}) collective-permute-start(f32[96,128]{1,0:T(8,128)S(1)} %get-tuple-element.28), channel_id=1, source_target_pairs={{0,1},{1,2},{2,3},{3,4},{4,5},{5,6},{6,7},{7,8},{8,9},{9,10},{10,1... | collective-permute-start | bytes 147464 | tf_op jit(solution)/shard_map/ppermute | solution.py:375

commit v7 on v5

--- a/solution.py
+++ b/solution.py
@@ -338,6 +338,9 @@
     to_left = [(i, i - 1) for i in range(1, tiles)]
     to_right = [(i, i + 1) for i in range(tiles - 1)]
     cores, halves = [[0, 1], [2, 3]], [[0, 2], [1, 3]]
+    layer = 16
+    places = [(g, i, g ^ 2 if i % layer == layer - 1 else g, i + 1) for g in range(4) for i in range(tiles - 1)]
+    sums_left = [(h * tiles + j, g * tiles + i) for g, i, h, j in places]
     count_r = 8
     count_l = frames.shape[0] - count_r
     packed = [shape_of((n // 4, half, quad_width)) for n in (count_l, count_r)]
@@ -358,7 +361,7 @@
     )
     both = lax.all_gather(sent, "frames", axis_index_groups=cores)
     (away,) = call(total_kernel, [folded], 3)(numbers, both, kept)
-    back = lax.ppermute(away, "tiles", to_left)
+    back = lax.ppermute(away, ("frames", "tiles"), sums_left)
     kept, sent = call(sum_kernel, [folded, folded], 8, scratch)(
         numbers, rows_l, halo_l, right_taper, lower_taper, away, before, own_l
     )

time: 75.7 us -> 76.6 us (1.012)
  waiting for transfers between devices: 14 us -> 16.1 us
  blocking collectives: 24.9 us -> 24.1 us
    ppermute x1, starting transfers between devices: 4.34 us -> 2.23 us  [on_device(): own = upper + lax.ppermute(lower, 'tiles', to_right)]
    ppermute x1, waiting for transfers between devices: 6.51 us -> 8.61 us  [on_device(): own = upper + lax.ppermute(lower, 'tiles', to_right)]
    ppermute x1, starting transfers between devices: 1.92 us -> 3.63 us  [on_device(): back = lax.ppermute(away, ('frames', 'tiles'), sums_left)]
    all_gather x1, blocking collectives: 4.29 us -> 3.15 us  [on_device(): both = lax.all_gather(own, 'frames', axis_index_groups=cores)]
  transfers between devices with their start and end apart: 4 -> 4, of which waited for: 2 -> 2; matrix products, arithmetic and copies ran while one was open for 3% -> 3% of each run, Pallas kernels for 13% -> 12%
where the time goes in v7:
time: 76.6 us; the launch traced here: 76.3 us
  blocking collectives  24.1 us (31%)
  starting transfers between devices  17.3 us (23%)
  waiting for transfers between devices  16.1 us (21%)
  Pallas kernels  13.7 us (18%)
  local copies, waits for them, and re-layouts  3.61 us (5%)
  between operations  1.47 us (2%)
    all_gather x1, blocking collectives, on_device(): both = lax.all_gather(here, 'frames', axis_index_groups=halves)  15.2 us
    ppermute x1, waiting for transfers between devices, on_device(): own = upper + lax.ppermute(lower, 'tiles', to_right)  8.61 us
    ppermute x1, starting transfers between devices, on_device(): halo_l = lax.ppermute(own_l, 'tiles', to_left)  8.18 us
    ppermute x1, waiting for transfers between devices, on_device(): halo_r = lax.ppermute(own_r, 'tiles', to_right)  7.45 us
    all_gather x2, blocking collectives, on_device(): both = lax.all_gather(sent, 'frames', axis_index_groups=cores)  5.79 us
    pallas_call x1, Pallas kernels, on_device(): call(sum_kernel, [folded, folded], 8, scratch)  3.99 us
    pallas_call x1, Pallas kernels, on_device(): call(sum_kernel, [folded, folded], 6, scratch)  3.95 us
    ppermute x1, starting transfers between devices, on_device(): back = lax.ppermute(away, ('frames', 'tiles'), sums_left)  3.63 us
  transfers between devices with their start and end apart: 4, of which 2 were waited for; matrix products, arithmetic and copies ran while one was open for 3% of the time, Pallas kernels for 12%

profile of v7, /device:TPU:257, one launch (start us, length us, event | category | flops | bytes accessed | tf_op | source)
XLA Modules:
  0.0 76.3 jit_solution(13444080556820930407)
XLA Ops:
  0.0 0.0 copy-start
  0.0 1.5 %copy-done = f32[20,64,320]{2,1,0:T(8,128)S(1)} copy-done((f32[20,64,320]{2,1,0:T(8,128)S(1)}, f32[20,64,320]{2,1,0:T(8,128)}, u32[]{:S(2)}) %copy-start) | copy-done | bytes 1638424
  1.5 0.0 copy-start.8
  1.5 0.0 copy-start.1
  1.6 0.0 copy-start.5
  1.6 0.0 copy-start.6
  1.6 0.2 shard_map.109
  1.7 3.3 %collective-permute-start.1 = (f32[2,64,1280]{2,1,0:T(8,128)S(1)}, f32[2,64,1280]{2,1,0:T(8,128)}, u32[]{:S(2)}, u32[]{:S(2)}) collective-permute-start(f32[2,64,1280]{2,1,0:T(8,128)S(1)} %get-tuple-element.18.own_r.refs_0_), channel_id=1, source_target_pairs={{0,1},{1,2},{2,3},{3,4},{4,5},{5,6},{6,7},{7,8},{8,9},{9,10},{10,1... | collective-permute-start | bytes 1966088 | tf_op jit(solution)/shard_map/ppermute | solution.py:349
  5.0 8.2 %collective-permute-start = (f32[3,64,1280]{2,1,0:T(8,128)S(1)}, f32[3,64,1280]{2,1,0:T(8,128)S(1)}, u32[]{:S(2)}, u32[]{:S(2)}) collective-permute-start(f32[3,64,1280]{2,1,0:T(8,128)S(1)} %get-tuple-element.17.own_l.refs_2_), channel_id=1, source_target_pairs={{1,0},{2,1},{3,2},{4,3},{5,4},{6,5},{7,6},{8,7},{9,8},{10,9},{11,1... | collective-permute-start | bytes 2949128 | tf_op jit(solution)/shard_map/ppermute | solution.py:348
  13.2 0.0 copy-done.8
  13.2 0.6 fusion
  15.1 1.4 %stack.15 = s32[6]{0:T(128)S(1)} concatenate(s32[1]{0:T(128)} %bitcast, s32[1]{0:T(128)} %bitcast.1, s32[1]{0:T(128)} %bitcast.2, s32[1]{0:T(128)} %bitcast.3, s32[1]{0:T(128)S(6)} %copy.12, s32[1]{0:T(128)S(6)} %copy.13), dimensions={0} | concatenate | bytes 48 | tf_op jit(solution)/shard_map/stack | solution.py:335
  16.5 0.1 broadcast_in_dim.2.numbers
  16.5 0.0 copy-done.1
  16.5 0.0 copy-done.5
  16.5 0.0 copy-done.6
  16.6 1.5 %shard_map.110 = (f32[4,3,128,128]{3,2,1,0:T(8,128)S(1)}, f32[128,128]{1,0:T(8,128)S(1)}, f32[3,256,640]{2,1,0:T(8,128)S(1)}, f32[2,256,640]{2,1,0:T(8,128)S(1)}) custom-call(s32[6,8,128]{2,1,0:T(8,128)S(1)} %broadcast_in_dim.2.numbers, f32[3,64,1280]{2,1,0:T(8,128)S(1)} %get-tuple-element.17.own_l.refs_2_, ...), custom_call_target="tpu_custom_call" | custom-call | flops 16000000000 | tf_op jit(solution)/shard_map/pallas_call | solution.py:356
  18.0 7.5 %collective-permute-done.1.halo = f32[2,64,1280]{2,1,0:T(8,128)} collective-permute-done((f32[2,64,1280]{2,1,0:T(8,128)S(1)}, f32[2,64,1280]{2,1,0:T(8,128)}, u32[]{:S(2)}, u32[]{:S(2)}) %collective-permute-start.1) | collective-permute-done | bytes 655392 | tf_op jit(solution)/shard_map/ppermute | solution.py:349
  25.5 3.9 %shard_map.111 = (f32[2,200,128]{2,1,0:T(8,128)S(1)}, f32[2,200,128]{2,1,0:T(8,128)S(1)}) custom-call(s32[6,8,128]{2,1,0:T(8,128)S(1)} %broadcast_in_dim.2.numbers, f32[2,256,640]{2,1,0:T(8,128)S(1)} %get-tuple-element.20.own, f32[2,64,1280]{2,1,0:T(8,128)} %collective-permute-done.1.halo, bf16[768,256]{1,0:T(8,128)(2,1)S(1)} %copy-done.1, ...), custom_call_target="tpu_custom_call" | custom-call | tf_op jit(solution)/shard_map/pallas_call | solution.py:359
  29.4 3.3 %all-gather = f32[4,200,128]{2,1,0:T(8,128)S(1)} all-gather(f32[2,200,128]{2,1,0:T(8,128)S(1)} %get-tuple-element.21), channel_id=2, replica_groups={{0,128},{256,384},{1,129},{257,385},{2,130},{258,386},{3,131},{259,387}..., dimensions={0}, use_global_device_ids=true | all-gather | bytes 614400 | tf_op jit(solution)/shard_map/all_gather | solution.py:362
  32.7 0.1 shard_map.112.refs_0_
  32.8 3.6 %collective-permute-start.2 = (f32[2,200,128]{2,1,0:T(8,128)S(1)}, f32[2,200,128]{2,1,0:T(8,128)S(1)}, u32[]{:S(2)}, u32[]{:S(2)}) collective-permute-start(f32[2,200,128]{2,1,0:T(8,128)S(1)} %shard_map.112.refs_0_), channel_id=1, source_target_pairs={{1,0},{2,1},{3,2},{4,3},{5,4},{6,5},{7,6},{8,7},{9,8},{10,9},{11,1... | collective-permute-start | bytes 614408 | tf_op jit(solution)/shard_map/ppermute | solution.py:364
  36.4 0.0 collective-permute-done.halo
  36.4 4.0 %shard_map.113 = (f32[2,200,128]{2,1,0:T(8,128)S(1)}, f32[2,200,128]{2,1,0:T(8,128)S(1)}) custom-call(s32[6,8,128]{2,1,0:T(8,128)S(1)} %broadcast_in_dim.2.numbers, f32[3,256,640]{2,1,0:T(8,128)S(1)} %get-tuple-element.19.own, f32[3,64,1280]{2,1,0:T(8,128)S(1)} %collective-permute-done.halo, bf16[768,256]{1,0:T(8,128)(2,1)S(1)} %copy-done.1, ...), custom_call_target="tpu_custom_call" | custom-call | tf_op jit(solution)/shard_map/pallas_call | solution.py:365
  40.4 0.0 copy-start.2
  40.4 0.0 copy-start.3
  40.5 0.0 copy-start.4
  40.5 0.0 copy-start.7
  40.5 2.5 %all-gather.1 = f32[4,200,128]{2,1,0:T(8,128)S(1)} all-gather(f32[2,200,128]{2,1,0:T(8,128)S(1)} %get-tuple-element.24), channel_id=3, replica_groups={{0,128},{256,384},{1,129},{257,385},{2,130},{258,386},{3,131},{259,387}..., dimensions={0}, use_global_device_ids=true | all-gather | bytes 614400 | tf_op jit(solution)/shard_map/all_gather | solution.py:368
  43.0 0.0 collective-permute-done.2.refs_1_
  43.0 0.1 shard_map.114
  43.1 15.2 %all-gather.2 = f32[4,200,128]{2,1,0:T(8,128)S(1)} all-gather(f32[2,200,128]{2,1,0:T(8,128)S(1)} %shard_map.114), channel_id=4, replica_groups={{0,256},{128,384},{1,257},{129,385},{2,258},{130,386},{3,259},{131,387}..., dimensions={0}, use_global_device_ids=true | all-gather | bytes 614400 | tf_op jit(solution)/shard_map/all_gather | solution.py:370
  58.3 0.0 copy-done.2
  58.3 0.0 copy-done.3
  58.3 0.0 copy-done.4
  58.3 0.0 copy-done.7
  58.3 3.3 %shard_map.115 = (f32[96,128]{1,0:T(8,128)S(1)}, f32[96,128]{1,0:T(8,128)S(1)}) custom-call(s32[6,8,128]{2,1,0:T(8,128)S(1)} %broadcast_in_dim.2.numbers, f32[2,2,200,128]{3,2,1,0:T(8,128)S(1)} %bitcast.8, f32[4,256,256]{2,1,0:T(8,128)S(1)} %copy-done.2, bf16[768,256]{1,0:T(8,128)(2,1)S(1)} %copy-done.3, bf16[256,768]{1,0:T(8,128)(2,1)S(1)} %copy-done.4, ...), custom_call_target="tpu_custom_call" | custom-call | tf_op jit(solution)/shard_map/pallas_call | solution.py:373
  61.6 2.2 %collective-permute-start.3 = (f32[96,128]{1,0:T(8,128)S(1)}, f32[96,128]{1,0:T(8,128)S(1)}, u32[]{:S(2)}, u32[]{:S(2)}) collective-permute-start(f32[96,128]{1,0:T(8,128)S(1)} %get-tuple-element.28), channel_id=1, source_target_pairs={{0,1},{1,2},{2,3},{3,4},{4,5},{5,6},{6,7},{7,8},{8,9},{9,10},{10,1... | collective-permute-start | bytes 147464 | tf_op jit(solution)/shard_map/ppermute | solution.py:376
  63.8 8.6 %collective-permute-done.3 = f32[96,128]{1,0:T(8,128)S(1)} collective-permute-done((f32[96,128]{1,0:T(8,128)S(1)}, f32[96,128]{1,0:T(8,128)S(1)}, u32[]{:S(2)}, u32[]{:S(2)}) %collective-permute-start.3) | collective-permute-done | bytes 49184 | tf_op jit(solution)/shard_map/ppermute | solution.py:376
  72.4 3.2 %all-gather.3 = f32[192,128]{1,0:T(8,128)S(1)} all-gather(f32[96,128]{1,0:T(8,128)S(1)} %add.8), channel_id=5, replica_groups={{0,128},{256,384},{1,129},{257,385},{2,130},{258,386},{3,131},{259,387}..., dimensions={0}, use_global_device_ids=true | all-gather | bytes 147456 | tf_op jit(solution)/shard_map/all_gather | solution.py:377
  75.6 0.7 shard_map.116
  (1 shorter events, 0.0 us)
Async XLA Ops:
  0.0 1.5 %copy-start = (f32[20,64,320]{2,1,0:T(8,128)S(1)}, f32[20,64,320]{2,1,0:T(8,128)}, u32[]{:S(2)}) copy-start(f32[20,64,320]{2,1,0:T(8,128)} %frames_ref.1) | copy-start | bytes 4915204
  1.5 11.7 %copy-start.8 = (s32[2,2]{1,0:T(2,128)S(1)}, s32[2,2]{1,0:T(2,128)}, u32[]{:S(2)}) copy-start(s32[2,2]{1,0:T(2,128)} %param.14) | copy-start | bytes 52
  1.5 15.0 %copy-start.1 = (bf16[768,256]{1,0:T(8,128)(2,1)S(1)}, bf16[768,256]{1,0:T(8,128)(2,1)}, u32[]{:S(2)}) copy-start(bf16[768,256]{1,0:T(8,128)(2,1)} %constant.38.clone.right_ref) | copy-start | bytes 1179652
  1.6 15.0 %copy-start.5 = (bf16[256,384]{1,0:T(8,128)(2,1)S(1)}, bf16[256,384]{1,0:T(8,128)(2,1)}, u32[]{:S(2)}) copy-start(bf16[256,384]{1,0:T(8,128)(2,1)} %constant.40.clone.lower_ref.left_ref) | copy-start | bytes 589828
  1.6 15.0 %copy-start.6 = (bf16[256,384]{1,0:T(8,128)(2,1)S(1)}, bf16[256,384]{1,0:T(8,128)(2,1)}, u32[]{:S(2)}) copy-start(bf16[256,384]{1,0:T(8,128)(2,1)} %constant.39.clone.upper_ref.left_ref) | copy-start | bytes 589828
  1.7 23.7 %collective-permute-start.1 = (f32[2,64,1280]{2,1,0:T(8,128)S(1)}, f32[2,64,1280]{2,1,0:T(8,128)}, u32[]{:S(2)}, u32[]{:S(2)}) collective-permute-start(f32[2,64,1280]{2,1,0:T(8,128)S(1)} %get-tuple-element.18.own_r.refs_0_), channel_id=1, source_target_pairs={{0,1},{1,2},{2,3},{3,4},{4,5},{5,6},{6,7},{7,8},{8,9},{9,10},{10,1... | collective-permute-start | bytes 1966088 | tf_op jit(solution)/shard_map/ppermute | solution.py:349
  5.0 31.4 %collective-permute-start = (f32[3,64,1280]{2,1,0:T(8,128)S(1)}, f32[3,64,1280]{2,1,0:T(8,128)S(1)}, u32[]{:S(2)}, u32[]{:S(2)}) collective-permute-start(f32[3,64,1280]{2,1,0:T(8,128)S(1)} %get-tuple-element.17.own_l.refs_2_), channel_id=1, source_target_pairs={{1,0},{2,1},{3,2},{4,3},{5,4},{6,5},{7,6},{8,7},{9,8},{10,9},{11,1... | collective-permute-start | bytes 2949128 | tf_op jit(solution)/shard_map/ppermute | solution.py:348
  32.8 10.2 %collective-permute-start.2 = (f32[2,200,128]{2,1,0:T(8,128)S(1)}, f32[2,200,128]{2,1,0:T(8,128)S(1)}, u32[]{:S(2)}, u32[]{:S(2)}) collective-permute-start(f32[2,200,128]{2,1,0:T(8,128)S(1)} %shard_map.112.refs_0_), channel_id=1, source_target_pairs={{1,0},{2,1},{3,2},{4,3},{5,4},{6,5},{7,6},{8,7},{9,8},{10,9},{11,1... | collective-permute-start | bytes 614408 | tf_op jit(solution)/shard_map/ppermute | solution.py:364
  40.4 17.9 %copy-start.2 = (f32[4,256,256]{2,1,0:T(8,128)S(1)}, f32[4,256,256]{2,1,0:T(8,128)}, u32[]{:S(2)}) copy-start(f32[4,256,256]{2,1,0:T(8,128)} %constant.41.clone.exact) | copy-start | bytes 3145732
  40.4 17.8 %copy-start.3 = (bf16[768,256]{1,0:T(8,128)(2,1)S(1)}, bf16[768,256]{1,0:T(8,128)(2,1)}, u32[]{:S(2)}) copy-start(bf16[768,256]{1,0:T(8,128)(2,1)} %constant.42.clone.right_back) | copy-start | bytes 1179652
  40.5 17.8 %copy-start.4 = (bf16[256,768]{1,0:T(8,128)(2,1)S(1)}, bf16[256,768]{1,0:T(8,128)(2,1)}, u32[]{:S(2)}) copy-start(bf16[256,768]{1,0:T(8,128)(2,1)} %constant.43.clone.left_back) | copy-start | bytes 1179652
  40.5 17.8 %copy-start.7 = (f32[128,128]{1,0:T(8,128)S(1)}, f32[128,128]{1,0:T(8,128)}, u32[]{:S(2)}) copy-start(f32[128,128]{1,0:T(8,128)} %constant.44.clone.window) | copy-start | bytes 196612
  61.6 10.8 %collective-permute-start.3 = (f32[96,128]{1,0:T(8,128)S(1)}, f32[96,128]{1,0:T(8,128)S(1)}, u32[]{:S(2)}, u32[]{:S(2)}) collective-permute-start(f32[96,128]{1,0:T(8,128)S(1)} %get-tuple-element.28), channel_id=1, source_target_pairs={{0,1},{1,2},{2,3},{3,4},{4,5},{5,6},{6,7},{7,8},{8,9},{9,10},{10,1... | collective-permute-start | bytes 147464 | tf_op jit(solution)/shard_map/ppermute | solution.py:376
